TPU v7x, 512 devices: a whole 4x4x16 slice. The times are simulated.
512 devices in a mesh: box: 128 (over z, x, core), slab: 4 (over y).
Axes of the slice: x: 4, y: 4, z: 16, core: 2. Of those that a mesh axis runs over, the one named last changes fastest.
Arguments:
- particle_volume: float32 [1048576], P(('box', 'slab')), may hold values from 0.02 to 0.2
- drag_coeff: float32 [1048576], P(('box', 'slab')), may hold values from 0.1 to 1
- drag_momentum: float32 [2, 1048576], P(None, ('box', 'slab')), may hold values from -6 to 6
- offsets: float32 [3, 1048576], P(None, ('box', 'slab')), may hold values from -0.5 to 0.5
- cell_index: int32 [1048576], P(('box', 'slab')), may hold values from 0 to 16383
- destinations: int32 [1048576, 1], P(('box', 'slab')), may hold values from 0 to 127; in each aligned block of 2048 rows (0 to 2047, 2048 to 4095, ...) at most 32 rows name the same one
- fluid_rhs: float32 [2048, 32, 128], P('box', 'slab'), may hold values from -5 to 7
- wall_mask: int32 [2048, 32, 128], P('box', 'slab'), may hold values from 0 to 1, as said below
Outputs:
- coupled: float32 [4, 2048, 32, 128], P(None, 'box', 'slab')
- pressure: float32 [2048, 32, 128], P('box', 'slab')
Inputs may be any that keep to these rules, and one draw needn't show every extreme that they name: `cell_index`: entries encode (x * 8 + y) * 128 + z. `destinations`: A particle keeps its slab. Among one device's 2048 rows no box index is named by more than 32 rows, and some box index by exactly 32 rows. `wall_mask`: obstacle cells fill whole aligned blocks of 4 x 4 x 4 cells.
All inputs are finite; a program needn't handle non-finite values.
Results may differ from a plain program's by a relative error of at most 0.0038.
Values sent between devices are 32-bit elements; how exact they have to be, the bound alone decides.
No kernel may reach another device: no remote copies, remote signals or barrier semaphores. Data moves between devices by JAX's collectives and lax.ppermute only.
A program may use at most 64 MiB of HBM per device.

v0:
```python
import jax
import jax.numpy as jnp
from jax import lax
from jax.sharding import PartitionSpec as P

LEVELS = 3
SWEEPS = 2
BOTTOM = 4
CYCLES = 2


OMEGA = 0.8


def extended_2(cells, sides, width):
    for axis, dim in sides:
        count = lax.axis_size(axis)
        head = lax.slice_in_dim(cells, 0, width, axis=dim)
        tail = lax.slice_in_dim(cells, cells.shape[dim] - width, cells.shape[dim], axis=dim)
        cells = jnp.concatenate(
            [
                lax.ppermute(tail, axis, [(i, (i + 1) % count) for i in range(count)]),
                cells,
                lax.ppermute(head, axis, [((i + 1) % count, i) for i in range(count)]),
            ],
            axis=dim,
        )
    return cells


def shifted(block, axis, distance):
    devices = range(lax.axis_size(axis))
    route = [((i - distance) % len(devices), i) for i in devices]
    return lax.ppermute(block, axis, route)


def tap_weights(frac):
    return [
        0.5 * (0.5 - frac) * (0.5 - frac),
        0.75 - frac * frac,
        0.5 * (0.5 + frac) * (0.5 + frac),
    ]


def neighbours(extended):
    beside = extended[2:, 1:-1, 1:-1] + extended[:-2, 1:-1, 1:-1]
    beside = beside + extended[1:-1, 2:, 1:-1] + extended[1:-1, :-2, 1:-1]
    beside = beside + extended[1:-1, 1:-1, 2:] + extended[1:-1, 1:-1, :-2]
    return beside


def applied_op(extended, damping, spacing):
    current = extended[1:-1, 1:-1, 1:-1]
    return spacing * (6.0 * current - neighbours(extended)) + damping * current


def relax_cells(extended, source, damping, opened, spacing):
    current = extended[1:-1, 1:-1, 1:-1]
    applied = spacing * (6.0 * current - neighbours(extended)) + damping * current
    return current + OMEGA * opened * (source - applied) / (6.0 * spacing + damping)


def extend_one(field):
    extended = extended_2(field, (("box", 0), ("slab", 1)), 1)
    return jnp.pad(extended, ((0, 0), (0, 0), (1, 1)))


def coarsen(field):
    sx, sy, sz = field.shape
    return field.reshape(sx // 2, 2, sy // 2, 2, sz // 2, 2).mean(axis=(1, 3, 5))


def coarsen_min(field):
    sx, sy, sz = field.shape
    return field.reshape(sx // 2, 2, sy // 2, 2, sz // 2, 2).min(axis=(1, 3, 5))


def prolong(field):
    return jnp.repeat(jnp.repeat(jnp.repeat(field, 2, axis=0), 2, axis=1), 2, axis=2)


def smooth_many(current, source, source_ext, level_data, repeats):
    damping, opened, spacing, coef_ext = level_data
    for repeat in range(repeats):
        current = relax_cells(extend_one(current), source, damping, opened, spacing)
    return (current, source_ext)


def vcycle(stratum, current, source, levels):
    level_data = levels[stratum]
    damping, opened, spacing, coef_ext = level_data
    if stratum == len(levels) - 1:
        current, unused = smooth_many(current, source, None, level_data, BOTTOM)
        return current
    current, source_ext = smooth_many(current, source, None, level_data, SWEEPS)
    residue = opened * (source - applied_op(extend_one(current), damping, spacing))
    coarse_source = coarsen(residue)
    correction = vcycle(stratum + 1, jnp.zeros_like(coarse_source), coarse_source, levels)
    current = current + opened * prolong(correction)
    current, unused = smooth_many(current, source, source_ext, level_data, SWEEPS)
    return current


def deposit_block(summed, record, cell_at, xcells, ycells, zcells):
    z_cell = cell_at % zcells
    y_cell = cell_at // zcells % ycells
    x_cell = cell_at // (zcells * ycells)
    weight_x = tap_weights(record[4])
    weight_y = tap_weights(record[5])
    weight_z = tap_weights(record[6])
    plane_size = (xcells + 2) * (ycells + 2)
    column = jnp.arange(plane_size, dtype=jnp.int32)[:, None]
    planar = jnp.zeros((plane_size, cell_at.shape[0]), jnp.float32)
    for i in range(3):
        for j in range(3):
            position = (x_cell + i) * (ycells + 2) + y_cell + j
            planar = planar + jnp.where(
                column == position[None, :], (weight_x[i] * weight_y[j])[None, :], 0.0
            )
    weighted = (record[:4][:, None, :] * planar[None, :, :]).astype(jnp.bfloat16)
    weighted = weighted.reshape(4 * plane_size, cell_at.shape[0])
    z_index = jnp.arange(zcells, dtype=jnp.int32)[None, :]
    vertical = jnp.zeros((cell_at.shape[0], zcells), jnp.float32)
    for k in range(3):
        vertical = vertical + jnp.where(
            z_index == (z_cell + k - 1)[:, None], weight_z[k][:, None], 0.0
        )
    return summed + jnp.dot(
        weighted, vertical.astype(jnp.bfloat16), preferred_element_type=jnp.float32
    )


def pass_box(rows, step):
    return shifted(rows, "box", step)


def pass_slab(rows, step):
    return shifted(rows, "slab", step)


def shards(
    particle_volume,
    drag_coeff,
    drag_momentum,
    offsets,
    cell_index,
    destinations,
    fluid_rhs,
    wall_mask,
):
    box_count = lax.axis_size("box")
    xcells, ycells, zcells = fluid_rhs.shape
    particle_count = particle_volume.shape[0]
    slot_count = 2 * particle_count
    capacity = slot_count // box_count
    target = destinations[:, 0]
    onehot = (target[:, None] == jnp.arange(box_count, dtype=jnp.int32)[None, :]).astype(jnp.int32)
    within = jnp.sum((jnp.cumsum(onehot, axis=0) - 1) * onehot, axis=1)
    slot_index = target * capacity + within
    record = jnp.concatenate(
        [particle_volume[None], drag_coeff[None], drag_momentum, offsets], axis=0
    )
    outgoing = jnp.zeros((7, slot_count), jnp.float32).at[:, slot_index].set(record)
    outgoing_cells = jnp.zeros((1, slot_count), jnp.int32).at[0, slot_index].set(cell_index)
    incoming, incoming_cells = (
        lax.all_to_all(outgoing, "box", split_axis=1, concat_axis=1, tiled=True),
        lax.all_to_all(outgoing_cells, "box", split_axis=1, concat_axis=1, tiled=True),
    )
    block_len = min(512, slot_count)
    block_count = slot_count // block_len
    records = incoming.reshape(7, block_count, block_len).transpose(1, 0, 2)
    cell_blocks = incoming_cells.reshape(block_count, block_len)
    plane_size = (xcells + 2) * (ycells + 2)
    start_sum = jnp.zeros((4 * plane_size, zcells), jnp.float32)

    def step_block(summed, pieces):
        block_record, block_cells = pieces
        updated = deposit_block(summed, block_record, block_cells, xcells, ycells, zcells)
        return (updated, None)

    summed, unused = lax.scan(step_block, start_sum, (records, cell_blocks))
    deposit = summed.reshape(4, xcells + 2, ycells + 2, zcells)
    halfway = xcells // 2
    from_below = pass_box(deposit[:, xcells + 1 :], 1)
    from_above = pass_box(deposit[:, :1], -1)
    interior = deposit[:, 1 : xcells + 1]
    interior = interior.at[:, :1].add(from_below).at[:, xcells - 1 :].add(from_above)
    moved = shifted(interior[:, :halfway], "box", -1)
    fluid_box = jnp.concatenate([interior[:, halfway:], moved], axis=1)
    slab_below = pass_slab(fluid_box[:, :, ycells + 1 :], 1)
    slab_above = pass_slab(fluid_box[:, :, :1], -1)
    coupled = fluid_box[:, :, 1 : ycells + 1]
    coupled = coupled.at[:, :, :1].add(slab_below).at[:, :, ycells - 1 :].add(slab_above)
    opened = wall_mask.astype(jnp.float32)
    source = opened * ((1.0 - coupled[0]) * fluid_rhs + coupled[2] + coupled[3])
    level_list = [(coupled[1], opened, 1.0)]
    for stratum in range(1, LEVELS):
        damping, opened_now, spacing = level_list[-1]
        level_list.append((coarsen(damping), coarsen_min(opened_now), spacing * 0.25))
    levels = []
    for stratum in range(LEVELS):
        damping, opened_now, spacing = level_list[stratum]
        levels.append((damping, opened_now, spacing, None))
    pressure = jnp.zeros_like(source)
    for repeat in range(CYCLES):
        pressure = vcycle(0, pressure, source, levels)
    return (coupled, pressure)


def solution(mesh):
    in_specs = (
        P(("box", "slab")),
        P(("box", "slab")),
        P(None, ("box", "slab")),
        P(None, ("box", "slab")),
        P(("box", "slab")),
        P(("box", "slab"), None),
        P("box", "slab", None),
        P("box", "slab", None),
    )
    out_specs = (P(None, "box", "slab", None), P("box", "slab", None))
    return jax.shard_map(shards, mesh=mesh, in_specs=in_specs, out_specs=out_specs, check_vma=False)
```

profile of v0, /device:TPU:1, one launch (start us, length us, event | category | flops | bytes accessed | tf_op | source)
XLA Modules:
  0.0 635.3 jit_solution(5667514506219118688)
XLA Ops:
  3.4 8.2 %scatter_custom_fusion.1 = s32[4096]{0:T(1024)S(1)} fusion(s32[2048]{0:T(1024)S(1)} %broadcast_select_fusion, s32[2048]{0:T(1024)} %param.22, s32[]{:T(128)} %constant.323.clone.1), kind=kCustom, calls=%fused_computation.645 | custom fusion | bytes 16896
  12.4 20.4 %all-to-all-start.1 = ((s32[1,128,32]{2,0,1:T(1,128)}), s32[1,128,32]{2,0,1:T(1,128)S(1)}, u32[]{:S(2)}, u32[]{:S(2)}) async-start(s32[1,128,32]{2,0,1:T(1,128)} %bitcast.12), calls=%async_computation.1 | async-start | bytes 131072 | tf_op jit(solution)/shard_map/all_to_all | solution.py:167
  33.2 6.1 scatter_custom_fusion
  41.1 6.5 %all-to-all-done.1 = s32[1,128,32]{2,0,1:T(1,128)S(1)} async-done(((s32[1,128,32]{2,0,1:T(1,128)}), s32[1,128,32]{2,0,1:T(1,128)S(1)}, u32[]{:S(2)}, u32[]{:S(2)}) %all-to-all-start.1) | async-done | bytes 16416 | tf_op jit(solution)/shard_map/all_to_all | solution.py:167
  47.6 9.6 %all-to-all-start = ((f32[128,1,224]{2,1,0:T(1,128)}), f32[128,1,224]{2,1,0:T(1,128)S(1)}, u32[]{:S(2)}, u32[]{:S(2)}) async-start(f32[128,1,224]{2,1,0:T(1,128)} %reshape.965), calls=%async_computation | async-start | bytes 262144 | tf_op jit(solution)/shard_map/all_to_all | solution.py:166
  58.6 14.6 %all-to-all-done = f32[128,1,224]{2,1,0:T(1,128)S(1)} async-done(((f32[128,1,224]{2,1,0:T(1,128)}), f32[128,1,224]{2,1,0:T(1,128)S(1)}, u32[]{:S(2)}, u32[]{:S(2)}) %all-to-all-start) | async-done | bytes 114720 | tf_op jit(solution)/shard_map/all_to_all | solution.py:166
  75.2 13.5 %while.20 = (s32[]{:T(128)}, f32[720,128]{1,0:T(8,128)S(1)}, f32[8,7,512]{2,0,1:T(8,128)S(1)}, s32[8,512]{1,0:T(8,128)S(1)}, s32[]{:T(128)}, /*index=5*/s32[]{:T(128)}, s32[]{}, s32[]{}, s32[]{}) while((s32[]{:T(128)}, f32[720,128]{1,0:T(8,128)S(1)}, f32[8,7,512]{2,0,1:T(8,128)S(1)}, s32[8,512]{1,0:T(8,128)S(1)}, s32[]{:T(128)}, ...), condition=%wide.region_6.7_spmd.clone, body=%wide.region_5.6_spmd.clone.sunk | while | flops 98328584 | bytes 4624555 | solution.py:181
  88.7 3.6 collective-permute-start
  94.5 3.3 collective-permute-done.1
  97.8 4.0 collective-permute-start.2
  101.8 7.2 %collective-permute-start.5 = (f32[1,8,128]{2,1,0:T(8,128)S(1)}, f32[1,8,128]{2,1,0:T(8,128)S(1)}, u32[]{:S(2)}, u32[]{:S(2)}) collective-permute-start(f32[1,8,128]{2,1,0:T(8,128)S(1)} %broadcast.1535), channel_id=1, source_target_pairs={{4,0},{8,4},{12,8},{16,12},{20,16},{24,20},{28,24},{32,28},{36,32}... | collective-permute-start | bytes 12296 | tf_op jit(solution)/shard_map/ppermute | solution.py:24
  112.0 4.6 collective-permute-start.7
  124.6 3.7 collective-permute-start.4
  129.6 9.7 %collective-permute-start.9 = (f32[1,8,128]{2,1,0:T(8,128)S(1)}, f32[1,8,128]{2,1,0:T(8,128)S(1)}, u32[]{:S(2)}, u32[]{:S(2)}) collective-permute-start(f32[1,8,128]{2,1,0:T(8,128)S(1)} %get-tuple-element.289), channel_id=1, source_target_pairs={{4,0},{8,4},{12,8},{16,12},{20,16},{24,20},{28,24},{32,28},{36,32}... | collective-permute-start | bytes 12296 | tf_op jit(solution)/shard_map/ppermute | solution.py:24
  142.4 4.9 collective-permute-start.11
  149.2 7.4 %collective-permute-start.17 = (f32[1,4,64]{2,1,0:T(4,128)S(1)}, f32[1,4,64]{2,1,0:T(4,128)S(1)}, u32[]{:S(2)}, u32[]{:S(2)}) collective-permute-start(f32[1,4,64]{2,1,0:T(4,128)S(1)} %broadcast.1539), channel_id=1, source_target_pairs={{4,0},{8,4},{12,8},{16,12},{20,16},{24,20},{28,24},{32,28},{36,32}... | collective-permute-start | bytes 3080 | tf_op jit(solution)/shard_map/ppermute | solution.py:24
  158.5 5.5 reshape.915
  169.4 3.2 collective-permute-start.14
  172.6 4.9 collective-permute-start.19
  179.4 4.6 collective-permute-start.15
  186.1 5.5 reshape_squeeze.3
  194.5 5.5 reshape.916
  202.7 6.1 collective-permute-start.21
  210.7 6.1 collective-permute-start.29
  219.5 4.6 collective-permute-start.23
  226.0 3.7 collective-permute-done.24
  229.9 8.3 %collective-permute-start.25 = (f32[1,4,64]{2,1,0:T(4,128)S(1)}, f32[1,4,64]{2,1,0:T(4,128)S(1)}, u32[]{:S(2)}, u32[]{:S(2)}) collective-permute-start(f32[1,4,64]{2,1,0:T(4,128)S(1)} %get-tuple-element.323), channel_id=1, source_target_pairs={{4,0},{8,4},{12,8},{16,12},{20,16},{24,20},{28,24},{32,28},{36,32}... | collective-permute-start | bytes 3080 | tf_op jit(solution)/shard_map/ppermute | solution.py:24
  242.1 3.4 collective-permute-start.32
  255.2 7.3 %collective-permute-start.33 = (f32[1,2,32]{2,0,1:T(1,128)S(1)}, f32[1,2,32]{2,0,1:T(1,128)S(1)}, u32[]{:S(2)}, u32[]{:S(2)}) collective-permute-start(f32[1,2,32]{2,0,1:T(1,128)S(1)} %get-tuple-element.351), channel_id=1, source_target_pairs={{4,0},{8,4},{12,8},{16,12},{20,16},{24,20},{28,24},{32,28},{36,32}... | collective-permute-start | bytes 776 | tf_op jit(solution)/shard_map/ppermute | solution.py:24
  264.4 3.9 collective-permute-done.34
  270.3 3.4 collective-permute-start.36
  276.0 8.8 %collective-permute-start.37 = (f32[1,2,32]{2,0,1:T(1,128)S(1)}, f32[1,2,32]{2,0,1:T(1,128)S(1)}, u32[]{:S(2)}, u32[]{:S(2)}) collective-permute-start(f32[1,2,32]{2,0,1:T(1,128)S(1)} %get-tuple-element.349), channel_id=1, source_target_pairs={{4,0},{8,4},{12,8},{16,12},{20,16},{24,20},{28,24},{32,28},{36,32}... | collective-permute-start | bytes 776 | tf_op jit(solution)/shard_map/ppermute | solution.py:24
  289.8 3.4 collective-permute-start.40
  295.5 8.2 %collective-permute-start.41 = (f32[1,2,32]{2,0,1:T(1,128)S(1)}, f32[1,2,32]{2,0,1:T(1,128)S(1)}, u32[]{:S(2)}, u32[]{:S(2)}) collective-permute-start(f32[1,2,32]{2,0,1:T(1,128)S(1)} %get-tuple-element.347), channel_id=1, source_target_pairs={{4,0},{8,4},{12,8},{16,12},{20,16},{24,20},{28,24},{32,28},{36,32}... | collective-permute-start | bytes 776 | tf_op jit(solution)/shard_map/ppermute | solution.py:24
  308.8 3.4 collective-permute-start.44
  314.8 8.3 %collective-permute-start.45 = (f32[1,4,64]{2,1,0:T(4,128)S(1)}, f32[1,4,64]{2,1,0:T(4,128)S(1)}, u32[]{:S(2)}, u32[]{:S(2)}) collective-permute-start(f32[1,4,64]{2,1,0:T(4,128)S(1)} %get-tuple-element.319), channel_id=1, source_target_pairs={{4,0},{8,4},{12,8},{16,12},{20,16},{24,20},{28,24},{32,28},{36,32}... | collective-permute-start | bytes 3080 | tf_op jit(solution)/shard_map/ppermute | solution.py:24
  334.4 8.5 %collective-permute-start.49 = (f32[1,4,64]{2,1,0:T(4,128)S(1)}, f32[1,4,64]{2,1,0:T(4,128)S(1)}, u32[]{:S(2)}, u32[]{:S(2)}) collective-permute-start(f32[1,4,64]{2,1,0:T(4,128)S(1)} %get-tuple-element.317), channel_id=1, source_target_pairs={{4,0},{8,4},{12,8},{16,12},{20,16},{24,20},{28,24},{32,28},{36,32}... | collective-permute-start | bytes 3080 | tf_op jit(solution)/shard_map/ppermute | solution.py:24
  347.9 3.4 collective-permute-start.52
  354.2 8.3 %collective-permute-start.53 = (f32[1,8,128]{2,1,0:T(8,128)S(1)}, f32[1,8,128]{2,1,0:T(8,128)S(1)}, u32[]{:S(2)}, u32[]{:S(2)}) collective-permute-start(f32[1,8,128]{2,1,0:T(8,128)S(1)} %get-tuple-element.285), channel_id=1, source_target_pairs={{4,0},{8,4},{12,8},{16,12},{20,16},{24,20},{28,24},{32,28},{36,32}... | collective-permute-start | bytes 12296 | tf_op jit(solution)/shard_map/ppermute | solution.py:24
  367.8 3.4 collective-permute-start.56
  373.8 8.3 %collective-permute-start.57 = (f32[1,8,128]{2,1,0:T(8,128)S(1)}, f32[1,8,128]{2,1,0:T(8,128)S(1)}, u32[]{:S(2)}, u32[]{:S(2)}) collective-permute-start(f32[1,8,128]{2,1,0:T(8,128)S(1)} %get-tuple-element.283), channel_id=1, source_target_pairs={{4,0},{8,4},{12,8},{16,12},{20,16},{24,20},{28,24},{32,28},{36,32}... | collective-permute-start | bytes 12296 | tf_op jit(solution)/shard_map/ppermute | solution.py:24
  387.0 3.4 collective-permute-start.60
  393.0 8.4 %collective-permute-start.61 = (f32[1,8,128]{2,1,0:T(8,128)S(1)}, f32[1,8,128]{2,1,0:T(8,128)S(1)}, u32[]{:S(2)}, u32[]{:S(2)}) collective-permute-start(f32[1,8,128]{2,1,0:T(8,128)S(1)} %get-tuple-element.281), channel_id=1, source_target_pairs={{4,0},{8,4},{12,8},{16,12},{20,16},{24,20},{28,24},{32,28},{36,32}... | collective-permute-start | bytes 12296 | tf_op jit(solution)/shard_map/ppermute | solution.py:24
  412.8 8.5 %collective-permute-start.65 = (f32[1,8,128]{2,1,0:T(8,128)S(1)}, f32[1,8,128]{2,1,0:T(8,128)S(1)}, u32[]{:S(2)}, u32[]{:S(2)}) collective-permute-start(f32[1,8,128]{2,1,0:T(8,128)S(1)} %get-tuple-element.279), channel_id=1, source_target_pairs={{4,0},{8,4},{12,8},{16,12},{20,16},{24,20},{28,24},{32,28},{36,32}... | collective-permute-start | bytes 12296 | tf_op jit(solution)/shard_map/ppermute | solution.py:24
  426.4 3.4 collective-permute-start.68
  432.3 8.3 %collective-permute-start.69 = (f32[1,8,128]{2,1,0:T(8,128)S(1)}, f32[1,8,128]{2,1,0:T(8,128)S(1)}, u32[]{:S(2)}, u32[]{:S(2)}) collective-permute-start(f32[1,8,128]{2,1,0:T(8,128)S(1)} %get-tuple-element.277), channel_id=1, source_target_pairs={{4,0},{8,4},{12,8},{16,12},{20,16},{24,20},{28,24},{32,28},{36,32}... | collective-permute-start | bytes 12296 | tf_op jit(solution)/shard_map/ppermute | solution.py:24
  445.7 3.4 collective-permute-start.72
  451.6 5.5 reshape.925
  459.8 8.3 %collective-permute-start.73 = (f32[1,4,64]{2,1,0:T(4,128)S(1)}, f32[1,4,64]{2,1,0:T(4,128)S(1)}, u32[]{:S(2)}, u32[]{:S(2)}) collective-permute-start(f32[1,4,64]{2,1,0:T(4,128)S(1)} %get-tuple-element.315), channel_id=1, source_target_pairs={{4,0},{8,4},{12,8},{16,12},{20,16},{24,20},{28,24},{32,28},{36,32}... | collective-permute-start | bytes 3080 | tf_op jit(solution)/shard_map/ppermute | solution.py:24
  473.0 3.4 collective-permute-start.76
  478.8 8.3 %collective-permute-start.77 = (f32[1,4,64]{2,1,0:T(4,128)S(1)}, f32[1,4,64]{2,1,0:T(4,128)S(1)}, u32[]{:S(2)}, u32[]{:S(2)}) collective-permute-start(f32[1,4,64]{2,1,0:T(4,128)S(1)} %get-tuple-element.313), channel_id=1, source_target_pairs={{4,0},{8,4},{12,8},{16,12},{20,16},{24,20},{28,24},{32,28},{36,32}... | collective-permute-start | bytes 3080 | tf_op jit(solution)/shard_map/ppermute | solution.py:24
  499.1 8.5 %collective-permute-start.81 = (f32[1,2,32]{2,0,1:T(1,128)S(1)}, f32[1,2,32]{2,0,1:T(1,128)S(1)}, u32[]{:S(2)}, u32[]{:S(2)}) collective-permute-start(f32[1,2,32]{2,0,1:T(1,128)S(1)} %get-tuple-element.345), channel_id=1, source_target_pairs={{4,0},{8,4},{12,8},{16,12},{20,16},{24,20},{28,24},{32,28},{36,32}... | collective-permute-start | bytes 776 | tf_op jit(solution)/shard_map/ppermute | solution.py:24
  512.7 3.4 collective-permute-start.84
  518.4 8.3 %collective-permute-start.85 = (f32[1,2,32]{2,0,1:T(1,128)S(1)}, f32[1,2,32]{2,0,1:T(1,128)S(1)}, u32[]{:S(2)}, u32[]{:S(2)}) collective-permute-start(f32[1,2,32]{2,0,1:T(1,128)S(1)} %get-tuple-element.343), channel_id=1, source_target_pairs={{4,0},{8,4},{12,8},{16,12},{20,16},{24,20},{28,24},{32,28},{36,32}... | collective-permute-start | bytes 776 | tf_op jit(solution)/shard_map/ppermute | solution.py:24
  531.7 3.4 collective-permute-start.88
  537.4 8.2 %collective-permute-start.89 = (f32[1,2,32]{2,0,1:T(1,128)S(1)}, f32[1,2,32]{2,0,1:T(1,128)S(1)}, u32[]{:S(2)}, u32[]{:S(2)}) collective-permute-start(f32[1,2,32]{2,0,1:T(1,128)S(1)} %get-tuple-element.341), channel_id=1, source_target_pairs={{4,0},{8,4},{12,8},{16,12},{20,16},{24,20},{28,24},{32,28},{36,32}... | collective-permute-start | bytes 776 | tf_op jit(solution)/shard_map/ppermute | solution.py:24
  550.7 3.4 collective-permute-start.92
  556.7 8.3 %collective-permute-start.93 = (f32[1,4,64]{2,1,0:T(4,128)S(1)}, f32[1,4,64]{2,1,0:T(4,128)S(1)}, u32[]{:S(2)}, u32[]{:S(2)}) collective-permute-start(f32[1,4,64]{2,1,0:T(4,128)S(1)} %get-tuple-element.311), channel_id=1, source_target_pairs={{4,0},{8,4},{12,8},{16,12},{20,16},{24,20},{28,24},{32,28},{36,32}... | collective-permute-start | bytes 3080 | tf_op jit(solution)/shard_map/ppermute | solution.py:24
  576.3 8.5 %collective-permute-start.97 = (f32[1,4,64]{2,1,0:T(4,128)S(1)}, f32[1,4,64]{2,1,0:T(4,128)S(1)}, u32[]{:S(2)}, u32[]{:S(2)}) collective-permute-start(f32[1,4,64]{2,1,0:T(4,128)S(1)} %get-tuple-element.309), channel_id=1, source_target_pairs={{4,0},{8,4},{12,8},{16,12},{20,16},{24,20},{28,24},{32,28},{36,32}... | collective-permute-start | bytes 3080 | tf_op jit(solution)/shard_map/ppermute | solution.py:24
  589.8 3.4 collective-permute-start.100
  596.1 8.3 %collective-permute-start.101 = (f32[1,8,128]{2,1,0:T(8,128)S(1)}, f32[1,8,128]{2,1,0:T(8,128)S(1)}, u32[]{:S(2)}, u32[]{:S(2)}) collective-permute-start(f32[1,8,128]{2,1,0:T(8,128)S(1)} %get-tuple-element.275), channel_id=1, source_target_pairs={{4,0},{8,4},{12,8},{16,12},{20,16},{24,20},{28,24},{32,28},{36,32}... | collective-permute-start | bytes 12296 | tf_op jit(solution)/shard_map/ppermute | solution.py:24
  609.5 3.4 collective-permute-start.104
  615.4 8.3 %collective-permute-start.105 = (f32[1,8,128]{2,1,0:T(8,128)S(1)}, f32[1,8,128]{2,1,0:T(8,128)S(1)}, u32[]{:S(2)}, u32[]{:S(2)}) collective-permute-start(f32[1,8,128]{2,1,0:T(8,128)S(1)} %get-tuple-element.273), channel_id=1, source_target_pairs={{4,0},{8,4},{12,8},{16,12},{20,16},{24,20},{28,24},{32,28},{36,32}... | collective-permute-start | bytes 12296 | tf_op jit(solution)/shard_map/ppermute | solution.py:24
  628.7 3.4 collective-permute-start.108
  (503 shorter events, 238.3 us)
Async XLA Ops:
  12.4 35.2 %all-to-all-start.1 = ((s32[1,128,32]{2,0,1:T(1,128)}), s32[1,128,32]{2,0,1:T(1,128)S(1)}, u32[]{:S(2)}, u32[]{:S(2)}) async-start(s32[1,128,32]{2,0,1:T(1,128)} %bitcast.12), calls=%async_computation.1 | async-start | bytes 131072 | tf_op jit(solution)/shard_map/all_to_all | solution.py:167
  47.6 25.7 %all-to-all-start = ((f32[128,1,224]{2,1,0:T(1,128)}), f32[128,1,224]{2,1,0:T(1,128)S(1)}, u32[]{:S(2)}, u32[]{:S(2)}) async-start(f32[128,1,224]{2,1,0:T(1,128)} %reshape.965), calls=%async_computation | async-start | bytes 262144 | tf_op jit(solution)/shard_map/all_to_all | solution.py:166
  88.7 5.7 collective-permute-start
  97.8 20.8 %collective-permute-start.2 = (f32[4,8,10,128]{3,2,1,0:T(8,128)S(1)}, f32[4,8,10,128]{3,2,1,0:T(8,128)S(1)}, u32[]{:S(2)}, u32[]{:S(2)}) collective-permute-start(f32[4,8,10,128]{3,2,1,0:T(8,128)S(1)} %get-tuple-element.250), channel_id=1, source_target_pairs={{4,0},{8,4},{12,8},{16,12},{20,16},{24,20},{28,24},{32,28},{36,32}... | collective-permute-start | bytes 491528 | tf_op jit(solution)/shard_map/ppermute | solution.py:34
  101.8 9.1 %collective-permute-start.5 = (f32[1,8,128]{2,1,0:T(8,128)S(1)}, f32[1,8,128]{2,1,0:T(8,128)S(1)}, u32[]{:S(2)}, u32[]{:S(2)}) collective-permute-start(f32[1,8,128]{2,1,0:T(8,128)S(1)} %broadcast.1535), channel_id=1, source_target_pairs={{4,0},{8,4},{12,8},{16,12},{20,16},{24,20},{28,24},{32,28},{36,32}... | collective-permute-start | bytes 12296 | tf_op jit(solution)/shard_map/ppermute | solution.py:24
  112.0 8.6 %collective-permute-start.7 = (f32[18,1,128]{2,1,0:T(1,128)S(1)}, f32[18,1,128]{2,1,0:T(1,128)S(1)}, u32[]{:S(2)}, u32[]{:S(2)}) collective-permute-start(f32[18,1,128]{2,1,0:T(1,128)S(1)} %get-tuple-element.271), channel_id=1, source_target_pairs={{1,0},{2,1},{3,2},{0,3},{5,4},{6,5},{7,6},{4,7},{9,8},{10,9},{11,1... | collective-permute-start | bytes 27656 | tf_op jit(solution)/shard_map/ppermute | solution.py:24
  116.7 5.6 collective-permute-start.8
  118.7 5.9 collective-permute-start.3
  129.6 11.6 %collective-permute-start.9 = (f32[1,8,128]{2,1,0:T(8,128)S(1)}, f32[1,8,128]{2,1,0:T(8,128)S(1)}, u32[]{:S(2)}, u32[]{:S(2)}) collective-permute-start(f32[1,8,128]{2,1,0:T(8,128)S(1)} %get-tuple-element.289), channel_id=1, source_target_pairs={{4,0},{8,4},{12,8},{16,12},{20,16},{24,20},{28,24},{32,28},{36,32}... | collective-permute-start | bytes 12296 | tf_op jit(solution)/shard_map/ppermute | solution.py:24
  142.4 24.2 %collective-permute-start.11 = (f32[18,1,128]{2,1,0:T(1,128)S(1)}, f32[18,1,128]{2,1,0:T(1,128)S(1)}, u32[]{:S(2)}, u32[]{:S(2)}) collective-permute-start(f32[18,1,128]{2,1,0:T(1,128)S(1)} %get-tuple-element.269), channel_id=1, source_target_pairs={{1,0},{2,1},{3,2},{0,3},{5,4},{6,5},{7,6},{4,7},{9,8},{10,9},{11,1... | collective-permute-start | bytes 27656 | tf_op jit(solution)/shard_map/ppermute | solution.py:24
  147.2 19.4 %collective-permute-start.12 = (f32[18,1,128]{2,1,0:T(1,128)S(1)}, f32[18,1,128]{2,1,0:T(1,128)S(1)}, u32[]{:S(2)}, u32[]{:S(2)}) collective-permute-start(f32[18,1,128]{2,1,0:T(1,128)S(1)} %get-tuple-element.268), channel_id=1, source_target_pairs={{0,1},{1,2},{2,3},{3,0},{4,5},{5,6},{6,7},{7,4},{8,9},{9,10},{10,1... | collective-permute-start | bytes 27656 | tf_op jit(solution)/shard_map/ppermute | solution.py:22
  149.2 23.4 %collective-permute-start.17 = (f32[1,4,64]{2,1,0:T(4,128)S(1)}, f32[1,4,64]{2,1,0:T(4,128)S(1)}, u32[]{:S(2)}, u32[]{:S(2)}) collective-permute-start(f32[1,4,64]{2,1,0:T(4,128)S(1)} %broadcast.1539), channel_id=1, source_target_pairs={{4,0},{8,4},{12,8},{16,12},{20,16},{24,20},{28,24},{32,28},{36,32}... | collective-permute-start | bytes 3080 | tf_op jit(solution)/shard_map/ppermute | solution.py:24
  156.6 16.0 %collective-permute-start.18 = (f32[1,4,64]{2,1,0:T(4,128)S(1)}, f32[1,4,64]{2,1,0:T(4,128)S(1)}, u32[]{:S(2)}, u32[]{:S(2)}) collective-permute-start(f32[1,4,64]{2,1,0:T(4,128)S(1)} %broadcast.1539), channel_id=1, source_target_pairs={{0,4},{4,8},{8,12},{12,16},{16,20},{20,24},{24,28},{28,32},{32,36}... | collective-permute-start | bytes 3080 | tf_op jit(solution)/shard_map/ppermute | solution.py:22
  166.9 12.4 %collective-permute-start.13 = (f32[1,8,128]{2,1,0:T(8,128)S(1)}, f32[1,8,128]{2,1,0:T(8,128)S(1)}, u32[]{:S(2)}, u32[]{:S(2)}) collective-permute-start(f32[1,8,128]{2,1,0:T(8,128)S(1)} %get-tuple-element.287), channel_id=1, source_target_pairs={{4,0},{8,4},{12,8},{16,12},{20,16},{24,20},{28,24},{32,28},{36,32}... | collective-permute-start | bytes 12296 | tf_op jit(solution)/shard_map/ppermute | solution.py:24
  169.4 10.0 %collective-permute-start.14 = (f32[1,8,128]{2,1,0:T(8,128)S(1)}, f32[1,8,128]{2,1,0:T(8,128)S(1)}, u32[]{:S(2)}, u32[]{:S(2)}) collective-permute-start(f32[1,8,128]{2,1,0:T(8,128)S(1)} %get-tuple-element.286), channel_id=1, source_target_pairs={{0,4},{4,8},{8,12},{12,16},{16,20},{20,24},{24,28},{28,32},{32,36}... | collective-permute-start | bytes 12296 | tf_op jit(solution)/shard_map/ppermute | solution.py:22
  172.6 13.3 %collective-permute-start.19 = (f32[10,1,64]{2,1,0:T(1,128)S(1)}, f32[10,1,64]{2,1,0:T(1,128)S(1)}, u32[]{:S(2)}, u32[]{:S(2)}) collective-permute-start(f32[10,1,64]{2,1,0:T(1,128)S(1)} %get-tuple-element.307), channel_id=1, source_target_pairs={{1,0},{2,1},{3,2},{0,3},{5,4},{6,5},{7,6},{4,7},{9,8},{10,9},{11,1... | collective-permute-start | bytes 7688 | tf_op jit(solution)/shard_map/ppermute | solution.py:24
  177.4 8.5 %collective-permute-start.20 = (f32[10,1,64]{2,1,0:T(1,128)S(1)}, f32[10,1,64]{2,1,0:T(1,128)S(1)}, u32[]{:S(2)}, u32[]{:S(2)}) collective-permute-start(f32[10,1,64]{2,1,0:T(1,128)S(1)} %get-tuple-element.306), channel_id=1, source_target_pairs={{0,1},{1,2},{2,3},{3,0},{4,5},{5,6},{6,7},{7,4},{8,9},{9,10},{10,1... | collective-permute-start | bytes 7688 | tf_op jit(solution)/shard_map/ppermute | solution.py:22
  179.4 14.7 %collective-permute-start.15 = (f32[18,1,128]{2,1,0:T(1,128)S(1)}, f32[18,1,128]{2,1,0:T(1,128)S(1)}, u32[]{:S(2)}, u32[]{:S(2)}) collective-permute-start(f32[18,1,128]{2,1,0:T(1,128)S(1)} %get-tuple-element.267), channel_id=1, source_target_pairs={{1,0},{2,1},{3,2},{0,3},{5,4},{6,5},{7,6},{4,7},{9,8},{10,9},{11,1... | collective-permute-start | bytes 27656 | tf_op jit(solution)/shard_map/ppermute | solution.py:24
  184.0 10.2 %collective-permute-start.16 = (f32[18,1,128]{2,1,0:T(1,128)S(1)}, f32[18,1,128]{2,1,0:T(1,128)S(1)}, u32[]{:S(2)}, u32[]{:S(2)}) collective-permute-start(f32[18,1,128]{2,1,0:T(1,128)S(1)} %get-tuple-element.266), channel_id=1, source_target_pairs={{0,1},{1,2},{2,3},{3,0},{4,5},{5,6},{6,7},{7,4},{8,9},{9,10},{10,1... | collective-permute-start | bytes 27656 | tf_op jit(solution)/shard_map/ppermute | solution.py:22
  202.7 16.8 %collective-permute-start.21 = (f32[1,4,64]{2,1,0:T(4,128)S(1)}, f32[1,4,64]{2,1,0:T(4,128)S(1)}, u32[]{:S(2)}, u32[]{:S(2)}) collective-permute-start(f32[1,4,64]{2,1,0:T(4,128)S(1)} %get-tuple-element.325), channel_id=1, source_target_pairs={{4,0},{8,4},{12,8},{16,12},{20,16},{24,20},{28,24},{32,28},{36,32}... | collective-permute-start | bytes 3080 | tf_op jit(solution)/shard_map/ppermute | solution.py:24
  208.8 10.7 %collective-permute-start.22 = (f32[1,4,64]{2,1,0:T(4,128)S(1)}, f32[1,4,64]{2,1,0:T(4,128)S(1)}, u32[]{:S(2)}, u32[]{:S(2)}) collective-permute-start(f32[1,4,64]{2,1,0:T(4,128)S(1)} %get-tuple-element.324), channel_id=1, source_target_pairs={{0,4},{4,8},{8,12},{12,16},{16,20},{20,24},{24,28},{28,32},{32,36}... | collective-permute-start | bytes 3080 | tf_op jit(solution)/shard_map/ppermute | solution.py:22
  210.7 15.3 %collective-permute-start.29 = (f32[1,2,32]{2,0,1:T(1,128)S(1)}, f32[1,2,32]{2,0,1:T(1,128)S(1)}, u32[]{:S(2)}, u32[]{:S(2)}) collective-permute-start(f32[1,2,32]{2,0,1:T(1,128)S(1)} %broadcast.1545), channel_id=1, source_target_pairs={{4,0},{8,4},{12,8},{16,12},{20,16},{24,20},{28,24},{32,28},{36,32}... | collective-permute-start | bytes 776 | tf_op jit(solution)/shard_map/ppermute | solution.py:24
  216.8 9.2 %collective-permute-start.30 = (f32[1,2,32]{2,0,1:T(1,128)S(1)}, f32[1,2,32]{2,0,1:T(1,128)S(1)}, u32[]{:S(2)}, u32[]{:S(2)}) collective-permute-start(f32[1,2,32]{2,0,1:T(1,128)S(1)} %broadcast.1545), channel_id=1, source_target_pairs={{0,4},{4,8},{8,12},{12,16},{16,20},{20,24},{24,28},{28,32},{32,36}... | collective-permute-start | bytes 776 | tf_op jit(solution)/shard_map/ppermute | solution.py:22
  219.5 6.6 %collective-permute-start.23 = (f32[10,1,64]{2,1,0:T(1,128)S(1)}, f32[10,1,64]{2,1,0:T(1,128)S(1)}, u32[]{:S(2)}, u32[]{:S(2)}) collective-permute-start(f32[10,1,64]{2,1,0:T(1,128)S(1)} %get-tuple-element.305), channel_id=1, source_target_pairs={{1,0},{2,1},{3,2},{0,3},{5,4},{6,5},{7,6},{4,7},{9,8},{10,9},{11,1... | collective-permute-start | bytes 7688 | tf_op jit(solution)/shard_map/ppermute | solution.py:24
  224.1 5.6 collective-permute-start.24
  229.9 15.6 %collective-permute-start.25 = (f32[1,4,64]{2,1,0:T(4,128)S(1)}, f32[1,4,64]{2,1,0:T(4,128)S(1)}, u32[]{:S(2)}, u32[]{:S(2)}) collective-permute-start(f32[1,4,64]{2,1,0:T(4,128)S(1)} %get-tuple-element.323), channel_id=1, source_target_pairs={{4,0},{8,4},{12,8},{16,12},{20,16},{24,20},{28,24},{32,28},{36,32}... | collective-permute-start | bytes 3080 | tf_op jit(solution)/shard_map/ppermute | solution.py:24
  238.2 7.3 %collective-permute-start.26 = (f32[1,4,64]{2,1,0:T(4,128)S(1)}, f32[1,4,64]{2,1,0:T(4,128)S(1)}, u32[]{:S(2)}, u32[]{:S(2)}) collective-permute-start(f32[1,4,64]{2,1,0:T(4,128)S(1)} %get-tuple-element.322), channel_id=1, source_target_pairs={{0,4},{4,8},{8,12},{12,16},{16,20},{20,24},{24,28},{28,32},{32,36}... | collective-permute-start | bytes 3080 | tf_op jit(solution)/shard_map/ppermute | solution.py:22
  240.2 10.6 %collective-permute-start.31 = (f32[6,1,32]{2,0,1:T(8,128)S(1)}, f32[6,1,32]{2,0,1:T(8,128)S(1)}, u32[]{:S(2)}, u32[]{:S(2)}) collective-permute-start(f32[6,1,32]{2,0,1:T(8,128)S(1)} %get-tuple-element.339), channel_id=1, source_target_pairs={{1,0},{2,1},{3,2},{0,3},{5,4},{6,5},{7,6},{4,7},{9,8},{10,9},{11,1... | collective-permute-start | bytes 2312 | tf_op jit(solution)/shard_map/ppermute | solution.py:24
  242.1 8.7 %collective-permute-start.32 = (f32[6,1,32]{2,0,1:T(8,128)S(1)}, f32[6,1,32]{2,0,1:T(8,128)S(1)}, u32[]{:S(2)}, u32[]{:S(2)}) collective-permute-start(f32[6,1,32]{2,0,1:T(8,128)S(1)} %get-tuple-element.338), channel_id=1, source_target_pairs={{0,1},{1,2},{2,3},{3,0},{4,5},{5,6},{6,7},{7,4},{8,9},{9,10},{10,1... | collective-permute-start | bytes 2312 | tf_op jit(solution)/shard_map/ppermute | solution.py:22
  245.5 6.1 collective-permute-start.27
  248.7 5.6 collective-permute-start.28
  255.2 9.2 %collective-permute-start.33 = (f32[1,2,32]{2,0,1:T(1,128)S(1)}, f32[1,2,32]{2,0,1:T(1,128)S(1)}, u32[]{:S(2)}, u32[]{:S(2)}) collective-permute-start(f32[1,2,32]{2,0,1:T(1,128)S(1)} %get-tuple-element.351), channel_id=1, source_target_pairs={{4,0},{8,4},{12,8},{16,12},{20,16},{24,20},{28,24},{32,28},{36,32}... | collective-permute-start | bytes 776 | tf_op jit(solution)/shard_map/ppermute | solution.py:24
  262.5 5.9 collective-permute-start.34
  276.0 10.8 %collective-permute-start.37 = (f32[1,2,32]{2,0,1:T(1,128)S(1)}, f32[1,2,32]{2,0,1:T(1,128)S(1)}, u32[]{:S(2)}, u32[]{:S(2)}) collective-permute-start(f32[1,2,32]{2,0,1:T(1,128)S(1)} %get-tuple-element.349), channel_id=1, source_target_pairs={{4,0},{8,4},{12,8},{16,12},{20,16},{24,20},{28,24},{32,28},{36,32}... | collective-permute-start | bytes 776 | tf_op jit(solution)/shard_map/ppermute | solution.py:24
  295.5 10.2 %collective-permute-start.41 = (f32[1,2,32]{2,0,1:T(1,128)S(1)}, f32[1,2,32]{2,0,1:T(1,128)S(1)}, u32[]{:S(2)}, u32[]{:S(2)}) collective-permute-start(f32[1,2,32]{2,0,1:T(1,128)S(1)} %get-tuple-element.347), channel_id=1, source_target_pairs={{4,0},{8,4},{12,8},{16,12},{20,16},{24,20},{28,24},{32,28},{36,32}... | collective-permute-start | bytes 776 | tf_op jit(solution)/shard_map/ppermute | solution.py:24
  314.8 10.3 %collective-permute-start.45 = (f32[1,4,64]{2,1,0:T(4,128)S(1)}, f32[1,4,64]{2,1,0:T(4,128)S(1)}, u32[]{:S(2)}, u32[]{:S(2)}) collective-permute-start(f32[1,4,64]{2,1,0:T(4,128)S(1)} %get-tuple-element.319), channel_id=1, source_target_pairs={{4,0},{8,4},{12,8},{16,12},{20,16},{24,20},{28,24},{32,28},{36,32}... | collective-permute-start | bytes 3080 | tf_op jit(solution)/shard_map/ppermute | solution.py:24
  328.6 5.6 collective-permute-start.48
  334.4 10.5 %collective-permute-start.49 = (f32[1,4,64]{2,1,0:T(4,128)S(1)}, f32[1,4,64]{2,1,0:T(4,128)S(1)}, u32[]{:S(2)}, u32[]{:S(2)}) collective-permute-start(f32[1,4,64]{2,1,0:T(4,128)S(1)} %get-tuple-element.317), channel_id=1, source_target_pairs={{4,0},{8,4},{12,8},{16,12},{20,16},{24,20},{28,24},{32,28},{36,32}... | collective-permute-start | bytes 3080 | tf_op jit(solution)/shard_map/ppermute | solution.py:24
  347.9 5.6 collective-permute-start.52
  354.2 10.3 %collective-permute-start.53 = (f32[1,8,128]{2,1,0:T(8,128)S(1)}, f32[1,8,128]{2,1,0:T(8,128)S(1)}, u32[]{:S(2)}, u32[]{:S(2)}) collective-permute-start(f32[1,8,128]{2,1,0:T(8,128)S(1)} %get-tuple-element.285), channel_id=1, source_target_pairs={{4,0},{8,4},{12,8},{16,12},{20,16},{24,20},{28,24},{32,28},{36,32}... | collective-permute-start | bytes 12296 | tf_op jit(solution)/shard_map/ppermute | solution.py:24
  367.8 5.6 collective-permute-start.56
  373.8 10.2 %collective-permute-start.57 = (f32[1,8,128]{2,1,0:T(8,128)S(1)}, f32[1,8,128]{2,1,0:T(8,128)S(1)}, u32[]{:S(2)}, u32[]{:S(2)}) collective-permute-start(f32[1,8,128]{2,1,0:T(8,128)S(1)} %get-tuple-element.283), channel_id=1, source_target_pairs={{4,0},{8,4},{12,8},{16,12},{20,16},{24,20},{28,24},{32,28},{36,32}... | collective-permute-start | bytes 12296 | tf_op jit(solution)/shard_map/ppermute | solution.py:24
  387.0 5.6 collective-permute-start.60
  393.0 10.3 %collective-permute-start.61 = (f32[1,8,128]{2,1,0:T(8,128)S(1)}, f32[1,8,128]{2,1,0:T(8,128)S(1)}, u32[]{:S(2)}, u32[]{:S(2)}) collective-permute-start(f32[1,8,128]{2,1,0:T(8,128)S(1)} %get-tuple-element.281), channel_id=1, source_target_pairs={{4,0},{8,4},{12,8},{16,12},{20,16},{24,20},{28,24},{32,28},{36,32}... | collective-permute-start | bytes 12296 | tf_op jit(solution)/shard_map/ppermute | solution.py:24
  406.9 5.6 collective-permute-start.64
  412.8 10.5 %collective-permute-start.65 = (f32[1,8,128]{2,1,0:T(8,128)S(1)}, f32[1,8,128]{2,1,0:T(8,128)S(1)}, u32[]{:S(2)}, u32[]{:S(2)}) collective-permute-start(f32[1,8,128]{2,1,0:T(8,128)S(1)} %get-tuple-element.279), channel_id=1, source_target_pairs={{4,0},{8,4},{12,8},{16,12},{20,16},{24,20},{28,24},{32,28},{36,32}... | collective-permute-start | bytes 12296 | tf_op jit(solution)/shard_map/ppermute | solution.py:24
  426.4 5.6 collective-permute-start.68
  432.3 10.3 %collective-permute-start.69 = (f32[1,8,128]{2,1,0:T(8,128)S(1)}, f32[1,8,128]{2,1,0:T(8,128)S(1)}, u32[]{:S(2)}, u32[]{:S(2)}) collective-permute-start(f32[1,8,128]{2,1,0:T(8,128)S(1)} %get-tuple-element.277), channel_id=1, source_target_pairs={{4,0},{8,4},{12,8},{16,12},{20,16},{24,20},{28,24},{32,28},{36,32}... | collective-permute-start | bytes 12296 | tf_op jit(solution)/shard_map/ppermute | solution.py:24
  445.7 5.6 collective-permute-start.72
  459.8 10.2 %collective-permute-start.73 = (f32[1,4,64]{2,1,0:T(4,128)S(1)}, f32[1,4,64]{2,1,0:T(4,128)S(1)}, u32[]{:S(2)}, u32[]{:S(2)}) collective-permute-start(f32[1,4,64]{2,1,0:T(4,128)S(1)} %get-tuple-element.315), channel_id=1, source_target_pairs={{4,0},{8,4},{12,8},{16,12},{20,16},{24,20},{28,24},{32,28},{36,32}... | collective-permute-start | bytes 3080 | tf_op jit(solution)/shard_map/ppermute | solution.py:24
  473.0 5.6 collective-permute-start.76
  478.8 10.3 %collective-permute-start.77 = (f32[1,4,64]{2,1,0:T(4,128)S(1)}, f32[1,4,64]{2,1,0:T(4,128)S(1)}, u32[]{:S(2)}, u32[]{:S(2)}) collective-permute-start(f32[1,4,64]{2,1,0:T(4,128)S(1)} %get-tuple-element.313), channel_id=1, source_target_pairs={{4,0},{8,4},{12,8},{16,12},{20,16},{24,20},{28,24},{32,28},{36,32}... | collective-permute-start | bytes 3080 | tf_op jit(solution)/shard_map/ppermute | solution.py:24
  492.7 5.6 collective-permute-start.80
  499.1 10.5 %collective-permute-start.81 = (f32[1,2,32]{2,0,1:T(1,128)S(1)}, f32[1,2,32]{2,0,1:T(1,128)S(1)}, u32[]{:S(2)}, u32[]{:S(2)}) collective-permute-start(f32[1,2,32]{2,0,1:T(1,128)S(1)} %get-tuple-element.345), channel_id=1, source_target_pairs={{4,0},{8,4},{12,8},{16,12},{20,16},{24,20},{28,24},{32,28},{36,32}... | collective-permute-start | bytes 776 | tf_op jit(solution)/shard_map/ppermute | solution.py:24
  518.4 10.3 %collective-permute-start.85 = (f32[1,2,32]{2,0,1:T(1,128)S(1)}, f32[1,2,32]{2,0,1:T(1,128)S(1)}, u32[]{:S(2)}, u32[]{:S(2)}) collective-permute-start(f32[1,2,32]{2,0,1:T(1,128)S(1)} %get-tuple-element.343), channel_id=1, source_target_pairs={{4,0},{8,4},{12,8},{16,12},{20,16},{24,20},{28,24},{32,28},{36,32}... | collective-permute-start | bytes 776 | tf_op jit(solution)/shard_map/ppermute | solution.py:24
  537.4 10.2 %collective-permute-start.89 = (f32[1,2,32]{2,0,1:T(1,128)S(1)}, f32[1,2,32]{2,0,1:T(1,128)S(1)}, u32[]{:S(2)}, u32[]{:S(2)}) collective-permute-start(f32[1,2,32]{2,0,1:T(1,128)S(1)} %get-tuple-element.341), channel_id=1, source_target_pairs={{4,0},{8,4},{12,8},{16,12},{20,16},{24,20},{28,24},{32,28},{36,32}... | collective-permute-start | bytes 776 | tf_op jit(solution)/shard_map/ppermute | solution.py:24
  556.7 10.3 %collective-permute-start.93 = (f32[1,4,64]{2,1,0:T(4,128)S(1)}, f32[1,4,64]{2,1,0:T(4,128)S(1)}, u32[]{:S(2)}, u32[]{:S(2)}) collective-permute-start(f32[1,4,64]{2,1,0:T(4,128)S(1)} %get-tuple-element.311), channel_id=1, source_target_pairs={{4,0},{8,4},{12,8},{16,12},{20,16},{24,20},{28,24},{32,28},{36,32}... | collective-permute-start | bytes 3080 | tf_op jit(solution)/shard_map/ppermute | solution.py:24
  570.5 5.6 collective-permute-start.96
  576.3 10.5 %collective-permute-start.97 = (f32[1,4,64]{2,1,0:T(4,128)S(1)}, f32[1,4,64]{2,1,0:T(4,128)S(1)}, u32[]{:S(2)}, u32[]{:S(2)}) collective-permute-start(f32[1,4,64]{2,1,0:T(4,128)S(1)} %get-tuple-element.309), channel_id=1, source_target_pairs={{4,0},{8,4},{12,8},{16,12},{20,16},{24,20},{28,24},{32,28},{36,32}... | collective-permute-start | bytes 3080 | tf_op jit(solution)/shard_map/ppermute | solution.py:24
  589.8 5.6 collective-permute-start.100
  596.1 10.3 %collective-permute-start.101 = (f32[1,8,128]{2,1,0:T(8,128)S(1)}, f32[1,8,128]{2,1,0:T(8,128)S(1)}, u32[]{:S(2)}, u32[]{:S(2)}) collective-permute-start(f32[1,8,128]{2,1,0:T(8,128)S(1)} %get-tuple-element.275), channel_id=1, source_target_pairs={{4,0},{8,4},{12,8},{16,12},{20,16},{24,20},{28,24},{32,28},{36,32}... | collective-permute-start | bytes 12296 | tf_op jit(solution)/shard_map/ppermute | solution.py:24
  609.5 5.6 collective-permute-start.104
  615.4 10.2 %collective-permute-start.105 = (f32[1,8,128]{2,1,0:T(8,128)S(1)}, f32[1,8,128]{2,1,0:T(8,128)S(1)}, u32[]{:S(2)}, u32[]{:S(2)}) collective-permute-start(f32[1,8,128]{2,1,0:T(8,128)S(1)} %get-tuple-element.273), channel_id=1, source_target_pairs={{4,0},{8,4},{12,8},{16,12},{20,16},{24,20},{28,24},{32,28},{36,32}... | collective-permute-start | bytes 12296 | tf_op jit(solution)/shard_map/ppermute | solution.py:24
  628.7 5.6 collective-permute-start.108
  (57 other events, 911.2 us)
where the time goes:
time: 643 us; the launch traced here: 635 us
  starting transfers between devices  446 us (69%)
  waiting for transfers between devices  105 us (16%)
  local copies, waits for them, and re-layouts  47.5 us (7%)
  other arithmetic  25.6 us (4%)
  matrix products  6.68 us (1%)
    ppermute x52, starting transfers between devices, extended_2(): lax.ppermute(head, axis, [((i + 1) % count, i) for i in range(count)])  273 us
    ppermute x52, starting transfers between devices, extended_2(): lax.ppermute(tail, axis, [(i, (i + 1) % count) for i in range(count)])  128 us
    ppermute x52, waiting for transfers between devices, extended_2(): lax.ppermute(tail, axis, [(i, (i + 1) % count) for i in range(count)])  78.1 us
    all_to_all x1, starting transfers between devices, shards(): lax.all_to_all(outgoing_cells, 'box', split_axis=1, concat_axis=1, tiled=...  20.4 us
    ppermute x5, starting transfers between devices, shifted(): return lax.ppermute(block, axis, route)  15.2 us
    all_to_all x1, waiting for transfers between devices, shards(): lax.all_to_all(outgoing, 'box', split_axis=1, concat_axis=1, tiled=True)  14.6 us
  transfers between devices with their start and end apart: 111, of which 48 were waited for; matrix products, arithmetic and copies ran while one was open for 4% of the time, Pallas kernels for 0%

commit v1 on v0

v1 whole, which is shorter than its diff:
```python
import jax
import jax.numpy as jnp
from jax import lax
from jax.experimental import pallas as pl
from jax.experimental.pallas import tpu as pltpu
from jax.sharding import PartitionSpec as P

F32 = jnp.float32
BF16 = jnp.bfloat16
I32 = jnp.int32

CX, CY, NZ = 16, 8, 128
PART = 2048
N_BOX = 128
CAP = 32
SLOTS = N_BOX * CAP
XE = CX + 2
OMEGA = 0.8

T0, T1, T2 = 30, 40, 20

LIMIT = 48 * 1024 * 1024

NT = (((1,), (1,)), ((), ()))


def tap_weights(frac):
    return (
        0.5 * (0.5 - frac) * (0.5 - frac),
        0.75 - frac * frac,
        0.5 * (0.5 + frac) * (0.5 + frac),
    )


def spread(index, at, taps):
    return jnp.where(
        index == at,
        taps[0],
        jnp.where(index == at + 1, taps[1], jnp.where(index == at + 2, taps[2], 0.0)),
    )


def route_kernel(vol, drag, mom, off, cell, dest, out, picked):
    target = dest[...]
    hot = lax.broadcasted_iota(I32, (N_BOX, PART), 0) == target
    hot_f = jnp.where(hot, 1.0, 0.0)
    hot_b = hot_f.astype(BF16)
    width = 256
    above = lax.broadcasted_iota(I32, (width, width), 0) < lax.broadcasted_iota(I32, (width, width), 1)
    before = jnp.where(above, 1.0, 0.0).astype(BF16)
    carry = jnp.zeros((N_BOX, 1), F32)
    places = []
    for k in range(PART // width):
        cut = slice(k * width, (k + 1) * width)
        rank = jnp.dot(hot_b[:, cut], before, preferred_element_type=F32) + carry
        places.append(jnp.sum(rank * hot_f[:, cut], axis=0, keepdims=True))
        carry = carry + jnp.sum(hot_f[:, cut], axis=1, keepdims=True)
    place = jnp.concatenate(places, axis=1).astype(I32)
    at_place = lax.broadcasted_iota(I32, (CAP, PART), 0) == place
    fields = [vol[...], drag[...], mom[0:1, :], mom[1:2, :]]
    fields += [off[0:1, :], off[1:2, :], off[2:3, :], cell[...].astype(F32)]
    for f, left in enumerate(fields):
        for part in range(3):
            rounded = left.astype(BF16).astype(F32)
            row = (part * 8 + f) * CAP
            picked[row : row + CAP, :] = jnp.where(at_place, rounded, 0.0).astype(BF16)
            left = left - rounded
    sums = lax.dot_general(picked[...], hot_b, NT, preferred_element_type=F32)
    half = 8 * CAP
    sums = sums[:half] + sums[half : 2 * half] + sums[2 * half :]
    out[...] = sums.T


def deposit_kernel(recv, rhs, wall, prev, pay, craw, par, cells, xs, amat, vmat, acc):
    fields = recv[...].T
    for c in range(4):
        par[c] = fields[c * CAP : (c + 1) * CAP]
    cell = fields[7 * CAP :].astype(I32)
    x_cell = cell // (NZ * CY)
    cells[0] = x_cell
    cells[1] = (cell // NZ) % CY
    cells[2] = cell % NZ
    for d in range(3):
        for k, tap in enumerate(tap_weights(fields[(4 + d) * CAP : (5 + d) * CAP])):
            par[4 + 3 * d + k] = tap
    for x in range(XE):
        xs[x] = spread(x, x_cell, (par[4], par[5], par[6]))
    sub24 = lax.broadcasted_iota(I32, (24, NZ), 0)
    sub8 = lax.broadcasted_iota(I32, (8, NZ), 0)
    sub128 = lax.broadcasted_iota(I32, (NZ, NZ), 0)

    def one(w):
        def row(k):
            return par[k, pl.ds(w, 1), :]

        lanes = pl.ds(pl.multiple_of(w * NZ, NZ), NZ)
        vals = [row(c) for c in range(4)]
        wx = [row(4 + k) for k in range(3)]
        wy = [row(7 + k) for k in range(3)]
        wz = [row(10 + k) for k in range(3)]
        xc, yc, zc = [cells[d, pl.ds(w, 1), :] for d in range(3)]
        y_tile = spread(sub8, yc - 1, wy)
        low = jnp.where(yc == 0, wy[0], 0.0)
        high = jnp.where(yc == CY - 1, wy[2], 0.0)
        x_tile = spread(sub24, xc, wx)
        edge = jnp.concatenate([x_tile * low, x_tile * high], axis=0)
        for c in range(4):
            amat[576 + 48 * c : 576 + 48 * (c + 1), lanes] = (vals[c] * edge).astype(BF16)
        for pair in range(XE // 2):
            plane = jnp.concatenate([xs[2 * pair + k, pl.ds(w, 1), :] * y_tile for k in range(2)], axis=0)
            for c in range(4):
                r = 144 * c + 16 * pair
                amat[r : r + 16, lanes] = (vals[c] * plane).astype(BF16)
        vmat[:, lanes] = spread(sub128, zc - 1, wz).astype(BF16)

    def pair_step(p, carry):
        one(2 * p)
        one(2 * p + 1)
        return carry

    lax.fori_loop(0, CAP // 2, pair_step, 0)
    acc[...] = lax.dot_general(amat[...], vmat[...], NT, preferred_element_type=F32)
    for x in range(XE):
        c = [acc[144 * k + 8 * x : 144 * k + 8 * x + 8, :] for k in range(4)]
        for k in range(4):
            craw[k, x] = c[k]
        if x < 9:
            right, opened = prev[x], prev[9 + x]
        else:
            right, opened = rhs[x - 9], wall[x - 9].astype(F32)
        whole = right - c[0] * right if x < CX else -(c[0] * right)
        pay[x] = opened * (whole + c[2] + c[3])
        pay[XE + x] = c[1]
        pay[2 * XE + x] = acc[pl.ds(576 + x, 8, stride=24), :]
        extra = jnp.concatenate([right[0:1], right[7:8], opened[0:1], opened[4:5]], axis=0)
        pay[3 * XE + x // 2, (x % 2) * 4 : (x % 2) * 4 + 4, :] = extra


def slab_kernel(slab, got, craw, send, keep, ssum, dsum, osum):
    s_me = slab[0]
    sub = lax.broadcasted_iota(I32, (8, NZ), 0)
    first, last = sub == 0, sub == 7

    def edges(tile, to_first, to_last):
        return tile + jnp.where(first, to_first, 0.0) + jnp.where(last, to_last, 0.0)

    for x in range(XE):
        g_row = (x % 2) * 4
        halos = [got[s, 2 * XE + x] for s in range(4)]
        for s in range(4):
            below, above = halos[(s + 3) % 4], halos[(s + 1) % 4]
            extra = got[s, 3 * XE + x // 2]
            rhs_f, rhs_l = extra[g_row : g_row + 1], extra[g_row + 1 : g_row + 2]
            o_f, o_l = extra[g_row + 2 : g_row + 3], extra[g_row + 3 : g_row + 4]
            from_below = o_f * (below[5:6] + below[7:8] - below[1:2] * rhs_f)
            from_above = o_l * (above[4:5] + above[6:7] - above[0:1] * rhs_l)
            at = x * 32 + s * 8
            ssum[at : at + 8, :] = edges(got[s, x], from_below, from_above)
            dsum[at : at + 8, :] = edges(got[s, XE + x], below[3:4], above[2:3])
            osum[x, 2 * s : 2 * s + 2, :] = extra[g_row + 2 : g_row + 4]
        below = got[(s_me + 3) % 4, 2 * XE + x]
        above = got[(s_me + 1) % 4, 2 * XE + x]
        for c in range(4):
            tile = edges(craw[c, x], below[2 * c + 1 : 2 * c + 2], above[2 * c : 2 * c + 1])
            if x < 9:
                send[128 + 9 * c + x] = tile
            else:
                keep[128 + 9 * c + x - 9] = tile
        for q in range(4):
            s_tile = ssum[pl.ds(x * 32 + q, 8, stride=4), :]
            d_tile = dsum[pl.ds(x * 32 + q, 8, stride=4), :]
            if x < CX:
                send[4 * x + q] = s_tile
                send[64 + 4 * x + q] = d_tile
            if x >= 2:
                keep[4 * (x - 2) + q] = s_tile
                keep[64 + 4 * (x - 2) + q] = d_tile
    for k, x in enumerate((1, 5, 9, 13)):
        send[164 + k] = osum[x]
    for k, x in enumerate((2, 5, 9, 13)):
        keep[164 + k] = osum[x]


def lane_index():
    return lax.broadcasted_iota(I32, (8, NZ), 1)


def take(tile, index):
    return jnp.take_along_axis(tile, index, axis=1)


def neighbour_sum(ref, t, count, whole_lanes):
    lane = lane_index()
    cur = [ref[t, q] for q in range(count)]
    sums = []
    for q in range(count):
        after = cur[q + 1] if q + 1 < count else pltpu.roll(cur[0], 7, 0)
        before = cur[q - 1] if q else pltpu.roll(cur[count - 1], 1, 0)
        left = pltpu.roll(cur[q], 1, 1)
        right = pltpu.roll(cur[q], NZ - 1, 1)
        if whole_lanes:
            left = jnp.where(lane == 0, 0.0, left)
            right = jnp.where(lane == NZ - 1, 0.0, right)
        beside = (ref[t - 1, q] + ref[t + 1, q]) + (after + before) + (left + right)
        sums.append(beside)
    return cur, sums


def rows_loop(low, high, step, body):
    passes = (high - low) // step
    assert low + passes * step == high

    def one(k, carry):
        for r in range(step):
            body(low + k * step + r)
        return carry

    lax.fori_loop(0, passes, one, 0)


def sweep(src, dst, coef, base, low, high, step, count, whole_lanes):
    def body(t):
        cur, sums = neighbour_sum(src, t, count, whole_lanes)
        for q in range(count):
            dst[t, q] = (1.0 - OMEGA) * cur[q] + base[t, q] + coef[t, q] * sums[q]

    rows_loop(low, high, step, body)


def residue_row(src, coef, base, weight, t, wt, count, whole_lanes):
    cur, sums = neighbour_sum(src, t, count, whole_lanes)
    return [weight[wt, q] * (base[t, q] + coef[t, q] * sums[q] - OMEGA * cur[q]) for q in range(count)]


def pair_lanes(tile):
    return tile + pltpu.roll(tile, NZ - 1, 1)


def start_kernel(keep, got, coupled, cc, cb, gg, v2, blocks, send, dk):
    for c in range(4):
        for x in range(CX):
            if x < 7:
                tile = keep[128 + 9 * c + x]
            elif x < 9:
                tile = keep[128 + 9 * c + x] + got[128 + 9 * c + x - 7]
            else:
                tile = got[128 + 9 * c + x - 7]
            coupled[c, x] = tile
    for k in range(4):
        blocks[k] = keep[164 + k]
        blocks[4 + k] = got[164 + k]

    def prepare(t, s_tile, d_tile, q, block):
        diag = 6.0 + d_tile
        coef = OMEGA * blocks[block] / diag
        cc[t, q] = coef
        cb[t, q] = coef * s_tile
        dk[t, q] = d_tile

    def from_keep(t):
        for q in range(4):
            prepare(t, keep[4 * t + q], keep[64 + 4 * t + q], q, (t + 1) // 4)

    def from_got(t):
        for q in range(4):
            at = 4 * (t - 14) + q
            prepare(t, got[at], got[64 + at], q, (t + 1) // 4)

    rows_loop(0, 14, 2, from_keep)
    for t in (14, 15):
        for q in range(4):
            own, at = 4 * t + q, 4 * (t - 14) + q
            prepare(t, keep[own] + got[at], keep[64 + own] + got[64 + at], q, (t + 1) // 4)
    rows_loop(16, 30, 2, from_got)
    sweep(cb, v2, cc, cb, 1, 29, 4, 4, True)

    lane = lane_index()
    even = (2 * lane) % NZ

    def coarse(k):
        b_sum, d_sum = [0.0, 0.0], [0.0, 0.0]
        for dx in range(2):
            t = 7 + 2 * k + dx
            for q in range(4):
                gg[2 * k + dx, q] = (1.0 / OMEGA) * (6.0 + dk[t, q])
                d_sum[q // 2] = d_sum[q // 2] + dk[t, q]
            for q, tile in enumerate(residue_row(v2, cc, cb, gg, t, 2 * k + dx, 4, True)):
                b_sum[q // 2] = b_sum[q // 2] + tile
        for q in range(2):
            b_tile = take(pair_lanes(b_sum[q]), even)
            d_tile = take(pair_lanes(d_sum[q]), even)
            send[2 * k + q] = 0.125 * jnp.where(lane < 64, b_tile, d_tile)

    rows_loop(0, 8, 2, coarse)
    for k in range(4):
        send[16 + k] = blocks[2 + k]


def levels_setup(parts, c1, g1, o1, c2, cb1):
    lane = lane_index()
    even = (2 * lane) % NZ
    for n, part in enumerate(parts):
        def block_step(blk, carry):
            half = jnp.where(lane < 64, take(part[16 + blk], even), 0.0)
            o1[4 * n + blk] = half
            o2 = jnp.where(lane < 32, take(half, even), 0.0)
            d_sum = 0.0
            for dx in range(2):
                for q in range(2):
                    tile = part[4 * blk + 2 * dx + q]
                    damp = jnp.where(lane < 64, pltpu.roll(tile, 64, 1), 0.0)
                    diag = 1.5 + damp
                    coef = OMEGA * half / diag
                    a = 8 * n + 2 * blk + dx
                    c1[a, q] = 0.25 * coef
                    cb1[a, q] = coef * jnp.where(lane < 64, tile, 0.0)
                    g1[a, q] = (1.0 / OMEGA) * diag
                    d_sum = d_sum + damp
            damp = jnp.where(lane < 32, 0.125 * take(pair_lanes(d_sum), even), 0.0)
            c2[4 * n + blk, 0] = 0.0625 * (OMEGA * o2 / (0.375 + damp))
            return carry

        lax.fori_loop(0, 4, block_step, 0)


def levels_solve(c1, g1, o1, c2, cb1, w_a, w_b, cb2, u_a, u_b):
    lane = lane_index()
    even, halved = (2 * lane) % NZ, lane // 2
    sweep(cb1, w_a, c1, cb1, 2, 38, 4, 2, False)

    def coarse(m):
        total = 0.0
        for dx in range(2):
            for tile in residue_row(w_a, c1, cb1, g1, 2 * m + dx, 2 * m + dx, 2, False):
                total = total + tile
        b2 = 0.125 * take(pair_lanes(total), even)
        cb2[m, 0] = 16.0 * c2[m, 0] * b2

    rows_loop(2, 18, 4, coarse)
    sweep(cb2, u_a, c2, cb2, 3, 17, 7, 1, False)
    sweep(u_a, u_b, c2, cb2, 4, 16, 6, 1, False)
    sweep(u_b, u_a, c2, cb2, 5, 15, 5, 1, False)

    def correct(m):
        step = take(u_a[m, 0], halved) * o1[m]
        for dx in range(2):
            for q in range(2):
                w_a[2 * m + dx, q] = w_a[2 * m + dx, q] + step

    rows_loop(5, 15, 2, correct)
    sweep(w_a, w_b, c1, cb1, 11, 29, 6, 2, False)
    sweep(w_b, w_a, c1, cb1, 13, 27, 7, 2, False)


def correct_fine(v_in, v_out, w, blocks, low, high):
    halved = lane_index() // 2

    def body(a):
        opened = blocks[(a - 12) // 2]
        for q in range(2):
            step = take(w[a, q], halved) * opened
            for dx in range(2):
                for k in range(2):
                    t = 2 * a - 25 + dx
                    v_out[t, 2 * q + k] = v_in[t, 2 * q + k] + step

    rows_loop(low, high, 2, body)


def middle_kernel(p0, p1, p2, p3, p4, cc, cb, gg, v2, blocks, v_out, c1, g1, o1, c2, send,
                  cb1, w_a, w_b, cb2, u_a, u_b, v_a, v_b):
    levels_setup((p0, p1, p2, p3, p4), c1, g1, o1, c2, cb1)
    levels_solve(c1, g1, o1, c2, cb1, w_a, w_b, cb2, u_a, u_b)
    correct_fine(v2, v_a, w_a, blocks, 13, 27)
    sweep(v_a, v_b, cc, cb, 2, 28, 2, 4, True)
    sweep(v_b, v_a, cc, cb, 3, 27, 4, 4, True)
    sweep(v_a, v_b, cc, cb, 4, 26, 2, 4, True)
    sweep(v_b, v_out, cc, cb, 5, 25, 4, 4, True)
    lane = lane_index()
    even = (2 * lane) % NZ

    def coarse(k):
        b_sum = [0.0, 0.0]
        for dx in range(2):
            for q, tile in enumerate(residue_row(v_out, cc, cb, gg, 7 + 2 * k + dx, 2 * k + dx, 4, True)):
                b_sum[q // 2] = b_sum[q // 2] + tile
        tiles = [take(pair_lanes(b_sum[q]), even) for q in range(2)]
        send[k] = 0.125 * jnp.where(lane < 64, tiles[0], tiles[1])

    rows_loop(0, 8, 2, coarse)


def last_kernel(slab, p0, p1, p2, p3, p4, cc, cb, v2, blocks, c1, g1, o1, c2, out,
                cb1, w_a, w_b, cb2, u_a, u_b, v_a, v_b, flat):
    lane = lane_index()
    for n, part in enumerate((p0, p1, p2, p3, p4)):
        for k in range(8):
            tile = part[k]
            a = 8 * n + k
            for q, cut in enumerate((tile, pltpu.roll(tile, 64, 1))):
                cb1[a, q] = 4.0 * c1[a, q] * jnp.where(lane < 64, cut, 0.0)
    levels_solve(c1, g1, o1, c2, cb1, w_a, w_b, cb2, u_a, u_b)
    correct_fine(v2, v_a, w_a, blocks, 15, 25)
    sweep(v_a, v_b, cc, cb, 6, 24, 3, 4, True)
    sweep(v_b, v_a, cc, cb, 7, 23, 4, 4, True)
    s_me = slab[0]
    for x in range(CX):
        for q in range(4):
            flat[pl.ds(x * 32 + q, 8, stride=4), :] = v_a[7 + x, q]
    for x in range(CX):
        out[x] = flat[pl.ds(pl.multiple_of(x * 32 + 8 * s_me, 8), 8), :]


def call(kernel, outs, scratch, operands, smem_first=False, cost=1000000):
    specs = [pl.BlockSpec(memory_space=pltpu.VMEM) for _ in operands]
    if smem_first:
        specs[0] = pl.BlockSpec(memory_space=pltpu.SMEM)
    shapes = [jax.ShapeDtypeStruct(shape, F32) for shape in outs]
    return pl.pallas_call(
        kernel,
        out_shape=shapes,
        in_specs=specs,
        out_specs=[pl.BlockSpec(memory_space=pltpu.VMEM) for _ in outs],
        scratch_shapes=[pltpu.VMEM(shape, kind) for shape, kind in scratch],
        compiler_params=pltpu.CompilerParams(vmem_limit_bytes=LIMIT),
        cost_estimate=pl.CostEstimate(flops=cost, bytes_accessed=cost, transcendentals=0),
    )(*operands)


def fetch(block, distance):
    count = lax.axis_size("box")
    return lax.ppermute(block, "box", [((i + distance) % count, i) for i in range(count)])


def shards(volume, drag, momentum, offsets, cell_index, destinations, rhs, wall):
    slab = lax.axis_index("slab").astype(I32).reshape(1)
    prev = fetch(jnp.concatenate([rhs[7:], wall[7:].astype(F32)], axis=0), -1)
    (outgoing,) = call(
        route_kernel,
        [(N_BOX, 8 * CAP)],
        [((24 * CAP, PART), BF16)],
        [volume.reshape(1, PART), drag.reshape(1, PART), momentum, offsets,
         cell_index.reshape(1, PART), destinations.reshape(1, PART)],
    )
    incoming = lax.all_to_all(outgoing, "box", split_axis=0, concat_axis=0, tiled=True)
    pay, craw = call(
        deposit_kernel,
        [(3 * XE + XE // 2, 8, NZ), (4, XE, 8, NZ)],
        [((13, CAP, NZ), F32), ((3, CAP, NZ), I32), ((XE, CAP, NZ), F32), ((768, SLOTS), BF16),
         ((NZ, SLOTS), BF16), ((768, NZ), F32)],
        [incoming, rhs, wall, prev],
    )
    slabs = lax.all_gather(pay, "slab")
    send, keep = call(
        slab_kernel,
        [(168, 8, NZ), (168, 8, NZ)],
        [((XE * 32, NZ), F32), ((XE * 32, NZ), F32), ((XE, 8, NZ), F32)],
        [slab, slabs, craw],
        smem_first=True,
    )
    got = fetch(send, 1)
    coupled, cc, cb, gg, v2, blocks, first = call(
        start_kernel,
        [(4, CX, 8, NZ), (T0, 4, 8, NZ), (T0, 4, 8, NZ), (CX, 4, 8, NZ), (T0, 4, 8, NZ), (8, 8, NZ), (20, 8, NZ)],
        [((T0, 4, 8, NZ), F32)],
        [keep, got],
    )
    parts = [fetch(first, -2), fetch(first, -1), first, fetch(first, 1), fetch(first, 2)]
    level_scratch = [
        ((T1, 2, 8, NZ), F32), ((T1, 2, 8, NZ), F32), ((T1, 2, 8, NZ), F32),
        ((T2, 1, 8, NZ), F32), ((T2, 1, 8, NZ), F32), ((T2, 1, 8, NZ), F32),
        ((T0, 4, 8, NZ), F32), ((T0, 4, 8, NZ), F32),
    ]
    v3, c1, g1, o1, c2, second = call(
        middle_kernel,
        [(T0, 4, 8, NZ), (T1, 2, 8, NZ), (T1, 2, 8, NZ), (T2, 8, NZ), (T2, 1, 8, NZ), (8, 8, NZ)],
        level_scratch,
        parts + [cc, cb, gg, v2, blocks],
    )
    parts = [fetch(second, -2), fetch(second, -1), second, fetch(second, 1), fetch(second, 2)]
    (pressure,) = call(
        last_kernel,
        [(CX, 8, NZ)],
        level_scratch + [((CX * 32, NZ), F32)],
        [slab] + parts + [cc, cb, v3, blocks, c1, g1, o1, c2],
        smem_first=True,
    )
    return coupled, pressure


def solution(mesh):
    in_specs = (
        P(("box", "slab")),
        P(("box", "slab")),
        P(None, ("box", "slab")),
        P(None, ("box", "slab")),
        P(("box", "slab")),
        P(("box", "slab"), None),
        P("box", "slab", None),
        P("box", "slab", None),
    )
    out_specs = (P(None, "box", "slab", None), P("box", "slab", None))
    return jax.shard_map(shards, mesh=mesh, in_specs=in_specs, out_specs=out_specs, check_vma=False)
```

time: 643 us -> 132 us (0.21); the launches traced: 635 us -> 131 us
  starting transfers between devices: 446 us -> 51.7 us
  waiting for transfers between devices: 105 us -> 32 us
  local copies, waits for them, and re-layouts: 47.5 us -> 6.66 us
  Pallas kernels: 0 us -> 26.8 us
  other arithmetic: 25.6 us -> 0.01 us
  blocking collectives: 0 us -> 13.4 us
  matrix products: 6.68 us -> 0 us
    ppermute x109 -> x10, starting transfers between devices: 416 us -> 31.3 us  [fetch(): lax.ppermute(block, 'box', [((i + distance) % count, i) for i in range(co...]
    ppermute x109 -> x10, waiting for transfers between devices: 84.3 us -> 21.1 us  [fetch(): lax.ppermute(block, 'box', [((i + distance) % count, i) for i in range(co...]
    pallas_call x0 -> x6, Pallas kernels: none -> 26.8 us  [call(): pl.pallas_call(kernel, out_shape=shapes, in_specs=specs, out_specs=[pl.Bl...]
    reshape x17 -> x0, local copies, waits for them, and re-layouts: 19.4 us -> none  [the longest x4 12.1 us: coarsen(): field.reshape(sx // 2, 2, sy // 2, 2, sz // 2, 2).mean(axis=(1, 3, 5))]
    all_gather x0 -> x1, blocking collectives: none -> 13.4 us  [shards(): slabs = lax.all_gather(pay, 'slab')]
    all_to_all x2 -> x1, waiting for transfers between devices: 21.1 us -> 10.9 us  [shards(): lax.all_to_all(outgoing, 'box', split_axis=0, concat_axis=0, tiled=True)]
    all_to_all x2 -> x1, starting transfers between devices: 30 us -> 20.4 us  [shards(): lax.all_to_all(outgoing, 'box', split_axis=0, concat_axis=0, tiled=True)]
    reduce_sum x7 -> x0, other arithmetic: 8.65 us -> none  [the longest x6 8.02 us: coarsen(): field.reshape(sx // 2, 2, sy // 2, 2, sz // 2, 2).mean(axis=(1, 3, 5))]
  transfers between devices with their start and end apart: 111 -> 11, of which waited for: 48 -> 4; matrix products, arithmetic and copies ran while one was open for 4% -> 0% of each run, Pallas kernels for 0% -> 0%
where the time goes in v1:
time: 132 us; the launch traced here: 131 us
  starting transfers between devices  51.7 us (39%)
  waiting for transfers between devices  32 us (24%)
  Pallas kernels  26.8 us (20%)
  blocking collectives  13.4 us (10%)
  local copies, waits for them, and re-layouts  6.66 us (5%)
    ppermute x10, starting transfers between devices, fetch(): lax.ppermute(block, 'box', [((i + distance) % count, i) for i in range(co...  31.3 us
    pallas_call x6, Pallas kernels, call(): pl.pallas_call(kernel, out_shape=shapes, in_specs=specs, out_specs=[pl.Bl...  26.8 us
    ppermute x10, waiting for transfers between devices, fetch(): lax.ppermute(block, 'box', [((i + distance) % count, i) for i in range(co...  21.1 us
    all_to_all x1, starting transfers between devices, shards(): lax.all_to_all(outgoing, 'box', split_axis=0, concat_axis=0, tiled=True)  20.4 us
    all_gather x1, blocking collectives, shards(): slabs = lax.all_gather(pay, 'slab')  13.4 us
    all_to_all x1, waiting for transfers between devices, shards(): lax.all_to_all(outgoing, 'box', split_axis=0, concat_axis=0, tiled=True)  10.9 us
    unnamed x17, local copies, waits for them, and re-layouts  5.1 us
  transfers between devices with their start and end apart: 11, of which 4 were waited for; matrix products, arithmetic and copies ran while one was open for 0% of the time, Pallas kernels for 0%

profile of v1, /device:TPU:1, one launch (start us, length us, event | category | flops | bytes accessed | tf_op | source)
XLA Modules:
  0.0 131.4 jit_solution(12185088438870457671)
XLA Ops:
  0.6 0.0 copy-start.2
  0.6 0.7 copy-done.2
  1.4 0.0 copy-start.3
  1.4 0.7 copy-done.3
  2.1 0.0 copy-start.4
  2.1 0.7 copy-done.4
  2.8 0.0 copy-start.5
  2.8 0.7 copy-done.5
  3.5 0.0 copy-start.6
  3.5 0.7 copy-done.6
  4.2 0.0 copy-start.7
  4.2 0.7 copy-done.7
  4.9 1.4 %shard_map.95 = f32[128,256]{1,0:T(8,128)S(1)} custom-call(f32[1,2048]{1,0:T(1,128)S(1)} %bitcast.13, f32[1,2048]{1,0:T(1,128)S(1)} %bitcast.14, f32[2,2048]{1,0:T(2,128)S(1)} %copy-done.3, f32[3,2048]{1,0:T(4,128)S(1)} %copy-done.2, s32[1,2048]{1,0:T(1,128)S(1)} %bitcast.15, s32[1,2048]{1,0:T(1,128)S(1)} %bitcast.16), custom_call_target="tpu_custom_call" | custom-call | flops 1000000 | bytes 1000000 | tf_op jit(solution)/shard_map/pallas_call | solution.py:419
  6.3 0.8 copy.10
  7.1 20.4 %all-to-all-start = ((f32[128,1,256]{2,1,0:T(1,128)}), f32[128,1,256]{2,1,0:T(1,128)S(1)}, u32[]{:S(2)}, u32[]{:S(2)}) async-start(f32[128,1,256]{2,1,0:T(1,128)} %copy.10), calls=%async_computation | async-start | bytes 262144 | tf_op jit(solution)/shard_map/all_to_all | solution.py:445
  27.5 0.0 copy-start.1
  27.6 0.8 copy-done.1
  28.4 0.0 slice-start
  28.4 0.8 slice-done
  29.2 3.5 %collective-permute-start = (f32[18,8,128]{2,1,0:T(8,128)S(1)}, f32[18,8,128]{2,1,0:T(8,128)S(1)}, u32[]{:S(2)}, u32[]{:S(2)}) collective-permute-start(f32[18,8,128]{2,1,0:T(8,128)S(1)} %pad_maximum_fusion), channel_id=1, source_target_pairs={{508,0},{0,4},{4,8},{8,12},{12,16},{16,20},{20,24},{24,28},{28,32}... | collective-permute-start | bytes 221192 | tf_op jit(solution)/shard_map/ppermute | solution.py:432
  32.7 0.0 copy-start
  32.7 10.9 %all-to-all-done = f32[128,1,256]{2,1,0:T(1,128)S(1)} async-done(((f32[128,1,256]{2,1,0:T(1,128)}), f32[128,1,256]{2,1,0:T(1,128)S(1)}, u32[]{:S(2)}, u32[]{:S(2)}) %all-to-all-start) | async-done | bytes 131104 | tf_op jit(solution)/shard_map/all_to_all | solution.py:445
  43.6 0.0 collective-permute-done.prev
  43.6 0.0 copy-done
  43.6 4.8 %shard_map.96 = (f32[63,8,128]{2,1,0:T(8,128)S(1)}, f32[4,18,8,128]{3,2,1,0:T(8,128)S(1)}) custom-call(f32[128,256]{1,0:T(8,128)S(1)} %bitcast.12, f32[16,8,128]{2,1,0:T(8,128)S(1)} %copy-done, s32[16,8,128]{2,1,0:T(8,128)S(1)} %copy-done.1, f32[18,8,128]{2,1,0:T(8,128)S(1)} %collective-permute-done.prev), custom_call_target="tpu_custom_call" | custom-call | flops 1000000 | bytes 1000000 | tf_op jit(solution)/shard_map/pallas_call | solution.py:419
  48.4 13.4 %all-gather = f32[252,8,128]{2,1,0:T(8,128)S(1)} all-gather(f32[63,8,128]{2,1,0:T(8,128)S(1)} %get-tuple-element.19), channel_id=2, replica_groups=mesh['box'=128,'slab'=4] {'slab'}, dimensions={0}, use_global_device_ids=true | all-gather | bytes 1290240 | tf_op jit(solution)/shard_map/all_gather | solution.py:453
  61.8 0.3 shard_map.97
  62.1 4.1 %collective-permute-start.1 = (f32[168,8,128]{2,1,0:T(8,128)S(1)}, f32[168,8,128]{2,1,0:T(8,128)S(1)}, u32[]{:S(2)}, u32[]{:S(2)}) collective-permute-start(f32[168,8,128]{2,1,0:T(8,128)S(1)} %get-tuple-element.22), channel_id=1, source_target_pairs={{4,0},{8,4},{12,8},{16,12},{20,16},{24,20},{28,24},{32,28},{36,32}... | collective-permute-start | bytes 2064392 | tf_op jit(solution)/shard_map/ppermute | solution.py:432
  66.3 9.9 %collective-permute-done.1.got = f32[168,8,128]{2,1,0:T(8,128)S(1)} collective-permute-done((f32[168,8,128]{2,1,0:T(8,128)S(1)}, f32[168,8,128]{2,1,0:T(8,128)S(1)}, u32[]{:S(2)}, u32[]{:S(2)}) %collective-permute-start.1) | collective-permute-done | bytes 688160 | tf_op jit(solution)/shard_map/ppermute | solution.py:432
  76.1 2.5 %shard_map.98 = (f32[4,16,8,128]{3,2,1,0:T(8,128)}, f32[30,4,8,128]{3,2,1,0:T(8,128)S(1)}, f32[30,4,8,128]{3,2,1,0:T(8,128)S(1)}, f32[16,4,8,128]{3,2,1,0:T(8,12...) custom-call(f32[168,8,128]{2,1,0:T(8,128)S(1)} %get-tuple-element.21.keep, ...), custom_call_target="tpu_custom_call" | custom-call | flops 1000000 | bytes 1000000 | tf_op jit(solution)/shard_map/pallas_call | solution.py:419
  78.6 5.3 %collective-permute-start.5 = (f32[20,8,128]{2,1,0:T(8,128)S(1)}, f32[20,8,128]{2,1,0:T(8,128)S(1)}, u32[]{:S(2)}, u32[]{:S(2)}) collective-permute-start(f32[20,8,128]{2,1,0:T(8,128)S(1)} %get-tuple-element.24.p2), channel_id=1, source_target_pairs={{8,0},{12,4},{16,8},{20,12},{24,16},{28,20},{32,24},{36,28},{40,32... | collective-permute-start | bytes 245768 | tf_op jit(solution)/shard_map/ppermute | solution.py:432
  83.9 1.9 %collective-permute-start.4 = (f32[20,8,128]{2,1,0:T(8,128)S(1)}, f32[20,8,128]{2,1,0:T(8,128)S(1)}, u32[]{:S(2)}, u32[]{:S(2)}) collective-permute-start(f32[20,8,128]{2,1,0:T(8,128)S(1)} %get-tuple-element.24.p2), channel_id=1, source_target_pairs={{4,0},{8,4},{12,8},{16,12},{20,16},{24,20},{28,24},{32,28},{36,32}... | collective-permute-start | bytes 245768 | tf_op jit(solution)/shard_map/ppermute | solution.py:432
  85.9 3.7 %collective-permute-start.3 = (f32[20,8,128]{2,1,0:T(8,128)S(1)}, f32[20,8,128]{2,1,0:T(8,128)S(1)}, u32[]{:S(2)}, u32[]{:S(2)}) collective-permute-start(f32[20,8,128]{2,1,0:T(8,128)S(1)} %get-tuple-element.24.p2), channel_id=1, source_target_pairs={{508,0},{0,4},{4,8},{8,12},{12,16},{16,20},{20,24},{24,28},{28,32}... | collective-permute-start | bytes 245768 | tf_op jit(solution)/shard_map/ppermute | solution.py:432
  89.5 1.9 %collective-permute-start.2 = (f32[20,8,128]{2,1,0:T(8,128)S(1)}, f32[20,8,128]{2,1,0:T(8,128)S(1)}, u32[]{:S(2)}, u32[]{:S(2)}) collective-permute-start(f32[20,8,128]{2,1,0:T(8,128)S(1)} %get-tuple-element.24.p2), channel_id=1, source_target_pairs={{504,0},{508,4},{0,8},{4,12},{8,16},{12,20},{16,24},{20,28},{24,32... | collective-permute-start | bytes 245768 | tf_op jit(solution)/shard_map/ppermute | solution.py:432
  91.5 0.0 collective-permute-done.5.p4
  91.5 0.0 collective-permute-done.4.p3
  91.5 0.0 collective-permute-done.3.p1
  91.5 6.6 %collective-permute-done.2.p0 = f32[20,8,128]{2,1,0:T(8,128)S(1)} collective-permute-done((f32[20,8,128]{2,1,0:T(8,128)S(1)}, f32[20,8,128]{2,1,0:T(8,128)S(1)}, u32[]{:S(2)}, u32[]{:S(2)}) %collective-permute-start.2) | collective-permute-done | bytes 81952 | tf_op jit(solution)/shard_map/ppermute | solution.py:432
  98.1 12.4 %shard_map.99 = (f32[30,4,8,128]{3,2,1,0:T(8,128)S(1)}, f32[40,2,8,128]{3,2,1,0:T(8,128)S(1)}, f32[40,2,8,128]{3,2,1,0:T(8,128)S(1)}, f32[20,8,128]{2,1,0:T(8,12...) custom-call(f32[20,8,128]{2,1,0:T(8,128)S(1)} %collective-permute-done.2.p0, ...), custom_call_target="tpu_custom_call" | custom-call | flops 1000000 | bytes 1000000 | tf_op jit(solution)/shard_map/pallas_call | solution.py:419
  110.6 1.9 %collective-permute-start.9 = (f32[8,8,128]{2,1,0:T(8,128)S(1)}, f32[8,8,128]{2,1,0:T(8,128)S(1)}, u32[]{:S(2)}, u32[]{:S(2)}) collective-permute-start(f32[8,8,128]{2,1,0:T(8,128)S(1)} %get-tuple-element.30.p2), channel_id=1, source_target_pairs={{8,0},{12,4},{16,8},{20,12},{24,16},{28,20},{32,24},{36,28},{40,32... | collective-permute-start | bytes 98312 | tf_op jit(solution)/shard_map/ppermute | solution.py:432
  112.5 1.9 %collective-permute-start.8 = (f32[8,8,128]{2,1,0:T(8,128)S(1)}, f32[8,8,128]{2,1,0:T(8,128)S(1)}, u32[]{:S(2)}, u32[]{:S(2)}) collective-permute-start(f32[8,8,128]{2,1,0:T(8,128)S(1)} %get-tuple-element.30.p2), channel_id=1, source_target_pairs={{4,0},{8,4},{12,8},{16,12},{20,16},{24,20},{28,24},{32,28},{36,32}... | collective-permute-start | bytes 98312 | tf_op jit(solution)/shard_map/ppermute | solution.py:432
  114.4 3.6 %collective-permute-start.7 = (f32[8,8,128]{2,1,0:T(8,128)S(1)}, f32[8,8,128]{2,1,0:T(8,128)S(1)}, u32[]{:S(2)}, u32[]{:S(2)}) collective-permute-start(f32[8,8,128]{2,1,0:T(8,128)S(1)} %get-tuple-element.30.p2), channel_id=1, source_target_pairs={{508,0},{0,4},{4,8},{8,12},{12,16},{16,20},{20,24},{24,28},{28,32}... | collective-permute-start | bytes 98312 | tf_op jit(solution)/shard_map/ppermute | solution.py:432
  118.1 3.4 %collective-permute-start.6 = (f32[8,8,128]{2,1,0:T(8,128)S(1)}, f32[8,8,128]{2,1,0:T(8,128)S(1)}, u32[]{:S(2)}, u32[]{:S(2)}) collective-permute-start(f32[8,8,128]{2,1,0:T(8,128)S(1)} %get-tuple-element.30.p2), channel_id=1, source_target_pairs={{504,0},{508,4},{0,8},{4,12},{8,16},{12,20},{16,24},{20,28},{24,32... | collective-permute-start | bytes 98312 | tf_op jit(solution)/shard_map/ppermute | solution.py:432
  121.5 0.0 collective-permute-done.9.p4
  121.5 0.0 collective-permute-done.8.p3
  121.5 0.0 collective-permute-done.7.p1
  121.5 4.6 %collective-permute-done.6.p0 = f32[8,8,128]{2,1,0:T(8,128)S(1)} collective-permute-done((f32[8,8,128]{2,1,0:T(8,128)S(1)}, f32[8,8,128]{2,1,0:T(8,128)S(1)}, u32[]{:S(2)}, u32[]{:S(2)}) %collective-permute-start.6) | collective-permute-done | bytes 32800 | tf_op jit(solution)/shard_map/ppermute | solution.py:432
  126.1 5.3 %shard_map.100 = f32[16,8,128]{2,1,0:T(8,128)} custom-call(s32[1]{0:T(128)} %bitcast.slab, f32[8,8,128]{2,1,0:T(8,128)S(1)} %collective-permute-done.6.p0, f32[8,8,128]{2,1,0:T(8,128)S(1)} %collective-permute-done.7.p1, f32[8,8,128]{2,1,0:T(8,128)S(1)} %get-tuple-element.30.p2, f32[8,8,128]{2,1,0:T(8,128)S(1)} %collective-permute-done.8.p3, ...), custom_call_target="tpu_custom_call" | custom-call | flops 1000000 | bytes 1000000 | tf_op jit(solution)/shard_map/pallas_call | solution.py:419
  (3 shorter events, 0.0 us)
Async XLA Ops:
  0.6 0.8 copy-start.2
  1.4 0.7 copy-start.3
  2.1 0.7 copy-start.4
  2.8 0.7 copy-start.5
  3.5 0.7 copy-start.6
  4.2 0.7 copy-start.7
  7.1 36.5 %all-to-all-start = ((f32[128,1,256]{2,1,0:T(1,128)}), f32[128,1,256]{2,1,0:T(1,128)S(1)}, u32[]{:S(2)}, u32[]{:S(2)}) async-start(f32[128,1,256]{2,1,0:T(1,128)} %copy.10), calls=%async_computation | async-start | bytes 262144 | tf_op jit(solution)/shard_map/all_to_all | solution.py:445
  27.5 0.8 copy-start.1
  28.4 0.8 slice-start
  29.2 14.5 %collective-permute-start = (f32[18,8,128]{2,1,0:T(8,128)S(1)}, f32[18,8,128]{2,1,0:T(8,128)S(1)}, u32[]{:S(2)}, u32[]{:S(2)}) collective-permute-start(f32[18,8,128]{2,1,0:T(8,128)S(1)} %pad_maximum_fusion), channel_id=1, source_target_pairs={{508,0},{0,4},{4,8},{8,12},{12,16},{16,20},{20,24},{24,28},{28,32}... | collective-permute-start | bytes 221192 | tf_op jit(solution)/shard_map/ppermute | solution.py:432
  32.7 10.9 %copy-start = (f32[16,8,128]{2,1,0:T(8,128)S(1)}, f32[16,8,128]{2,1,0:T(8,128)}, u32[]{:S(2)}) copy-start(f32[16,8,128]{2,1,0:T(8,128)} %rhs.1) | copy-start | bytes 196612
  62.1 14.0 %collective-permute-start.1 = (f32[168,8,128]{2,1,0:T(8,128)S(1)}, f32[168,8,128]{2,1,0:T(8,128)S(1)}, u32[]{:S(2)}, u32[]{:S(2)}) collective-permute-start(f32[168,8,128]{2,1,0:T(8,128)S(1)} %get-tuple-element.22), channel_id=1, source_target_pairs={{4,0},{8,4},{12,8},{16,12},{20,16},{24,20},{28,24},{32,28},{36,32}... | collective-permute-start | bytes 2064392 | tf_op jit(solution)/shard_map/ppermute | solution.py:432
  78.6 12.8 %collective-permute-start.5 = (f32[20,8,128]{2,1,0:T(8,128)S(1)}, f32[20,8,128]{2,1,0:T(8,128)S(1)}, u32[]{:S(2)}, u32[]{:S(2)}) collective-permute-start(f32[20,8,128]{2,1,0:T(8,128)S(1)} %get-tuple-element.24.p2), channel_id=1, source_target_pairs={{8,0},{12,4},{16,8},{20,12},{24,16},{28,20},{32,24},{36,28},{40,32... | collective-permute-start | bytes 245768 | tf_op jit(solution)/shard_map/ppermute | solution.py:432
  83.9 7.5 %collective-permute-start.4 = (f32[20,8,128]{2,1,0:T(8,128)S(1)}, f32[20,8,128]{2,1,0:T(8,128)S(1)}, u32[]{:S(2)}, u32[]{:S(2)}) collective-permute-start(f32[20,8,128]{2,1,0:T(8,128)S(1)} %get-tuple-element.24.p2), channel_id=1, source_target_pairs={{4,0},{8,4},{12,8},{16,12},{20,16},{24,20},{28,24},{32,28},{36,32}... | collective-permute-start | bytes 245768 | tf_op jit(solution)/shard_map/ppermute | solution.py:432
  85.9 5.6 %collective-permute-start.3 = (f32[20,8,128]{2,1,0:T(8,128)S(1)}, f32[20,8,128]{2,1,0:T(8,128)S(1)}, u32[]{:S(2)}, u32[]{:S(2)}) collective-permute-start(f32[20,8,128]{2,1,0:T(8,128)S(1)} %get-tuple-element.24.p2), channel_id=1, source_target_pairs={{508,0},{0,4},{4,8},{8,12},{12,16},{16,20},{20,24},{24,28},{28,32}... | collective-permute-start | bytes 245768 | tf_op jit(solution)/shard_map/ppermute | solution.py:432
  89.5 8.6 %collective-permute-start.2 = (f32[20,8,128]{2,1,0:T(8,128)S(1)}, f32[20,8,128]{2,1,0:T(8,128)S(1)}, u32[]{:S(2)}, u32[]{:S(2)}) collective-permute-start(f32[20,8,128]{2,1,0:T(8,128)S(1)} %get-tuple-element.24.p2), channel_id=1, source_target_pairs={{504,0},{508,4},{0,8},{4,12},{8,16},{12,20},{16,24},{20,28},{24,32... | collective-permute-start | bytes 245768 | tf_op jit(solution)/shard_map/ppermute | solution.py:432
  110.6 10.9 %collective-permute-start.9 = (f32[8,8,128]{2,1,0:T(8,128)S(1)}, f32[8,8,128]{2,1,0:T(8,128)S(1)}, u32[]{:S(2)}, u32[]{:S(2)}) collective-permute-start(f32[8,8,128]{2,1,0:T(8,128)S(1)} %get-tuple-element.30.p2), channel_id=1, source_target_pairs={{8,0},{12,4},{16,8},{20,12},{24,16},{28,20},{32,24},{36,28},{40,32... | collective-permute-start | bytes 98312 | tf_op jit(solution)/shard_map/ppermute | solution.py:432
  112.5 9.0 %collective-permute-start.8 = (f32[8,8,128]{2,1,0:T(8,128)S(1)}, f32[8,8,128]{2,1,0:T(8,128)S(1)}, u32[]{:S(2)}, u32[]{:S(2)}) collective-permute-start(f32[8,8,128]{2,1,0:T(8,128)S(1)} %get-tuple-element.30.p2), channel_id=1, source_target_pairs={{4,0},{8,4},{12,8},{16,12},{20,16},{24,20},{28,24},{32,28},{36,32}... | collective-permute-start | bytes 98312 | tf_op jit(solution)/shard_map/ppermute | solution.py:432
  114.4 7.0 %collective-permute-start.7 = (f32[8,8,128]{2,1,0:T(8,128)S(1)}, f32[8,8,128]{2,1,0:T(8,128)S(1)}, u32[]{:S(2)}, u32[]{:S(2)}) collective-permute-start(f32[8,8,128]{2,1,0:T(8,128)S(1)} %get-tuple-element.30.p2), channel_id=1, source_target_pairs={{508,0},{0,4},{4,8},{8,12},{12,16},{16,20},{20,24},{24,28},{28,32}... | collective-permute-start | bytes 98312 | tf_op jit(solution)/shard_map/ppermute | solution.py:432
  118.1 8.0 %collective-permute-start.6 = (f32[8,8,128]{2,1,0:T(8,128)S(1)}, f32[8,8,128]{2,1,0:T(8,128)S(1)}, u32[]{:S(2)}, u32[]{:S(2)}) collective-permute-start(f32[8,8,128]{2,1,0:T(8,128)S(1)} %get-tuple-element.30.p2), channel_id=1, source_target_pairs={{504,0},{508,4},{0,8},{4,12},{8,16},{12,20},{16,24},{20,28},{24,32... | collective-permute-start | bytes 98312 | tf_op jit(solution)/shard_map/ppermute | solution.py:432

commit v2 on v1

v2 whole, which is shorter than its diff:
```python
import jax
import jax.numpy as jnp
from jax import lax
from jax.experimental import pallas as pl
from jax.experimental.pallas import tpu as pltpu
from jax.sharding import PartitionSpec as P

F32 = jnp.float32
BF16 = jnp.bfloat16
I32 = jnp.int32

CX, CY, NZ = 16, 8, 128
PART = 2048
N_BOX = 128
CAP = 32
SLOTS = N_BOX * CAP
XE = CX + 2
OMEGA = 0.8

T0, T1, T2 = 30, 40, 20

CHUNKS = 4

LIMIT = 48 * 1024 * 1024

NT = (((1,), (1,)), ((), ()))


def tap_weights(frac):
    return (
        0.5 * (0.5 - frac) * (0.5 - frac),
        0.75 - frac * frac,
        0.5 * (0.5 + frac) * (0.5 + frac),
    )


def spread(index, at, taps):
    return jnp.where(
        index == at,
        taps[0],
        jnp.where(index == at + 1, taps[1], jnp.where(index == at + 2, taps[2], 0.0)),
    )


def route_kernel(vol_in, drag_in, mom_in, off_in, cell_in, dest_in, out, vol, drag, mom, off, cell, dest, picked, ordered, sems):
    pairs = ((dest_in, dest), (vol_in, vol), (drag_in, drag), (mom_in, mom), (off_in, off), (cell_in, cell))
    copies = [pltpu.make_async_copy(a, b, sems.at[k]) for k, (a, b) in enumerate(pairs)]
    for copy in copies:
        copy.start()
    for copy in copies:
        copy.wait()
    target = dest[...]
    hot = lax.broadcasted_iota(I32, (N_BOX, PART), 0) == target
    hot_f = jnp.where(hot, 1.0, 0.0)
    hot_b = hot_f.astype(BF16)
    width = 256
    above = lax.broadcasted_iota(I32, (width, width), 0) < lax.broadcasted_iota(I32, (width, width), 1)
    before = jnp.where(above, 1.0, 0.0).astype(BF16)
    carry = jnp.zeros((N_BOX, 1), F32)
    places = []
    for k in range(PART // width):
        cut = slice(k * width, (k + 1) * width)
        rank = jnp.dot(hot_b[:, cut], before, preferred_element_type=F32) + carry
        places.append(jnp.sum(rank * hot_f[:, cut], axis=0, keepdims=True))
        carry = carry + jnp.sum(hot_f[:, cut], axis=1, keepdims=True)
    place = jnp.concatenate(places, axis=1).astype(I32)
    at_place = lax.broadcasted_iota(I32, (CAP, PART), 0) == place
    fields = [vol[...], drag[...], mom[0:1, :], mom[1:2, :]]
    fields += [off[0:1, :], off[1:2, :], off[2:3, :], cell[...].astype(F32)]
    for f, left in enumerate(fields):
        for part in range(3):
            rounded = left.astype(BF16).astype(F32)
            row = (part * 8 + f) * CAP
            picked[row : row + CAP, :] = jnp.where(at_place, rounded, 0.0).astype(BF16)
            left = left - rounded
    sums = lax.dot_general(picked[...], hot_b, NT, preferred_element_type=F32)
    half = 8 * CAP
    sums = sums[:half] + sums[half : 2 * half] + sums[2 * half :]
    ordered[...] = sums.T
    for r in range(N_BOX):
        out[r] = ordered[r : r + 1, :]


def deposit_kernel(recv, rhs, wall, prev, pay, craw, par, cells, xs, acc, *mats):
    amats, vmats = mats[:CHUNKS], mats[CHUNKS:]
    fields = recv[...].T
    for c in range(4):
        par[c] = fields[c * CAP : (c + 1) * CAP]
    cell = fields[7 * CAP :].astype(I32)
    x_cell = cell // (NZ * CY)
    cells[0] = x_cell
    cells[1] = (cell // NZ) % CY
    cells[2] = cell % NZ
    for d in range(3):
        for k, tap in enumerate(tap_weights(fields[(4 + d) * CAP : (5 + d) * CAP])):
            par[4 + 3 * d + k] = tap
    for x in range(XE):
        xs[x] = spread(x, x_cell, (par[4], par[5], par[6]))
    sub24 = lax.broadcasted_iota(I32, (24, NZ), 0)
    sub8 = lax.broadcasted_iota(I32, (8, NZ), 0)
    sub128 = lax.broadcasted_iota(I32, (NZ, NZ), 0)

    def one(w, amat, vmat, at):
        def row(k):
            return par[k, w : w + 1, :]

        lanes = slice(at, at + NZ)
        vals = [row(c) for c in range(4)]
        wx = [row(4 + k) for k in range(3)]
        wy = [row(7 + k) for k in range(3)]
        wz = [row(10 + k) for k in range(3)]
        xc, yc, zc = [cells[d, w : w + 1, :] for d in range(3)]
        y_tile = spread(sub8, yc - 1, wy)
        low = jnp.where(yc == 0, wy[0], 0.0)
        high = jnp.where(yc == CY - 1, wy[2], 0.0)
        x_tile = spread(sub24, xc, wx)
        edge = jnp.concatenate([x_tile * low, x_tile * high], axis=0)
        for c in range(4):
            amat[576 + 48 * c : 576 + 48 * (c + 1), lanes] = (vals[c] * edge).astype(BF16)
        for pair in range(XE // 2):
            plane = jnp.concatenate([xs[2 * pair + k, w : w + 1, :] * y_tile for k in range(2)], axis=0)
            for c in range(4):
                r = 144 * c + 16 * pair
                amat[r : r + 16, lanes] = (vals[c] * plane).astype(BF16)
        vmat[:, lanes] = spread(sub128, zc - 1, wz).astype(BF16)

    each = CAP // CHUNKS
    for n in range(CHUNKS):
        for k in range(each):
            one(n * each + k, amats[n], vmats[n], k * NZ)
        part = lax.dot_general(amats[n][...], vmats[n][...], NT, preferred_element_type=F32)
        acc[...] = part if n == 0 else acc[...] + part
    for x in range(XE):
        c = [acc[144 * k + 8 * x : 144 * k + 8 * x + 8, :] for k in range(4)]
        for k in range(4):
            craw[k, x] = c[k]
        if x < 9:
            right, opened = prev[x], prev[9 + x]
        else:
            right, opened = rhs[x - 9], wall[x - 9].astype(F32)
        whole = right - c[0] * right if x < CX else -(c[0] * right)
        pay[x] = opened * (whole + c[2] + c[3])
        pay[XE + x] = c[1]
        pay[2 * XE + x] = acc[pl.ds(576 + x, 8, stride=24), :]
        extra = jnp.concatenate([right[0:1], right[7:8], opened[0:1], opened[4:5]], axis=0)
        pay[3 * XE + x // 2, (x % 2) * 4 : (x % 2) * 4 + 4, :] = extra


def slab_kernel(slab, got, craw, send, keep, ssum, dsum, osum):
    s_me = slab[0]
    sub = lax.broadcasted_iota(I32, (8, NZ), 0)
    first, last = sub == 0, sub == 7

    def edges(tile, to_first, to_last):
        return tile + jnp.where(first, to_first, 0.0) + jnp.where(last, to_last, 0.0)

    for x in range(XE):
        g_row = (x % 2) * 4
        halos = [got[s, 2 * XE + x] for s in range(4)]
        for s in range(4):
            below, above = halos[(s + 3) % 4], halos[(s + 1) % 4]
            extra = got[s, 3 * XE + x // 2]
            rhs_f, rhs_l = extra[g_row : g_row + 1], extra[g_row + 1 : g_row + 2]
            o_f, o_l = extra[g_row + 2 : g_row + 3], extra[g_row + 3 : g_row + 4]
            from_below = o_f * (below[5:6] + below[7:8] - below[1:2] * rhs_f)
            from_above = o_l * (above[4:5] + above[6:7] - above[0:1] * rhs_l)
            at = x * 32 + s * 8
            ssum[at : at + 8, :] = edges(got[s, x], from_below, from_above)
            dsum[at : at + 8, :] = edges(got[s, XE + x], below[3:4], above[2:3])
            osum[x, 2 * s : 2 * s + 2, :] = extra[g_row + 2 : g_row + 4]
        below = got[(s_me + 3) % 4, 2 * XE + x]
        above = got[(s_me + 1) % 4, 2 * XE + x]
        for c in range(4):
            tile = edges(craw[c, x], below[2 * c + 1 : 2 * c + 2], above[2 * c : 2 * c + 1])
            if x < 9:
                send[128 + 9 * c + x] = tile
            else:
                keep[128 + 9 * c + x - 9] = tile
        for q in range(4):
            s_tile = ssum[pl.ds(x * 32 + q, 8, stride=4), :]
            d_tile = dsum[pl.ds(x * 32 + q, 8, stride=4), :]
            if x < CX:
                send[4 * x + q] = s_tile
                send[64 + 4 * x + q] = d_tile
            if x >= 2:
                keep[4 * (x - 2) + q] = s_tile
                keep[64 + 4 * (x - 2) + q] = d_tile
    for k, x in enumerate((1, 5, 9, 13)):
        send[164 + k] = osum[x]
    for k, x in enumerate((2, 5, 9, 13)):
        keep[164 + k] = osum[x]


def lane_index():
    return lax.broadcasted_iota(I32, (8, NZ), 1)


def take(tile, index):
    return jnp.take_along_axis(tile, index, axis=1)


def pair_lanes(tile):
    return tile + pltpu.roll(tile, NZ - 1, 1)


def fine_sums(ref, t):
    lane = lane_index()
    cur = [ref[t, q] for q in range(4)]
    sums = []
    for q in range(4):
        after = cur[q + 1] if q < 3 else pltpu.roll(cur[0], 7, 0)
        before = cur[q - 1] if q else pltpu.roll(cur[3], 1, 0)
        left = jnp.where(lane == 0, 0.0, pltpu.roll(cur[q], 1, 1))
        right = jnp.where(lane == NZ - 1, 0.0, pltpu.roll(cur[q], NZ - 1, 1))
        sums.append((ref[t - 1, q] + ref[t + 1, q]) + (after + before) + (left + right))
    return cur, sums


def fine_sweep(src, dst, coef, base, low, high):
    for t in range(low, high):
        cur, sums = fine_sums(src, t)
        for q in range(4):
            dst[t, q] = (1.0 - OMEGA) * cur[q] + base[t, q] + coef[t, q] * sums[q]


def fine_residue(src, coef, base, weight, k):
    total = [0.0, 0.0]
    for dx in range(2):
        t = 7 + 2 * k + dx
        cur, sums = fine_sums(src, t)
        for q in range(4):
            tile = weight[2 * k + dx, q] * (base[t, q] + coef[t, q] * sums[q] - OMEGA * cur[q])
            total[q // 2] = total[q // 2] + tile
    return 0.125 * pack(total)


def pack(total):
    lane = lane_index()
    even = (2 * lane) % NZ
    return jnp.where(lane < 64, take(pair_lanes(total[0]), even), take(pair_lanes(total[1]), even))


def fine_correct(v_in, v_out, w, coef, low, high):
    lane = lane_index()
    for a in range(low, high):
        for half in range(2):
            step = take(w[a], lane // 2 + 64 * half)
            for dx in range(2):
                t = 2 * a - 25 + dx
                for q in (2 * half, 2 * half + 1):
                    v_out[t, q] = v_in[t, q] + jnp.where(coef[t, q] > 0.0, step, 0.0)


def mid_sums(ref, a):
    lane = lane_index()
    cur = ref[a]
    turned = pltpu.roll(cur, 64, 1)
    beside = turned + jnp.where(lane < 64, pltpu.roll(turned, 1, 0), pltpu.roll(turned, 7, 0))
    left = jnp.where(lane % 64 == 0, 0.0, pltpu.roll(cur, 1, 1))
    right = jnp.where(lane % 64 == 63, 0.0, pltpu.roll(cur, NZ - 1, 1))
    return cur, (ref[a - 1] + ref[a + 1]) + beside + (left + right)


def mid_sweep(src, dst, coef, base, low, high):
    for a in range(low, high):
        cur, total = mid_sums(src, a)
        dst[a] = (1.0 - OMEGA) * cur + base[a] + coef[a] * total


def low_sweep(src, dst, coef, base, low, high):
    for m in range(low, high):
        cur = src[m]
        total = (src[m - 1] + src[m + 1]) + (pltpu.roll(cur, 1, 0) + pltpu.roll(cur, 7, 0))
        total = total + (pltpu.roll(cur, 1, 1) + pltpu.roll(cur, NZ - 1, 1))
        dst[m] = (1.0 - OMEGA) * cur + base[m] + coef[m] * total


def levels_solve(c1, g1, c2, cb1, w_a, w_b, cb2, u_a, u_b):
    lane = lane_index()
    even = (2 * lane) % NZ
    mid_sweep(cb1, w_a, c1, cb1, 3, 37)
    for m in range(2, 18):
        total = 0.0
        for a in (2 * m, 2 * m + 1):
            cur, beside = mid_sums(w_a, a)
            total = total + g1[a] * (cb1[a] + c1[a] * beside - OMEGA * cur)
        total = total + pltpu.roll(total, 64, 1)
        cb2[m] = 2.0 * c2[m] * take(pair_lanes(total), even)
    low_sweep(cb2, u_a, c2, cb2, 3, 17)
    low_sweep(u_a, u_b, c2, cb2, 4, 16)
    low_sweep(u_b, u_a, c2, cb2, 5, 15)
    for m in range(5, 15):
        step = take(u_a[m], (lane % 64) // 2)
        for a in (2 * m, 2 * m + 1):
            w_a[a] = w_a[a] + jnp.where(c1[a] > 0.0, step, 0.0)
    mid_sweep(w_a, w_b, c1, cb1, 12, 28)
    mid_sweep(w_b, w_a, c1, cb1, 13, 27)


def coupled_kernel(keep, got, coupled):
    for c in range(4):
        for x in range(CX):
            if x < 7:
                tile = keep[128 + 9 * c + x]
            elif x < 9:
                tile = keep[128 + 9 * c + x] + got[128 + 9 * c + x - 7]
            else:
                tile = got[128 + 9 * c + x - 7]
            coupled[c, x] = tile


def start_kernel(keep, got, cc, cb, gg, v2, send, dk):
    for t in range(T0):
        block = (t + 1) // 4
        opened = keep[164 + block] if block < 4 else got[160 + block]
        for q in range(4):
            at = 4 * (t - 14) + q
            if t < 14:
                s_tile, d_tile = keep[4 * t + q], keep[64 + 4 * t + q]
            elif t < 16:
                s_tile, d_tile = keep[4 * t + q] + got[at], keep[64 + 4 * t + q] + got[64 + at]
            else:
                s_tile, d_tile = got[at], got[64 + at]
            diag = 6.0 + d_tile
            coef = OMEGA * opened / diag
            cc[t, q] = coef
            cb[t, q] = coef * s_tile
            if 7 <= t < 23:
                dk[t - 7, q] = d_tile
                gg[t - 7, q] = (1.0 / OMEGA) * diag
    fine_sweep(cb, v2, cc, cb, 1, 29)
    lane = lane_index()
    even = (2 * lane) % NZ
    for k in range(8):
        block = 2 + k // 2
        opened = take(keep[164 + block] if block < 4 else got[160 + block], even)
        d_sum = [0.0, 0.0]
        for dx in range(2):
            for q in range(4):
                d_sum[q // 2] = d_sum[q // 2] + dk[2 * k + dx, q]
        damp = 0.125 * pack(d_sum)
        diag = 1.5 + damp
        coef = OMEGA * opened / diag
        send[k] = coef * fine_residue(v2, cc, cb, gg, k)
        send[8 + k] = 0.25 * coef
        send[16 + k] = (1.0 / OMEGA) * diag
        if k % 2 == 0:
            above = damp
        else:
            total = above + damp
            total = total + pltpu.roll(total, 64, 1)
            low = 0.375 + 0.125 * take(pair_lanes(total), even)
            send[24 + k // 2] = jnp.where(lane < 32, 0.0625 * (OMEGA * take(opened, even) / low), 0.0)


def window(core, far_low, second, own, first, far_high):
    even = core == 0

    def part(n, k):
        if n == 1:
            return jnp.where(even, second[k], first[k])
        if n == 3:
            return jnp.where(even, first[k], second[k])
        return (far_low, None, own, None, far_high)[n][k]

    return part


def middle_kernel(place, far_low, second, own, first, far_high, cc, cb, gg, v2, v_out, c1, g1, c2, send,
                  cb1, w_a, w_b, cb2, u_a, u_b, v_a, v_b):
    part = window(place[1], far_low, second, own, first, far_high)
    for n in range(5):
        for k in range(8):
            cb1[8 * n + k] = part(n, k)
            c1[8 * n + k] = part(n, 8 + k)
            g1[8 * n + k] = part(n, 16 + k)
        for k in range(4):
            c2[4 * n + k] = part(n, 24 + k)
    levels_solve(c1, g1, c2, cb1, w_a, w_b, cb2, u_a, u_b)
    fine_correct(v2, v_a, w_a, cc, 13, 27)
    fine_sweep(v_a, v_b, cc, cb, 2, 28)
    fine_sweep(v_b, v_a, cc, cb, 3, 27)
    fine_sweep(v_a, v_b, cc, cb, 4, 26)
    fine_sweep(v_b, v_out, cc, cb, 5, 25)
    for k in range(8):
        send[k] = 4.0 * c1[16 + k] * fine_residue(v_out, cc, cb, gg, k)


def last_kernel(place, far_low, second, own, first, far_high, cc, cb, v2, c1, g1, c2, out,
                cb1, w_a, w_b, cb2, u_a, u_b, v_a, v_b, flat):
    part = window(place[1], far_low, second, own, first, far_high)
    for n in range(5):
        for k in range(8):
            cb1[8 * n + k] = part(n, k)
    levels_solve(c1, g1, c2, cb1, w_a, w_b, cb2, u_a, u_b)
    fine_correct(v2, v_a, w_a, cc, 15, 25)
    fine_sweep(v_a, v_b, cc, cb, 6, 24)
    fine_sweep(v_b, v_a, cc, cb, 7, 23)
    for x in range(CX):
        for q in range(4):
            flat[pl.ds(x * 32 + q, 8, stride=4), :] = v_a[7 + x, q]
    for x in range(CX):
        out[x] = flat[pl.ds(pl.multiple_of(x * 32 + 8 * place[0], 8), 8), :]


def call(kernel, outs, scratch, operands, smem_first=False, in_hbm=False, cost=1000000, limit=LIMIT):
    kind = pltpu.HBM if in_hbm else pltpu.VMEM
    specs = [pl.BlockSpec(memory_space=kind) for _ in operands]
    if smem_first:
        specs[0] = pl.BlockSpec(memory_space=pltpu.SMEM)
    shapes = [jax.ShapeDtypeStruct(shape, F32) for shape in outs]
    return pl.pallas_call(
        kernel,
        out_shape=shapes,
        in_specs=specs,
        out_specs=[pl.BlockSpec(memory_space=pltpu.VMEM) for _ in outs],
        scratch_shapes=[pltpu.VMEM(*piece) if isinstance(piece, tuple) else piece for piece in scratch],
        compiler_params=pltpu.CompilerParams(vmem_limit_bytes=limit),
        cost_estimate=pl.CostEstimate(flops=cost, bytes_accessed=cost, transcendentals=0),
    )(*operands)


def fetch(block, distance):
    count = lax.axis_size("box")
    return lax.ppermute(block, "box", [((i + distance) % count, i) for i in range(count)])


def swap(block):
    return lax.ppermute(block, "box", [(i ^ 1, i) for i in range(lax.axis_size("box"))])


def around(block, core):
    far_low, far_high = fetch(block, -2), fetch(block, 2)
    first = swap(block)
    second = swap(jnp.where(core == 0, far_high, far_low))
    return [far_low, second, block, first, far_high]


def shards(volume, drag, momentum, offsets, cell_index, destinations, rhs, wall):
    core = lax.axis_index("box").astype(I32) % 2
    place = jnp.stack([lax.axis_index("slab").astype(I32), core])
    prev = fetch(jnp.concatenate([rhs[7:], wall[7:].astype(F32)], axis=0), -1)
    one = (1, PART)
    (outgoing,) = call(
        route_kernel,
        [(N_BOX, 1, 8 * CAP)],
        [(one, F32), (one, F32), ((2, PART), F32), ((3, PART), F32), (one, I32), (one, I32),
         ((24 * CAP, PART), BF16), ((N_BOX, 8 * CAP), F32), pltpu.SemaphoreType.DMA((6,))],
        [volume.reshape(one), drag.reshape(one), momentum, offsets, cell_index.reshape(one), destinations.reshape(one)],
        in_hbm=True,
        limit=62 * 1024 * 1024,
    )
    incoming = lax.all_to_all(outgoing, "box", split_axis=0, concat_axis=0, tiled=True)
    pay, craw = call(
        deposit_kernel,
        [(3 * XE + XE // 2, 8, NZ), (4, XE, 8, NZ)],
        [((13, CAP, NZ), F32), ((3, CAP, NZ), I32), ((XE, CAP, NZ), F32), ((768, NZ), F32)]
        + [((768, SLOTS // CHUNKS), BF16)] * CHUNKS + [((NZ, SLOTS // CHUNKS), BF16)] * CHUNKS,
        [incoming.reshape(N_BOX, 8 * CAP), rhs, wall, prev],
    )
    slabs = lax.all_gather(pay, "slab")
    send, keep = call(
        slab_kernel,
        [(168, 8, NZ), (168, 8, NZ)],
        [((XE * 32, NZ), F32), ((XE * 32, NZ), F32), ((XE, 8, NZ), F32)],
        [place, slabs, craw],
        smem_first=True,
    )
    got = fetch(send, 1)
    fine, mid, low = (T0, 4, 8, NZ), (T1, 8, NZ), (T2, 8, NZ)
    cc, cb, gg, v2, first = call(
        start_kernel, [fine, fine, (CX, 4, 8, NZ), fine, (28, 8, NZ)], [((CX, 4, 8, NZ), F32)], [keep, got]
    )
    (coupled,) = call(coupled_kernel, [(4, CX, 8, NZ)], [], [keep, got])
    scratch = [(mid, F32), (mid, F32), (mid, F32), (low, F32), (low, F32), (low, F32), (fine, F32), (fine, F32)]
    v3, c1, g1, c2, second = call(
        middle_kernel,
        [fine, mid, mid, low, (8, 8, NZ)],
        scratch,
        [place] + around(first, core) + [cc, cb, gg, v2],
        smem_first=True,
    )
    (pressure,) = call(
        last_kernel,
        [(CX, 8, NZ)],
        scratch + [((CX * 32, NZ), F32)],
        [place] + around(second, core) + [cc, cb, v3, c1, g1, c2],
        smem_first=True,
    )
    return coupled, pressure


def solution(mesh):
    in_specs = (
        P(("box", "slab")),
        P(("box", "slab")),
        P(None, ("box", "slab")),
        P(None, ("box", "slab")),
        P(("box", "slab")),
        P(("box", "slab"), None),
        P("box", "slab", None),
        P("box", "slab", None),
    )
    out_specs = (P(None, "box", "slab", None), P("box", "slab", None))
    return jax.shard_map(shards, mesh=mesh, in_specs=in_specs, out_specs=out_specs, check_vma=False)
```

time: 132 us -> 112 us (0.85)
  Pallas kernels: 26.8 us -> 16.1 us
  local copies, waits for them, and re-layouts: 6.66 us -> 1.61 us
  waiting for transfers between devices: 32 us -> 29 us
    ppermute x10 -> x6, starting transfers between devices: 31.3 us -> 20.2 us  [fetch(): lax.ppermute(block, 'box', [((i + distance) % count, i) for i in range(co...]
    pallas_call x6 -> x7, Pallas kernels: 26.8 us -> 16.1 us  [call(): pl.pallas_call(kernel, out_shape=shapes, in_specs=specs, out_specs=[pl.Bl...]
    ppermute x0 -> x4, starting transfers between devices: none -> 10.1 us  [swap(): lax.ppermute(block, 'box', [(i ^ 1, i) for i in range(lax.axis_size('box'...]
    ppermute x10 -> x6, waiting for transfers between devices: 21.1 us -> 16.8 us  [fetch(): lax.ppermute(block, 'box', [((i + distance) % count, i) for i in range(co...]
    unnamed x17 -> x5, local copies, waits for them, and re-layouts: 5.1 us -> 0.85 us
    ppermute x0 -> x4, waiting for transfers between devices: none -> 1.4 us  [swap(): lax.ppermute(block, 'box', [(i ^ 1, i) for i in range(lax.axis_size('box'...]
  transfers between devices with their start and end apart: 11 -> 11, of which waited for: 4 -> 6; matrix products, arithmetic and copies ran while one was open for 0% -> 0% of each run, Pallas kernels for 0% -> 1%
where the time goes in v2:
time: 112 us
  starting transfers between devices  50.7 us (45%)
  waiting for transfers between devices  29 us (26%)
  Pallas kernels  16.1 us (14%)
  blocking collectives  13.4 us (12%)
  local copies, waits for them, and re-layouts  1.61 us (1%)
    all_to_all x1, starting transfers between devices, shards(): lax.all_to_all(outgoing, 'box', split_axis=0, concat_axis=0, tiled=True)  20.4 us
    ppermute x6, starting transfers between devices, fetch(): lax.ppermute(block, 'box', [((i + distance) % count, i) for i in range(co...  20.2 us
    ppermute x6, waiting for transfers between devices, fetch(): lax.ppermute(block, 'box', [((i + distance) % count, i) for i in range(co...  16.8 us
    pallas_call x7, Pallas kernels, call(): pl.pallas_call(kernel, out_shape=shapes, in_specs=specs, out_specs=[pl.Bl...  16.1 us
    all_gather x1, blocking collectives, shards(): slabs = lax.all_gather(pay, 'slab')  13.4 us
    all_to_all x1, waiting for transfers between devices, shards(): lax.all_to_all(outgoing, 'box', split_axis=0, concat_axis=0, tiled=True)  10.8 us
    ppermute x4, starting transfers between devices, swap(): lax.ppermute(block, 'box', [(i ^ 1, i) for i in range(lax.axis_size('box'...  10.1 us
  transfers between devices with their start and end apart: 11, of which 6 were waited for; matrix products, arithmetic and copies ran while one was open for 0% of the time, Pallas kernels for 1%

profile of v2, /device:TPU:1, one launch (start us, length us, event | category | flops | bytes accessed | tf_op | source)
XLA Modules:
  0.0 111.7 jit_solution(3618337821128732322)
XLA Ops:
  0.6 3.0 %shard_map.95 = f32[128,1,256]{2,1,0:T(1,128)} custom-call(f32[1,2048]{1,0:T(1,128)} %bitcast.12, f32[1,2048]{1,0:T(1,128)} %bitcast.13, f32[2,2048]{1,0:T(2,128)} %mom_in.1, f32[3,2048]{1,0:T(4,128)} %off_in.1, s32[1,2048]{1,0:T(1,128)} %bitcast.14, s32[1,2048]{1,0:T(1,128)} %bitcast.15), custom_call_target="tpu_custom_call" | custom-call | flops 1000000 | bytes 1000000 | tf_op jit(solution)/shard_map/pallas_call | solution.py:412
  3.7 20.4 %all-to-all-start = ((f32[128,1,256]{2,1,0:T(1,128)}), f32[128,1,256]{2,1,0:T(1,128)S(1)}, u32[]{:S(2)}, u32[]{:S(2)}) async-start(f32[128,1,256]{2,1,0:T(1,128)} %shard_map.95), calls=%async_computation | async-start | bytes 262144 | tf_op jit(solution)/shard_map/all_to_all | solution.py:453
  24.1 0.0 copy-start.1
  24.1 0.8 copy-done.1
  24.9 0.0 slice-start
  24.9 0.8 slice-done
  25.7 3.5 %collective-permute-start = (f32[18,8,128]{2,1,0:T(8,128)S(1)}, f32[18,8,128]{2,1,0:T(8,128)S(1)}, u32[]{:S(2)}, u32[]{:S(2)}) collective-permute-start(f32[18,8,128]{2,1,0:T(8,128)S(1)} %pad_maximum_fusion), channel_id=1, source_target_pairs={{508,0},{0,4},{4,8},{8,12},{12,16},{16,20},{20,24},{24,28},{28,32}... | collective-permute-start | bytes 221192 | tf_op jit(solution)/shard_map/ppermute | solution.py:425
  29.3 0.1 pad_add_fusion.slab.place
  29.3 0.0 copy-start
  29.3 10.8 %all-to-all-done = f32[128,1,256]{2,1,0:T(1,128)S(1)} async-done(((f32[128,1,256]{2,1,0:T(1,128)}), f32[128,1,256]{2,1,0:T(1,128)S(1)}, u32[]{:S(2)}, u32[]{:S(2)}) %all-to-all-start) | async-done | bytes 131104 | tf_op jit(solution)/shard_map/all_to_all | solution.py:453
  40.2 0.0 collective-permute-done.prev
  40.2 0.0 copy-done
  40.2 3.3 %shard_map.96 = (f32[63,8,128]{2,1,0:T(8,128)S(1)}, f32[4,18,8,128]{3,2,1,0:T(8,128)S(1)}) custom-call(f32[128,256]{1,0:T(8,128)S(1)} %bitcast.11, f32[16,8,128]{2,1,0:T(8,128)S(1)} %copy-done, s32[16,8,128]{2,1,0:T(8,128)S(1)} %copy-done.1, f32[18,8,128]{2,1,0:T(8,128)S(1)} %collective-permute-done.prev), custom_call_target="tpu_custom_call" | custom-call | flops 1000000 | bytes 1000000 | tf_op jit(solution)/shard_map/pallas_call | solution.py:412
  43.4 13.4 %all-gather = f32[252,8,128]{2,1,0:T(8,128)S(1)} all-gather(f32[63,8,128]{2,1,0:T(8,128)S(1)} %get-tuple-element.16), channel_id=2, replica_groups=mesh['box'=128,'slab'=4] {'slab'}, dimensions={0}, use_global_device_ids=true | all-gather | bytes 1290240 | tf_op jit(solution)/shard_map/all_gather | solution.py:461
  56.8 0.9 shard_map.97
  57.7 4.1 %collective-permute-start.1 = (f32[168,8,128]{2,1,0:T(8,128)S(1)}, f32[168,8,128]{2,1,0:T(8,128)S(1)}, u32[]{:S(2)}, u32[]{:S(2)}) collective-permute-start(f32[168,8,128]{2,1,0:T(8,128)S(1)} %get-tuple-element.19), channel_id=1, source_target_pairs={{4,0},{8,4},{12,8},{16,12},{20,16},{24,20},{28,24},{32,28},{36,32}... | collective-permute-start | bytes 2064392 | tf_op jit(solution)/shard_map/ppermute | solution.py:425
  61.8 9.9 %collective-permute-done.1.got = f32[168,8,128]{2,1,0:T(8,128)S(1)} collective-permute-done((f32[168,8,128]{2,1,0:T(8,128)S(1)}, f32[168,8,128]{2,1,0:T(8,128)S(1)}, u32[]{:S(2)}, u32[]{:S(2)}) %collective-permute-start.1) | collective-permute-done | bytes 688160 | tf_op jit(solution)/shard_map/ppermute | solution.py:425
  71.7 1.5 %shard_map.99 = (f32[30,4,8,128]{3,2,1,0:T(8,128)S(1)}, f32[30,4,8,128]{3,2,1,0:T(8,128)S(1)}, f32[16,4,8,128]{3,2,1,0:T(8,128)S(1)}, f32[30,4,8,128]{3,2,1,0:T(8,128)S(1)}, f32[28,8,128]{2,1,0:T(8,128)S(1)}) custom-call(f32[168,8,128]{2,1,0:T(8,128)S(1)} %get-tuple-element.18.keep, f32[168,8,128]{2,1,0:T(8,128)S(1)} %collective-permute-done.1.got), custom_call_target="tpu_custom_call" | custom-call | flops 1000000 | bytes 1000000 | tf_op jit(solution)/shard_map/pallas_call | solution.py:412
  73.2 5.3 %collective-permute-start.3 = (f32[28,8,128]{2,1,0:T(8,128)S(1)}, f32[28,8,128]{2,1,0:T(8,128)S(1)}, u32[]{:S(2)}, u32[]{:S(2)}) collective-permute-start(f32[28,8,128]{2,1,0:T(8,128)S(1)} %get-tuple-element.20.own), channel_id=1, source_target_pairs={{8,0},{12,4},{16,8},{20,12},{24,16},{28,20},{32,24},{36,28},{40,32... | collective-permute-start | bytes 344072 | tf_op jit(solution)/shard_map/ppermute | solution.py:425
  78.5 1.9 %collective-permute-start.2 = (f32[28,8,128]{2,1,0:T(8,128)S(1)}, f32[28,8,128]{2,1,0:T(8,128)S(1)}, u32[]{:S(2)}, u32[]{:S(2)}) collective-permute-start(f32[28,8,128]{2,1,0:T(8,128)S(1)} %get-tuple-element.20.own), channel_id=1, source_target_pairs={{504,0},{508,4},{0,8},{4,12},{8,16},{12,20},{16,24},{20,28},{24,32... | collective-permute-start | bytes 344072 | tf_op jit(solution)/shard_map/ppermute | solution.py:425
  80.5 1.9 %collective-permute-start.5 = (f32[28,8,128]{2,1,0:T(8,128)S(1)}, f32[28,8,128]{2,1,0:T(8,128)S(1)}, u32[]{:S(2)}, u32[]{:S(2)}) collective-permute-start(f32[28,8,128]{2,1,0:T(8,128)S(1)} %get-tuple-element.20.own), channel_id=1, source_target_pairs={{4,0},{0,4},{12,8},{8,12},{20,16},{16,20},{28,24},{24,28},{36,32},... | collective-permute-start | bytes 344072 | tf_op jit(solution)/shard_map/ppermute | solution.py:429
  82.4 0.0 collective-permute-done.3.far_high
  82.4 5.0 %collective-permute-done.2.far_low = f32[28,8,128]{2,1,0:T(8,128)S(1)} collective-permute-done((f32[28,8,128]{2,1,0:T(8,128)S(1)}, f32[28,8,128]{2,1,0:T(8,128)S(1)}, u32[]{:S(2)}, u32[]{:S(2)}) %collective-permute-start.2) | collective-permute-done | bytes 114720 | tf_op jit(solution)/shard_map/ppermute | solution.py:425
  87.4 1.9 %collective-permute-start.4 = (f32[28,8,128]{2,1,0:T(8,128)S(1)}, f32[28,8,128]{2,1,0:T(8,128)S(1)}, u32[]{:S(2)}, u32[]{:S(2)}) collective-permute-start(f32[28,8,128]{2,1,0:T(8,128)S(1)} %broadcast_select_fusion), channel_id=1, source_target_pairs={{4,0},{0,4},{12,8},{8,12},{20,16},{16,20},{28,24},{24,28},{36,32},... | collective-permute-start | bytes 344072 | tf_op jit(solution)/shard_map/ppermute | solution.py:429
  89.3 0.0 collective-permute-done.5.first
  89.3 1.3 %collective-permute-done.4.second = f32[28,8,128]{2,1,0:T(8,128)S(1)} collective-permute-done((f32[28,8,128]{2,1,0:T(8,128)S(1)}, f32[28,8,128]{2,1,0:T(8,128)S(1)}, u32[]{:S(2)}, u32[]{:S(2)}) %collective-permute-start.4) | collective-permute-done | bytes 114720 | tf_op jit(solution)/shard_map/ppermute | solution.py:429
  90.6 3.8 %shard_map.100 = (f32[30,4,8,128]{3,2,1,0:T(8,128)S(1)}, f32[40,8,128]{2,1,0:T(8,128)S(1)}, f32[40,8,128]{2,1,0:T(8,128)S(1)}, f32[20,8,128]{2,1,0:T(8,128)S(1)}, f32[8,8,128]{2,1,0:T(8,128)S(1)}) custom-call(s32[2]{0:T(128)S(1)} %pad_add_fusion.slab.place, f32[28,8,128]{2,1,0:T(8,128)S(1)} %collective-permute-done.2.far_low, ...), custom_call_target="tpu_custom_call" | custom-call | flops 1000000 | bytes 1000000 | tf_op jit(solution)/shard_map/pallas_call | solution.py:412
  94.4 1.9 %collective-permute-start.7 = (f32[8,8,128]{2,1,0:T(8,128)S(1)}, f32[8,8,128]{2,1,0:T(8,128)S(1)}, u32[]{:S(2)}, u32[]{:S(2)}) collective-permute-start(f32[8,8,128]{2,1,0:T(8,128)S(1)} %get-tuple-element.25.own), channel_id=1, source_target_pairs={{8,0},{12,4},{16,8},{20,12},{24,16},{28,20},{32,24},{36,28},{40,32... | collective-permute-start | bytes 98312 | tf_op jit(solution)/shard_map/ppermute | solution.py:425
  96.4 3.4 %collective-permute-start.6 = (f32[8,8,128]{2,1,0:T(8,128)S(1)}, f32[8,8,128]{2,1,0:T(8,128)S(1)}, u32[]{:S(2)}, u32[]{:S(2)}) collective-permute-start(f32[8,8,128]{2,1,0:T(8,128)S(1)} %get-tuple-element.25.own), channel_id=1, source_target_pairs={{504,0},{508,4},{0,8},{4,12},{8,16},{12,20},{16,24},{20,28},{24,32... | collective-permute-start | bytes 98312 | tf_op jit(solution)/shard_map/ppermute | solution.py:425
  99.7 2.6 %collective-permute-start.9 = (f32[8,8,128]{2,1,0:T(8,128)S(1)}, f32[8,8,128]{2,1,0:T(8,128)S(1)}, u32[]{:S(2)}, u32[]{:S(2)}) collective-permute-start(f32[8,8,128]{2,1,0:T(8,128)S(1)} %get-tuple-element.25.own), channel_id=1, source_target_pairs={{4,0},{0,4},{12,8},{8,12},{20,16},{16,20},{28,24},{24,28},{36,32},... | collective-permute-start | bytes 98312 | tf_op jit(solution)/shard_map/ppermute | solution.py:429
  102.4 0.0 collective-permute-done.7.far_high
  102.4 2.0 %collective-permute-done.6.far_low = f32[8,8,128]{2,1,0:T(8,128)S(1)} collective-permute-done((f32[8,8,128]{2,1,0:T(8,128)S(1)}, f32[8,8,128]{2,1,0:T(8,128)S(1)}, u32[]{:S(2)}, u32[]{:S(2)}) %collective-permute-start.6) | collective-permute-done | bytes 32800 | tf_op jit(solution)/shard_map/ppermute | solution.py:425
  104.4 3.6 %collective-permute-start.8 = (f32[8,8,128]{2,1,0:T(8,128)S(1)}, f32[8,8,128]{2,1,0:T(8,128)S(1)}, u32[]{:S(2)}, u32[]{:S(2)}) collective-permute-start(f32[8,8,128]{2,1,0:T(8,128)S(1)} %broadcast_select_fusion.1), channel_id=1, source_target_pairs={{4,0},{0,4},{12,8},{8,12},{20,16},{16,20},{28,24},{24,28},{36,32},... | collective-permute-start | bytes 98312 | tf_op jit(solution)/shard_map/ppermute | solution.py:429
  108.0 0.7 shard_map.98
  108.7 0.0 collective-permute-done.9.first
  108.7 0.1 collective-permute-done.8.second
  108.8 2.9 %shard_map.101 = f32[16,8,128]{2,1,0:T(8,128)} custom-call(s32[2]{0:T(128)S(1)} %pad_add_fusion.slab.place, f32[8,8,128]{2,1,0:T(8,128)S(1)} %collective-permute-done.6.far_low, f32[8,8,128]{2,1,0:T(8,128)S(1)} %collective-permute-done.8.second, f32[8,8,128]{2,1,0:T(8,128)S(1)} %get-tuple-element.25.own, f32[8,8,128]{2,1,0:T(8,128)S(1)} %collective-permute-done.9.first, ...), custom_call_target="tpu_custom_call" | custom-call | flops 1000000 | bytes 1000000 | tf_op jit(solution)/shard_map/pallas_call | solution.py:412
  (5 shorter events, 0.0 us)
Async XLA Ops:
  3.7 36.5 %all-to-all-start = ((f32[128,1,256]{2,1,0:T(1,128)}), f32[128,1,256]{2,1,0:T(1,128)S(1)}, u32[]{:S(2)}, u32[]{:S(2)}) async-start(f32[128,1,256]{2,1,0:T(1,128)} %shard_map.95), calls=%async_computation | async-start | bytes 262144 | tf_op jit(solution)/shard_map/all_to_all | solution.py:453
  24.1 0.8 copy-start.1
  24.9 0.8 slice-start
  25.7 14.5 %collective-permute-start = (f32[18,8,128]{2,1,0:T(8,128)S(1)}, f32[18,8,128]{2,1,0:T(8,128)S(1)}, u32[]{:S(2)}, u32[]{:S(2)}) collective-permute-start(f32[18,8,128]{2,1,0:T(8,128)S(1)} %pad_maximum_fusion), channel_id=1, source_target_pairs={{508,0},{0,4},{4,8},{8,12},{12,16},{16,20},{20,24},{24,28},{28,32}... | collective-permute-start | bytes 221192 | tf_op jit(solution)/shard_map/ppermute | solution.py:425
  29.3 10.8 %copy-start = (f32[16,8,128]{2,1,0:T(8,128)S(1)}, f32[16,8,128]{2,1,0:T(8,128)}, u32[]{:S(2)}) copy-start(f32[16,8,128]{2,1,0:T(8,128)} %rhs.1) | copy-start | bytes 196612
  57.7 14.0 %collective-permute-start.1 = (f32[168,8,128]{2,1,0:T(8,128)S(1)}, f32[168,8,128]{2,1,0:T(8,128)S(1)}, u32[]{:S(2)}, u32[]{:S(2)}) collective-permute-start(f32[168,8,128]{2,1,0:T(8,128)S(1)} %get-tuple-element.19), channel_id=1, source_target_pairs={{4,0},{8,4},{12,8},{16,12},{20,16},{24,20},{28,24},{32,28},{36,32}... | collective-permute-start | bytes 2064392 | tf_op jit(solution)/shard_map/ppermute | solution.py:425
  73.2 9.2 %collective-permute-start.3 = (f32[28,8,128]{2,1,0:T(8,128)S(1)}, f32[28,8,128]{2,1,0:T(8,128)S(1)}, u32[]{:S(2)}, u32[]{:S(2)}) collective-permute-start(f32[28,8,128]{2,1,0:T(8,128)S(1)} %get-tuple-element.20.own), channel_id=1, source_target_pairs={{8,0},{12,4},{16,8},{20,12},{24,16},{28,20},{32,24},{36,28},{40,32... | collective-permute-start | bytes 344072 | tf_op jit(solution)/shard_map/ppermute | solution.py:425
  78.5 8.9 %collective-permute-start.2 = (f32[28,8,128]{2,1,0:T(8,128)S(1)}, f32[28,8,128]{2,1,0:T(8,128)S(1)}, u32[]{:S(2)}, u32[]{:S(2)}) collective-permute-start(f32[28,8,128]{2,1,0:T(8,128)S(1)} %get-tuple-element.20.own), channel_id=1, source_target_pairs={{504,0},{508,4},{0,8},{4,12},{8,16},{12,20},{16,24},{20,28},{24,32... | collective-permute-start | bytes 344072 | tf_op jit(solution)/shard_map/ppermute | solution.py:425
  80.5 8.9 %collective-permute-start.5 = (f32[28,8,128]{2,1,0:T(8,128)S(1)}, f32[28,8,128]{2,1,0:T(8,128)S(1)}, u32[]{:S(2)}, u32[]{:S(2)}) collective-permute-start(f32[28,8,128]{2,1,0:T(8,128)S(1)} %get-tuple-element.20.own), channel_id=1, source_target_pairs={{4,0},{0,4},{12,8},{8,12},{20,16},{16,20},{28,24},{24,28},{36,32},... | collective-permute-start | bytes 344072 | tf_op jit(solution)/shard_map/ppermute | solution.py:429
  87.4 3.2 %collective-permute-start.4 = (f32[28,8,128]{2,1,0:T(8,128)S(1)}, f32[28,8,128]{2,1,0:T(8,128)S(1)}, u32[]{:S(2)}, u32[]{:S(2)}) collective-permute-start(f32[28,8,128]{2,1,0:T(8,128)S(1)} %broadcast_select_fusion), channel_id=1, source_target_pairs={{4,0},{0,4},{12,8},{8,12},{20,16},{16,20},{28,24},{24,28},{36,32},... | collective-permute-start | bytes 344072 | tf_op jit(solution)/shard_map/ppermute | solution.py:429
  94.4 7.9 %collective-permute-start.7 = (f32[8,8,128]{2,1,0:T(8,128)S(1)}, f32[8,8,128]{2,1,0:T(8,128)S(1)}, u32[]{:S(2)}, u32[]{:S(2)}) collective-permute-start(f32[8,8,128]{2,1,0:T(8,128)S(1)} %get-tuple-element.25.own), channel_id=1, source_target_pairs={{8,0},{12,4},{16,8},{20,12},{24,16},{28,20},{32,24},{36,28},{40,32... | collective-permute-start | bytes 98312 | tf_op jit(solution)/shard_map/ppermute | solution.py:425
  96.4 8.0 %collective-permute-start.6 = (f32[8,8,128]{2,1,0:T(8,128)S(1)}, f32[8,8,128]{2,1,0:T(8,128)S(1)}, u32[]{:S(2)}, u32[]{:S(2)}) collective-permute-start(f32[8,8,128]{2,1,0:T(8,128)S(1)} %get-tuple-element.25.own), channel_id=1, source_target_pairs={{504,0},{508,4},{0,8},{4,12},{8,16},{12,20},{16,24},{20,28},{24,32... | collective-permute-start | bytes 98312 | tf_op jit(solution)/shard_map/ppermute | solution.py:425
  99.7 9.0 %collective-permute-start.9 = (f32[8,8,128]{2,1,0:T(8,128)S(1)}, f32[8,8,128]{2,1,0:T(8,128)S(1)}, u32[]{:S(2)}, u32[]{:S(2)}) collective-permute-start(f32[8,8,128]{2,1,0:T(8,128)S(1)} %get-tuple-element.25.own), channel_id=1, source_target_pairs={{4,0},{0,4},{12,8},{8,12},{20,16},{16,20},{28,24},{24,28},{36,32},... | collective-permute-start | bytes 98312 | tf_op jit(solution)/shard_map/ppermute | solution.py:429
  104.4 4.5 %collective-permute-start.8 = (f32[8,8,128]{2,1,0:T(8,128)S(1)}, f32[8,8,128]{2,1,0:T(8,128)S(1)}, u32[]{:S(2)}, u32[]{:S(2)}) collective-permute-start(f32[8,8,128]{2,1,0:T(8,128)S(1)} %broadcast_select_fusion.1), channel_id=1, source_target_pairs={{4,0},{0,4},{12,8},{8,12},{20,16},{16,20},{28,24},{24,28},{36,32},... | collective-permute-start | bytes 98312 | tf_op jit(solution)/shard_map/ppermute | solution.py:429

commit v3 on v2

--- a/solution.py
+++ b/solution.py
@@ -19,7 +19,8 @@
 
 T0, T1, T2 = 30, 40, 20
 
-CHUNKS = 4
+OTHERS = (0, 2, 3)
+CHUNKS = 8
 
 LIMIT = 48 * 1024 * 1024
 
@@ -47,8 +48,7 @@
     copies = [pltpu.make_async_copy(a, b, sems.at[k]) for k, (a, b) in enumerate(pairs)]
     for copy in copies:
         copy.start()
-    for copy in copies:
-        copy.wait()
+    copies[0].wait()
     target = dest[...]
     hot = lax.broadcasted_iota(I32, (N_BOX, PART), 0) == target
     hot_f = jnp.where(hot, 1.0, 0.0)
@@ -65,6 +65,8 @@
         carry = carry + jnp.sum(hot_f[:, cut], axis=1, keepdims=True)
     place = jnp.concatenate(places, axis=1).astype(I32)
     at_place = lax.broadcasted_iota(I32, (CAP, PART), 0) == place
+    for copy in copies[1:]:
+        copy.wait()
     fields = [vol[...], drag[...], mom[0:1, :], mom[1:2, :]]
     fields += [off[0:1, :], off[1:2, :], off[2:3, :], cell[...].astype(F32)]
     for f, left in enumerate(fields):
@@ -132,8 +134,8 @@
         acc[...] = part if n == 0 else acc[...] + part
     for x in range(XE):
         c = [acc[144 * k + 8 * x : 144 * k + 8 * x + 8, :] for k in range(4)]
-        for k in range(4):
-            craw[k, x] = c[k]
+        for k, channel in enumerate(OTHERS):
+            craw[k, x] = c[channel]
         if x < 9:
             right, opened = prev[x], prev[9 + x]
         else:
@@ -170,12 +172,12 @@
             osum[x, 2 * s : 2 * s + 2, :] = extra[g_row + 2 : g_row + 4]
         below = got[(s_me + 3) % 4, 2 * XE + x]
         above = got[(s_me + 1) % 4, 2 * XE + x]
-        for c in range(4):
-            tile = edges(craw[c, x], below[2 * c + 1 : 2 * c + 2], above[2 * c : 2 * c + 1])
+        for k, c in enumerate(OTHERS):
+            tile = edges(craw[k, x], below[2 * c + 1 : 2 * c + 2], above[2 * c : 2 * c + 1])
             if x < 9:
-                send[128 + 9 * c + x] = tile
+                send[128 + 9 * k + x] = tile
             else:
-                keep[128 + 9 * c + x - 9] = tile
+                keep[128 + 9 * k + x - 9] = tile
         for q in range(4):
             s_tile = ssum[pl.ds(x * 32 + q, 8, stride=4), :]
             d_tile = dsum[pl.ds(x * 32 + q, 8, stride=4), :]
@@ -186,9 +188,9 @@
                 keep[4 * (x - 2) + q] = s_tile
                 keep[64 + 4 * (x - 2) + q] = d_tile
     for k, x in enumerate((1, 5, 9, 13)):
-        send[164 + k] = osum[x]
+        send[155 + k] = osum[x]
     for k, x in enumerate((2, 5, 9, 13)):
-        keep[164 + k] = osum[x]
+        keep[155 + k] = osum[x]
 
 
 def lane_index():
@@ -297,30 +299,37 @@
     mid_sweep(w_b, w_a, c1, cb1, 13, 27)
 
 
-def coupled_kernel(keep, got, coupled):
-    for c in range(4):
+def joined(keep, got, t, at):
+    own, other = at + 4 * t, at + 4 * (t - 14)
+    if t < 14:
+        return keep[own]
+    return keep[own] + got[other] if t < 16 else got[other]
+
+
+def coupled_kernel(place, keep, got, coupled, flat):
+    for k, c in enumerate(OTHERS):
         for x in range(CX):
+            at = 128 + 9 * k + x
             if x < 7:
-                tile = keep[128 + 9 * c + x]
+                tile = keep[at]
             elif x < 9:
-                tile = keep[128 + 9 * c + x] + got[128 + 9 * c + x - 7]
+                tile = keep[at] + got[at - 7]
             else:
-                tile = got[128 + 9 * c + x - 7]
+                tile = got[at - 7]
             coupled[c, x] = tile
+    for x in range(CX):
+        for q in range(4):
+            flat[pl.ds(x * 32 + q, 8, stride=4), :] = joined(keep, got, 7 + x, 64 + q)
+    for x in range(CX):
+        coupled[1, x] = flat[pl.ds(pl.multiple_of(x * 32 + 8 * place[0], 8), 8), :]
 
 
 def start_kernel(keep, got, cc, cb, gg, v2, send, dk):
     for t in range(T0):
         block = (t + 1) // 4
-        opened = keep[164 + block] if block < 4 else got[160 + block]
+        opened = keep[155 + block] if block < 4 else got[151 + block]
         for q in range(4):
-            at = 4 * (t - 14) + q
-            if t < 14:
-                s_tile, d_tile = keep[4 * t + q], keep[64 + 4 * t + q]
-            elif t < 16:
-                s_tile, d_tile = keep[4 * t + q] + got[at], keep[64 + 4 * t + q] + got[64 + at]
-            else:
-                s_tile, d_tile = got[at], got[64 + at]
+            s_tile, d_tile = joined(keep, got, t, q), joined(keep, got, t, 64 + q)
             diag = 6.0 + d_tile
             coef = OMEGA * opened / diag
             cc[t, q] = coef
@@ -333,7 +342,7 @@
     even = (2 * lane) % NZ
     for k in range(8):
         block = 2 + k // 2
-        opened = take(keep[164 + block] if block < 4 else got[160 + block], even)
+        opened = take(keep[155 + block] if block < 4 else got[151 + block], even)
         d_sum = [0.0, 0.0]
         for dx in range(2):
             for q in range(4):
@@ -429,11 +438,13 @@
     return lax.ppermute(block, "box", [(i ^ 1, i) for i in range(lax.axis_size("box"))])
 
 
-def around(block, core):
+def around(block, core, beside=None):
     far_low, far_high = fetch(block, -2), fetch(block, 2)
     first = swap(block)
-    second = swap(jnp.where(core == 0, far_high, far_low))
-    return [far_low, second, block, first, far_high]
+    onward = jnp.where(core == 0, far_high, far_low)
+    if beside is not None:
+        onward, beside = lax.optimization_barrier((onward, beside))
+    return [far_low, swap(onward), block, first, far_high], beside
 
 
 def shards(volume, drag, momentum, offsets, cell_index, destinations, rhs, wall):
@@ -453,7 +464,7 @@
     incoming = lax.all_to_all(outgoing, "box", split_axis=0, concat_axis=0, tiled=True)
     pay, craw = call(
         deposit_kernel,
-        [(3 * XE + XE // 2, 8, NZ), (4, XE, 8, NZ)],
+        [(3 * XE + XE // 2, 8, NZ), (3, XE, 8, NZ)],
         [((13, CAP, NZ), F32), ((3, CAP, NZ), I32), ((XE, CAP, NZ), F32), ((768, NZ), F32)]
         + [((768, SLOTS // CHUNKS), BF16)] * CHUNKS + [((NZ, SLOTS // CHUNKS), BF16)] * CHUNKS,
         [incoming.reshape(N_BOX, 8 * CAP), rhs, wall, prev],
@@ -461,7 +472,7 @@
     slabs = lax.all_gather(pay, "slab")
     send, keep = call(
         slab_kernel,
-        [(168, 8, NZ), (168, 8, NZ)],
+        [(159, 8, NZ), (159, 8, NZ)],
         [((XE * 32, NZ), F32), ((XE * 32, NZ), F32), ((XE, 8, NZ), F32)],
         [place, slabs, craw],
         smem_first=True,
@@ -471,20 +482,28 @@
     cc, cb, gg, v2, first = call(
         start_kernel, [fine, fine, (CX, 4, 8, NZ), fine, (28, 8, NZ)], [((CX, 4, 8, NZ), F32)], [keep, got]
     )
-    (coupled,) = call(coupled_kernel, [(4, CX, 8, NZ)], [], [keep, got])
+    (coupled,) = call(
+        coupled_kernel,
+        [(4, CX, 8, NZ)],
+        [((CX * 32, NZ), F32)],
+        [place, keep, got],
+        smem_first=True,
+    )
     scratch = [(mid, F32), (mid, F32), (mid, F32), (low, F32), (low, F32), (low, F32), (fine, F32), (fine, F32)]
+    parts, coupled = around(first, core, coupled)
     v3, c1, g1, c2, second = call(
         middle_kernel,
         [fine, mid, mid, low, (8, 8, NZ)],
         scratch,
-        [place] + around(first, core) + [cc, cb, gg, v2],
+        [place] + parts + [cc, cb, gg, v2],
         smem_first=True,
     )
+    parts, _ = around(second, core)
     (pressure,) = call(
         last_kernel,
         [(CX, 8, NZ)],
         scratch + [((CX * 32, NZ), F32)],
-        [place] + around(second, core) + [cc, cb, v3, c1, g1, c2],
+        [place] + parts + [cc, cb, v3, c1, g1, c2],
         smem_first=True,
     )
     return coupled, pressure

time: 112 us -> 113 us (level)
  starting transfers between devices: 50.7 us -> 54.8 us
  waiting for transfers between devices: 29 us -> 25.8 us
    ppermute x6, starting transfers between devices: 20.2 us -> 24.2 us  [fetch(): lax.ppermute(block, 'box', [((i + distance) % count, i) for i in range(co...]
    ppermute x6, waiting for transfers between devices: 16.8 us -> 13.2 us  [fetch(): lax.ppermute(block, 'box', [((i + distance) % count, i) for i in range(co...]
  transfers between devices with their start and end apart: 11 -> 11, of which waited for: 6 -> 5; matrix products, arithmetic and copies ran while one was open for 0% -> 0% of each run, Pallas kernels for 1% -> 1%
where the time goes in v3:
time: 113 us
  starting transfers between devices  54.8 us (48%)
  waiting for transfers between devices  25.8 us (23%)
  Pallas kernels  16.2 us (14%)
  blocking collectives  13.4 us (12%)
  local copies, waits for them, and re-layouts  1.61 us (1%)
    ppermute x6, starting transfers between devices, fetch(): lax.ppermute(block, 'box', [((i + distance) % count, i) for i in range(co...  24.2 us
    all_to_all x1, starting transfers between devices, shards(): lax.all_to_all(outgoing, 'box', split_axis=0, concat_axis=0, tiled=True)  20.4 us
    pallas_call x7, Pallas kernels, call(): pl.pallas_call(kernel, out_shape=shapes, in_specs=specs, out_specs=[pl.Bl...  16.2 us
    all_gather x1, blocking collectives, shards(): slabs = lax.all_gather(pay, 'slab')  13.4 us
    ppermute x6, waiting for transfers between devices, fetch(): lax.ppermute(block, 'box', [((i + distance) % count, i) for i in range(co...  13.2 us
    all_to_all x1, waiting for transfers between devices, shards(): lax.all_to_all(outgoing, 'box', split_axis=0, concat_axis=0, tiled=True)  10.8 us
    ppermute x4, starting transfers between devices, swap(): lax.ppermute(block, 'box', [(i ^ 1, i) for i in range(lax.axis_size('box'...  10.2 us
  transfers between devices with their start and end apart: 11, of which 5 were waited for; matrix products, arithmetic and copies ran while one was open for 0% of the time, Pallas kernels for 1%

profile of v3, /device:TPU:1, one launch (start us, length us, event | category | flops | bytes accessed | tf_op | source)
XLA Modules:
  0.0 112.6 jit_solution(7022911151116659974)
XLA Ops:
  0.6 2.9 %shard_map.95 = f32[128,1,256]{2,1,0:T(1,128)} custom-call(f32[1,2048]{1,0:T(1,128)} %bitcast.12, f32[1,2048]{1,0:T(1,128)} %bitcast.13, f32[2,2048]{1,0:T(2,128)} %mom_in.1, f32[3,2048]{1,0:T(4,128)} %off_in.1, s32[1,2048]{1,0:T(1,128)} %bitcast.14, s32[1,2048]{1,0:T(1,128)} %bitcast.15), custom_call_target="tpu_custom_call" | custom-call | flops 1000000 | bytes 1000000 | tf_op jit(solution)/shard_map/pallas_call | solution.py:421
  3.6 20.4 %all-to-all-start = ((f32[128,1,256]{2,1,0:T(1,128)}), f32[128,1,256]{2,1,0:T(1,128)S(1)}, u32[]{:S(2)}, u32[]{:S(2)}) async-start(f32[128,1,256]{2,1,0:T(1,128)} %shard_map.95), calls=%async_computation | async-start | bytes 262144 | tf_op jit(solution)/shard_map/all_to_all | solution.py:464
  24.0 0.0 copy-start.1
  24.0 0.8 copy-done.1
  24.8 0.0 slice-start
  24.8 0.8 slice-done
  25.6 3.5 %collective-permute-start = (f32[18,8,128]{2,1,0:T(8,128)S(1)}, f32[18,8,128]{2,1,0:T(8,128)S(1)}, u32[]{:S(2)}, u32[]{:S(2)}) collective-permute-start(f32[18,8,128]{2,1,0:T(8,128)S(1)} %pad_maximum_fusion), channel_id=1, source_target_pairs={{508,0},{0,4},{4,8},{8,12},{12,16},{16,20},{20,24},{24,28},{28,32}... | collective-permute-start | bytes 221192 | tf_op jit(solution)/shard_map/ppermute | solution.py:434
  29.2 0.1 pad_add_fusion.slab.place
  29.2 0.0 copy-start
  29.2 10.8 %all-to-all-done = f32[128,1,256]{2,1,0:T(1,128)S(1)} async-done(((f32[128,1,256]{2,1,0:T(1,128)}), f32[128,1,256]{2,1,0:T(1,128)S(1)}, u32[]{:S(2)}, u32[]{:S(2)}) %all-to-all-start) | async-done | bytes 131104 | tf_op jit(solution)/shard_map/all_to_all | solution.py:464
  40.1 0.0 collective-permute-done.prev
  40.1 0.0 copy-done
  40.1 2.7 %shard_map.96 = (f32[63,8,128]{2,1,0:T(8,128)S(1)}, f32[3,18,8,128]{3,2,1,0:T(8,128)S(1)}) custom-call(f32[128,256]{1,0:T(8,128)S(1)} %bitcast.11, f32[16,8,128]{2,1,0:T(8,128)S(1)} %copy-done, s32[16,8,128]{2,1,0:T(8,128)S(1)} %copy-done.1, f32[18,8,128]{2,1,0:T(8,128)S(1)} %collective-permute-done.prev), custom_call_target="tpu_custom_call" | custom-call | flops 1000000 | bytes 1000000 | tf_op jit(solution)/shard_map/pallas_call | solution.py:421
  42.8 13.4 %all-gather = f32[252,8,128]{2,1,0:T(8,128)S(1)} all-gather(f32[63,8,128]{2,1,0:T(8,128)S(1)} %get-tuple-element.18), channel_id=2, replica_groups=mesh['box'=128,'slab'=4] {'slab'}, dimensions={0}, use_global_device_ids=true | all-gather | bytes 1290240 | tf_op jit(solution)/shard_map/all_gather | solution.py:472
  56.2 0.9 shard_map.97
  57.1 4.1 %collective-permute-start.1 = (f32[159,8,128]{2,1,0:T(8,128)S(1)}, f32[159,8,128]{2,1,0:T(8,128)S(1)}, u32[]{:S(2)}, u32[]{:S(2)}) collective-permute-start(f32[159,8,128]{2,1,0:T(8,128)S(1)} %get-tuple-element.21), channel_id=1, source_target_pairs={{4,0},{8,4},{12,8},{16,12},{20,16},{24,20},{28,24},{32,28},{36,32}... | collective-permute-start | bytes 1953800 | tf_op jit(solution)/shard_map/ppermute | solution.py:434
  61.2 9.5 %collective-permute-done.1.got = f32[159,8,128]{2,1,0:T(8,128)S(1)} collective-permute-done((f32[159,8,128]{2,1,0:T(8,128)S(1)}, f32[159,8,128]{2,1,0:T(8,128)S(1)}, u32[]{:S(2)}, u32[]{:S(2)}) %collective-permute-start.1) | collective-permute-done | bytes 651296 | tf_op jit(solution)/shard_map/ppermute | solution.py:434
  70.7 1.5 %shard_map.98 = (f32[30,4,8,128]{3,2,1,0:T(8,128)S(1)}, f32[30,4,8,128]{3,2,1,0:T(8,128)S(1)}, f32[16,4,8,128]{3,2,1,0:T(8,128)S(1)}, f32[30,4,8,128]{3,2,1,0:T(8,128)S(1)}, f32[28,8,128]{2,1,0:T(8,128)S(1)}) custom-call(f32[159,8,128]{2,1,0:T(8,128)S(1)} %get-tuple-element.20.keep, f32[159,8,128]{2,1,0:T(8,128)S(1)} %collective-permute-done.1.got), custom_call_target="tpu_custom_call" | custom-call | flops 1000000 | bytes 1000000 | tf_op jit(solution)/shard_map/pallas_call | solution.py:421
  72.2 3.0 %collective-permute-start.3 = (f32[28,8,128]{2,1,0:T(8,128)S(1)}, f32[28,8,128]{2,1,0:T(8,128)S(1)}, u32[]{:S(2)}, u32[]{:S(2)}) collective-permute-start(f32[28,8,128]{2,1,0:T(8,128)S(1)} %get-tuple-element.22.own), channel_id=1, source_target_pairs={{504,0},{508,4},{0,8},{4,12},{8,16},{12,20},{16,24},{20,28},{24,32... | collective-permute-start | bytes 344072 | tf_op jit(solution)/shard_map/ppermute | solution.py:434
  75.3 5.6 %collective-permute-start.2 = (f32[28,8,128]{2,1,0:T(8,128)S(1)}, f32[28,8,128]{2,1,0:T(8,128)S(1)}, u32[]{:S(2)}, u32[]{:S(2)}) collective-permute-start(f32[28,8,128]{2,1,0:T(8,128)S(1)} %get-tuple-element.22.own), channel_id=1, source_target_pairs={{8,0},{12,4},{16,8},{20,12},{24,16},{28,20},{32,24},{36,28},{40,32... | collective-permute-start | bytes 344072 | tf_op jit(solution)/shard_map/ppermute | solution.py:434
  80.8 1.9 %collective-permute-start.5 = (f32[28,8,128]{2,1,0:T(8,128)S(1)}, f32[28,8,128]{2,1,0:T(8,128)S(1)}, u32[]{:S(2)}, u32[]{:S(2)}) collective-permute-start(f32[28,8,128]{2,1,0:T(8,128)S(1)} %get-tuple-element.22.own), channel_id=1, source_target_pairs={{4,0},{0,4},{12,8},{8,12},{20,16},{16,20},{28,24},{24,28},{36,32},... | collective-permute-start | bytes 344072 | tf_op jit(solution)/shard_map/ppermute | solution.py:438
  82.8 1.3 %shard_map.99 = f32[4,16,8,128]{3,2,1,0:T(8,128)} custom-call(s32[2]{0:T(128)S(1)} %pad_add_fusion.slab.place, f32[159,8,128]{2,1,0:T(8,128)S(1)} %get-tuple-element.20.keep, f32[159,8,128]{2,1,0:T(8,128)S(1)} %collective-permute-done.1.got), custom_call_target="tpu_custom_call" | custom-call | flops 1000000 | bytes 1000000 | tf_op jit(solution)/shard_map/pallas_call | solution.py:421
  84.1 0.0 collective-permute-done.3.far_low
  84.1 0.0 collective-permute-done.2.far_high
  84.1 2.4 %collective-permute-start.4 = (f32[28,8,128]{2,1,0:T(8,128)S(1)}, f32[28,8,128]{2,1,0:T(8,128)S(1)}, u32[]{:S(2)}, u32[]{:S(2)}) collective-permute-start(f32[28,8,128]{2,1,0:T(8,128)S(1)} %broadcast_select_fusion), channel_id=1, source_target_pairs={{4,0},{0,4},{12,8},{8,12},{20,16},{16,20},{28,24},{24,28},{36,32},... | collective-permute-start | bytes 344072 | tf_op jit(solution)/shard_map/ppermute | solution.py:438
  86.5 0.0 collective-permute-done.5.first
  86.5 0.9 collective-permute-done.4.second
  87.4 3.9 %shard_map.100 = (f32[30,4,8,128]{3,2,1,0:T(8,128)S(1)}, f32[40,8,128]{2,1,0:T(8,128)S(1)}, f32[40,8,128]{2,1,0:T(8,128)S(1)}, f32[20,8,128]{2,1,0:T(8,128)S(1)}, f32[8,8,128]{2,1,0:T(8,128)S(1)}) custom-call(s32[2]{0:T(128)S(1)} %pad_add_fusion.slab.place, f32[28,8,128]{2,1,0:T(8,128)S(1)} %collective-permute-done.3.far_low, ...), custom_call_target="tpu_custom_call" | custom-call | flops 1000000 | bytes 1000000 | tf_op jit(solution)/shard_map/pallas_call | solution.py:421
  91.4 6.0 %collective-permute-start.7 = (f32[8,8,128]{2,1,0:T(8,128)S(1)}, f32[8,8,128]{2,1,0:T(8,128)S(1)}, u32[]{:S(2)}, u32[]{:S(2)}) collective-permute-start(f32[8,8,128]{2,1,0:T(8,128)S(1)} %get-tuple-element.29.own), channel_id=1, source_target_pairs={{8,0},{12,4},{16,8},{20,12},{24,16},{28,20},{32,24},{36,28},{40,32... | collective-permute-start | bytes 98312 | tf_op jit(solution)/shard_map/ppermute | solution.py:434
  97.4 1.9 %collective-permute-start.6 = (f32[8,8,128]{2,1,0:T(8,128)S(1)}, f32[8,8,128]{2,1,0:T(8,128)S(1)}, u32[]{:S(2)}, u32[]{:S(2)}) collective-permute-start(f32[8,8,128]{2,1,0:T(8,128)S(1)} %get-tuple-element.29.own), channel_id=1, source_target_pairs={{504,0},{508,4},{0,8},{4,12},{8,16},{12,20},{16,24},{20,28},{24,32... | collective-permute-start | bytes 98312 | tf_op jit(solution)/shard_map/ppermute | solution.py:434
  99.3 2.4 %collective-permute-start.9 = (f32[8,8,128]{2,1,0:T(8,128)S(1)}, f32[8,8,128]{2,1,0:T(8,128)S(1)}, u32[]{:S(2)}, u32[]{:S(2)}) collective-permute-start(f32[8,8,128]{2,1,0:T(8,128)S(1)} %get-tuple-element.29.own), channel_id=1, source_target_pairs={{4,0},{0,4},{12,8},{8,12},{20,16},{16,20},{28,24},{24,28},{36,32},... | collective-permute-start | bytes 98312 | tf_op jit(solution)/shard_map/ppermute | solution.py:438
  101.7 0.0 collective-permute-done.7.far_high
  101.7 3.7 %collective-permute-done.6.far_low = f32[8,8,128]{2,1,0:T(8,128)S(1)} collective-permute-done((f32[8,8,128]{2,1,0:T(8,128)S(1)}, f32[8,8,128]{2,1,0:T(8,128)S(1)}, u32[]{:S(2)}, u32[]{:S(2)}) %collective-permute-start.6) | collective-permute-done | bytes 32800 | tf_op jit(solution)/shard_map/ppermute | solution.py:434
  105.4 3.5 %collective-permute-start.8 = (f32[8,8,128]{2,1,0:T(8,128)S(1)}, f32[8,8,128]{2,1,0:T(8,128)S(1)}, u32[]{:S(2)}, u32[]{:S(2)}) collective-permute-start(f32[8,8,128]{2,1,0:T(8,128)S(1)} %broadcast_select_fusion.1), channel_id=1, source_target_pairs={{4,0},{0,4},{12,8},{8,12},{20,16},{16,20},{28,24},{24,28},{36,32},... | collective-permute-start | bytes 98312 | tf_op jit(solution)/shard_map/ppermute | solution.py:438
  108.9 0.0 collective-permute-done.9.first
  108.9 0.8 collective-permute-done.8.second
  109.7 2.9 %shard_map.101 = f32[16,8,128]{2,1,0:T(8,128)} custom-call(s32[2]{0:T(128)S(1)} %pad_add_fusion.slab.place, f32[8,8,128]{2,1,0:T(8,128)S(1)} %collective-permute-done.6.far_low, f32[8,8,128]{2,1,0:T(8,128)S(1)} %collective-permute-done.8.second, f32[8,8,128]{2,1,0:T(8,128)S(1)} %get-tuple-element.29.own, f32[8,8,128]{2,1,0:T(8,128)S(1)} %collective-permute-done.9.first, ...), custom_call_target="tpu_custom_call" | custom-call | flops 1000000 | bytes 1000000 | tf_op jit(solution)/shard_map/pallas_call | solution.py:421
  (5 shorter events, 0.0 us)
Async XLA Ops:
  3.6 36.5 %all-to-all-start = ((f32[128,1,256]{2,1,0:T(1,128)}), f32[128,1,256]{2,1,0:T(1,128)S(1)}, u32[]{:S(2)}, u32[]{:S(2)}) async-start(f32[128,1,256]{2,1,0:T(1,128)} %shard_map.95), calls=%async_computation | async-start | bytes 262144 | tf_op jit(solution)/shard_map/all_to_all | solution.py:464
  24.0 0.8 copy-start.1
  24.8 0.8 slice-start
  25.6 14.5 %collective-permute-start = (f32[18,8,128]{2,1,0:T(8,128)S(1)}, f32[18,8,128]{2,1,0:T(8,128)S(1)}, u32[]{:S(2)}, u32[]{:S(2)}) collective-permute-start(f32[18,8,128]{2,1,0:T(8,128)S(1)} %pad_maximum_fusion), channel_id=1, source_target_pairs={{508,0},{0,4},{4,8},{8,12},{12,16},{16,20},{20,24},{24,28},{28,32}... | collective-permute-start | bytes 221192 | tf_op jit(solution)/shard_map/ppermute | solution.py:434
  29.2 10.8 %copy-start = (f32[16,8,128]{2,1,0:T(8,128)S(1)}, f32[16,8,128]{2,1,0:T(8,128)}, u32[]{:S(2)}) copy-start(f32[16,8,128]{2,1,0:T(8,128)} %rhs.1) | copy-start | bytes 196612
  57.1 13.6 %collective-permute-start.1 = (f32[159,8,128]{2,1,0:T(8,128)S(1)}, f32[159,8,128]{2,1,0:T(8,128)S(1)}, u32[]{:S(2)}, u32[]{:S(2)}) collective-permute-start(f32[159,8,128]{2,1,0:T(8,128)S(1)} %get-tuple-element.21), channel_id=1, source_target_pairs={{4,0},{8,4},{12,8},{16,12},{20,16},{24,20},{28,24},{32,28},{36,32}... | collective-permute-start | bytes 1953800 | tf_op jit(solution)/shard_map/ppermute | solution.py:434
  72.2 11.8 %collective-permute-start.3 = (f32[28,8,128]{2,1,0:T(8,128)S(1)}, f32[28,8,128]{2,1,0:T(8,128)S(1)}, u32[]{:S(2)}, u32[]{:S(2)}) collective-permute-start(f32[28,8,128]{2,1,0:T(8,128)S(1)} %get-tuple-element.22.own), channel_id=1, source_target_pairs={{504,0},{508,4},{0,8},{4,12},{8,16},{12,20},{16,24},{20,28},{24,32... | collective-permute-start | bytes 344072 | tf_op jit(solution)/shard_map/ppermute | solution.py:434
  75.3 8.8 %collective-permute-start.2 = (f32[28,8,128]{2,1,0:T(8,128)S(1)}, f32[28,8,128]{2,1,0:T(8,128)S(1)}, u32[]{:S(2)}, u32[]{:S(2)}) collective-permute-start(f32[28,8,128]{2,1,0:T(8,128)S(1)} %get-tuple-element.22.own), channel_id=1, source_target_pairs={{8,0},{12,4},{16,8},{20,12},{24,16},{28,20},{32,24},{36,28},{40,32... | collective-permute-start | bytes 344072 | tf_op jit(solution)/shard_map/ppermute | solution.py:434
  80.8 5.7 %collective-permute-start.5 = (f32[28,8,128]{2,1,0:T(8,128)S(1)}, f32[28,8,128]{2,1,0:T(8,128)S(1)}, u32[]{:S(2)}, u32[]{:S(2)}) collective-permute-start(f32[28,8,128]{2,1,0:T(8,128)S(1)} %get-tuple-element.22.own), channel_id=1, source_target_pairs={{4,0},{0,4},{12,8},{8,12},{20,16},{16,20},{28,24},{24,28},{36,32},... | collective-permute-start | bytes 344072 | tf_op jit(solution)/shard_map/ppermute | solution.py:438
  84.1 3.4 %collective-permute-start.4 = (f32[28,8,128]{2,1,0:T(8,128)S(1)}, f32[28,8,128]{2,1,0:T(8,128)S(1)}, u32[]{:S(2)}, u32[]{:S(2)}) collective-permute-start(f32[28,8,128]{2,1,0:T(8,128)S(1)} %broadcast_select_fusion), channel_id=1, source_target_pairs={{4,0},{0,4},{12,8},{8,12},{20,16},{16,20},{28,24},{24,28},{36,32},... | collective-permute-start | bytes 344072 | tf_op jit(solution)/shard_map/ppermute | solution.py:438
  91.4 10.3 %collective-permute-start.7 = (f32[8,8,128]{2,1,0:T(8,128)S(1)}, f32[8,8,128]{2,1,0:T(8,128)S(1)}, u32[]{:S(2)}, u32[]{:S(2)}) collective-permute-start(f32[8,8,128]{2,1,0:T(8,128)S(1)} %get-tuple-element.29.own), channel_id=1, source_target_pairs={{8,0},{12,4},{16,8},{20,12},{24,16},{28,20},{32,24},{36,28},{40,32... | collective-permute-start | bytes 98312 | tf_op jit(solution)/shard_map/ppermute | solution.py:434
  97.4 8.0 %collective-permute-start.6 = (f32[8,8,128]{2,1,0:T(8,128)S(1)}, f32[8,8,128]{2,1,0:T(8,128)S(1)}, u32[]{:S(2)}, u32[]{:S(2)}) collective-permute-start(f32[8,8,128]{2,1,0:T(8,128)S(1)} %get-tuple-element.29.own), channel_id=1, source_target_pairs={{504,0},{508,4},{0,8},{4,12},{8,16},{12,20},{16,24},{20,28},{24,32... | collective-permute-start | bytes 98312 | tf_op jit(solution)/shard_map/ppermute | solution.py:434
  99.3 9.6 %collective-permute-start.9 = (f32[8,8,128]{2,1,0:T(8,128)S(1)}, f32[8,8,128]{2,1,0:T(8,128)S(1)}, u32[]{:S(2)}, u32[]{:S(2)}) collective-permute-start(f32[8,8,128]{2,1,0:T(8,128)S(1)} %get-tuple-element.29.own), channel_id=1, source_target_pairs={{4,0},{0,4},{12,8},{8,12},{20,16},{16,20},{28,24},{24,28},{36,32},... | collective-permute-start | bytes 98312 | tf_op jit(solution)/shard_map/ppermute | solution.py:438
  105.4 4.3 %collective-permute-start.8 = (f32[8,8,128]{2,1,0:T(8,128)S(1)}, f32[8,8,128]{2,1,0:T(8,128)S(1)}, u32[]{:S(2)}, u32[]{:S(2)}) collective-permute-start(f32[8,8,128]{2,1,0:T(8,128)S(1)} %broadcast_select_fusion.1), channel_id=1, source_target_pairs={{4,0},{0,4},{12,8},{8,12},{20,16},{16,20},{28,24},{24,28},{36,32},... | collective-permute-start | bytes 98312 | tf_op jit(solution)/shard_map/ppermute | solution.py:438

commit v4 on v3

--- a/solution.py
+++ b/solution.py
@@ -148,15 +148,13 @@
         pay[3 * XE + x // 2, (x % 2) * 4 : (x % 2) * 4 + 4, :] = extra
 
 
-def slab_kernel(slab, got, craw, send, keep, ssum, dsum, osum):
-    s_me = slab[0]
+HEAD = 11
+LATE = CX - HEAD
+
+
+def slab_sums(got, rows, ssum, dsum):
     sub = lax.broadcasted_iota(I32, (8, NZ), 0)
-    first, last = sub == 0, sub == 7
-
-    def edges(tile, to_first, to_last):
-        return tile + jnp.where(first, to_first, 0.0) + jnp.where(last, to_last, 0.0)
-
-    for x in range(XE):
+    for n, x in enumerate(rows):
         g_row = (x % 2) * 4
         halos = [got[s, 2 * XE + x] for s in range(4)]
         for s in range(4):
@@ -166,31 +164,104 @@
             o_f, o_l = extra[g_row + 2 : g_row + 3], extra[g_row + 3 : g_row + 4]
             from_below = o_f * (below[5:6] + below[7:8] - below[1:2] * rhs_f)
             from_above = o_l * (above[4:5] + above[6:7] - above[0:1] * rhs_l)
-            at = x * 32 + s * 8
-            ssum[at : at + 8, :] = edges(got[s, x], from_below, from_above)
-            dsum[at : at + 8, :] = edges(got[s, XE + x], below[3:4], above[2:3])
-            osum[x, 2 * s : 2 * s + 2, :] = extra[g_row + 2 : g_row + 4]
+            at = n * 32 + s * 8
+            ssum[at : at + 8, :] = edges(sub, got[s, x], from_below, from_above)
+            dsum[at : at + 8, :] = edges(sub, got[s, XE + x], below[3:4], above[2:3])
+
+
+def edges(sub, tile, to_first, to_last):
+    return tile + jnp.where(sub == 0, to_first, 0.0) + jnp.where(sub == 7, to_last, 0.0)
+
+
+def opened_block(got, x, out, at):
+    g_row = (x % 2) * 4
+    for s in range(4):
+        out[at, 2 * s : 2 * s + 2, :] = got[s, 3 * XE + x // 2, g_row + 2 : g_row + 4, :]
+
+
+def head_kernel(got, head, ssum, dsum):
+    slab_sums(got, range(HEAD), ssum, dsum)
+    for x in range(HEAD):
+        for q in range(4):
+            head[4 * x + q] = ssum[pl.ds(x * 32 + q, 8, stride=4), :]
+            head[4 * (HEAD + x) + q] = dsum[pl.ds(x * 32 + q, 8, stride=4), :]
+    for k, x in enumerate((1, 5, 9)):
+        opened_block(got, x, head, 8 * HEAD + k)
+
+
+def late_kernel(place, got, craw, late, keep, ssum, dsum):
+    s_me = place[0]
+    sub = lax.broadcasted_iota(I32, (8, NZ), 0)
+    slab_sums(got, range(HEAD, XE), ssum, dsum)
+    for n in range(XE - HEAD):
+        for q in range(4):
+            s_tile = ssum[pl.ds(n * 32 + q, 8, stride=4), :]
+            d_tile = dsum[pl.ds(n * 32 + q, 8, stride=4), :]
+            if n < LATE:
+                late[4 * n + q] = s_tile
+                late[4 * (LATE + n) + q] = d_tile
+            else:
+                keep[4 * (n - LATE) + q] = s_tile
+                keep[4 * (n - LATE + 2) + q] = d_tile
+    for x in range(XE):
         below = got[(s_me + 3) % 4, 2 * XE + x]
         above = got[(s_me + 1) % 4, 2 * XE + x]
         for k, c in enumerate(OTHERS):
-            tile = edges(craw[k, x], below[2 * c + 1 : 2 * c + 2], above[2 * c : 2 * c + 1])
+            tile = edges(sub, craw[k, x], below[2 * c + 1 : 2 * c + 2], above[2 * c : 2 * c + 1])
             if x < 9:
-                send[128 + 9 * k + x] = tile
+                late[8 * LATE + 9 * k + x] = tile
             else:
-                keep[128 + 9 * k + x - 9] = tile
-        for q in range(4):
-            s_tile = ssum[pl.ds(x * 32 + q, 8, stride=4), :]
-            d_tile = dsum[pl.ds(x * 32 + q, 8, stride=4), :]
-            if x < CX:
-                send[4 * x + q] = s_tile
-                send[64 + 4 * x + q] = d_tile
-            if x >= 2:
-                keep[4 * (x - 2) + q] = s_tile
-                keep[64 + 4 * (x - 2) + q] = d_tile
-    for k, x in enumerate((1, 5, 9, 13)):
-        send[155 + k] = osum[x]
-    for k, x in enumerate((2, 5, 9, 13)):
-        keep[155 + k] = osum[x]
+                keep[16 + 9 * k + x - 9] = tile
+    opened_block(got, 13, late, 8 * LATE + 27)
+
+
+class Parts:
+    def __init__(self, own_head, own_late, keep, next_head, next_late=None):
+        self.own = (own_head, own_late, keep)
+        self.next = (next_head, next_late)
+
+    @staticmethod
+    def tile(parts, x, kind, q):
+        if x < HEAD:
+            return parts[0][4 * (HEAD * kind + x) + q]
+        if x < CX:
+            return parts[1][4 * (LATE * kind + x - HEAD) + q]
+        return parts[2][4 * (2 * kind + x - CX) + q]
+
+    def joined(self, t, kind, q):
+        if t < 14:
+            return self.tile(self.own, t + 2, kind, q)
+        other = self.tile(self.next, t - 14, kind, q)
+        return other if t > 15 else other + self.tile(self.own, t + 2, kind, q)
+
+    def opened(self, block):
+        head, late = (self.own if block < 4 else self.next)[:2]
+        k = block % 4
+        return head[8 * HEAD + k] if k < 3 else late[8 * LATE + 27]
+
+    def coefficient(self, t, q):
+        diag = 6.0 + self.joined(t, 1, q)
+        coef = OMEGA * self.opened((t + 1) // 4) / diag
+        return coef, coef * self.joined(t, 0, q), diag
+
+
+class Rows:
+    def __init__(self, mid, rest, low, high):
+        self.mid, self.rest, self.low, self.high = mid, rest, low, high
+
+    def place(self, index):
+        t, q = index
+        if self.low <= t < self.high:
+            return self.mid, (t, q)
+        return self.rest, (t if t < self.low else t - self.high + self.low, q)
+
+    def __getitem__(self, index):
+        ref, at = self.place(index)
+        return ref[at]
+
+    def __setitem__(self, index, tile):
+        ref, at = self.place(index)
+        ref[at] = tile
 
 
 def lane_index():
@@ -299,54 +370,47 @@
     mid_sweep(w_b, w_a, c1, cb1, 13, 27)
 
 
-def joined(keep, got, t, at):
-    own, other = at + 4 * t, at + 4 * (t - 14)
-    if t < 14:
-        return keep[own]
-    return keep[own] + got[other] if t < 16 else got[other]
-
-
-def coupled_kernel(place, keep, got, coupled, flat):
+def rest_kernel(place, own_head, own_late, keep, next_head, next_late, cc, cb, coupled, cc_r, cb_r, v2_r, flat):
+    parts = Parts(own_head, own_late, keep, next_head, next_late)
     for k, c in enumerate(OTHERS):
         for x in range(CX):
-            at = 128 + 9 * k + x
+            own, other = 16 + 9 * k + x, 8 * LATE + 9 * k + x - 7
             if x < 7:
-                tile = keep[at]
+                tile = keep[own]
             elif x < 9:
-                tile = keep[at] + got[at - 7]
+                tile = keep[own] + next_late[other]
             else:
-                tile = got[at - 7]
+                tile = next_late[other]
             coupled[c, x] = tile
     for x in range(CX):
         for q in range(4):
-            flat[pl.ds(x * 32 + q, 8, stride=4), :] = joined(keep, got, 7 + x, 64 + q)
+            flat[pl.ds(x * 32 + q, 8, stride=4), :] = parts.joined(7 + x, 1, q)
     for x in range(CX):
         coupled[1, x] = flat[pl.ds(pl.multiple_of(x * 32 + 8 * place[0], 8), 8), :]
-
-
-def start_kernel(keep, got, cc, cb, gg, v2, send, dk):
-    for t in range(T0):
-        block = (t + 1) // 4
-        opened = keep[155 + block] if block < 4 else got[151 + block]
-        for q in range(4):
-            s_tile, d_tile = joined(keep, got, t, q), joined(keep, got, t, 64 + q)
-            diag = 6.0 + d_tile
-            coef = OMEGA * opened / diag
-            cc[t, q] = coef
-            cb[t, q] = coef * s_tile
+    coefs, bases, v2 = Rows(cc, cc_r, 5, 25), Rows(cb, cb_r, 5, 25), Rows(None, v2_r, 6, 24)
+    for t in (*range(5), *range(25, T0)):
+        for q in range(4):
+            coefs[t, q], bases[t, q], _ = parts.coefficient(t, q)
+    fine_sweep(bases, v2, coefs, bases, 1, 6)
+    fine_sweep(bases, v2, coefs, bases, 24, 29)
+
+
+def start_kernel(own_head, own_late, keep, next_head, cc, cb, gg, v2, send):
+    parts = Parts(own_head, own_late, keep, next_head)
+    for t in range(5, 25):
+        for q in range(4):
+            cc[t, q], cb[t, q], diag = parts.coefficient(t, q)
             if 7 <= t < 23:
-                dk[t - 7, q] = d_tile
                 gg[t - 7, q] = (1.0 / OMEGA) * diag
-    fine_sweep(cb, v2, cc, cb, 1, 29)
+    fine_sweep(cb, v2, cc, cb, 6, 24)
     lane = lane_index()
     even = (2 * lane) % NZ
     for k in range(8):
-        block = 2 + k // 2
-        opened = take(keep[155 + block] if block < 4 else got[151 + block], even)
+        opened = take(parts.opened(2 + k // 2), even)
         d_sum = [0.0, 0.0]
         for dx in range(2):
             for q in range(4):
-                d_sum[q // 2] = d_sum[q // 2] + dk[2 * k + dx, q]
+                d_sum[q // 2] = d_sum[q // 2] + parts.joined(7 + 2 * k + dx, 1, q)
         damp = 0.125 * pack(d_sum)
         diag = 1.5 + damp
         coef = OMEGA * opened / diag
@@ -375,7 +439,7 @@
     return part
 
 
-def middle_kernel(place, far_low, second, own, first, far_high, cc, cb, gg, v2, v_out, c1, g1, c2, send,
+def middle_kernel(place, far_low, second, own, first, far_high, cc, cb, gg, v2, cc_r, cb_r, v2_r, v_out, c1, g1, c2, send,
                   cb1, w_a, w_b, cb2, u_a, u_b, v_a, v_b):
     part = window(place[1], far_low, second, own, first, far_high)
     for n in range(5):
@@ -386,6 +450,7 @@
         for k in range(4):
             c2[4 * n + k] = part(n, 24 + k)
     levels_solve(c1, g1, c2, cb1, w_a, w_b, cb2, u_a, u_b)
+    cc, cb, v2 = Rows(cc, cc_r, 5, 25), Rows(cb, cb_r, 5, 25), Rows(v2, v2_r, 6, 24)
     fine_correct(v2, v_a, w_a, cc, 13, 27)
     fine_sweep(v_a, v_b, cc, cb, 2, 28)
     fine_sweep(v_b, v_a, cc, cb, 3, 27)
@@ -470,23 +535,22 @@
         [incoming.reshape(N_BOX, 8 * CAP), rhs, wall, prev],
     )
     slabs = lax.all_gather(pay, "slab")
-    send, keep = call(
-        slab_kernel,
-        [(159, 8, NZ), (159, 8, NZ)],
-        [((XE * 32, NZ), F32), ((XE * 32, NZ), F32), ((XE, 8, NZ), F32)],
-        [place, slabs, craw],
-        smem_first=True,
-    )
-    got = fetch(send, 1)
+    sums = [((HEAD * 32, NZ), F32)] * 2
+    (head,) = call(head_kernel, [(8 * HEAD + 3, 8, NZ)], sums, [slabs])
+    next_head = fetch(head, 1)
+    late, keep = call(
+        late_kernel, [(8 * LATE + 28, 8, NZ), (43, 8, NZ)], sums, [place, slabs, craw], smem_first=True
+    )
+    next_late = fetch(late, 1)
     fine, mid, low = (T0, 4, 8, NZ), (T1, 8, NZ), (T2, 8, NZ)
     cc, cb, gg, v2, first = call(
-        start_kernel, [fine, fine, (CX, 4, 8, NZ), fine, (28, 8, NZ)], [((CX, 4, 8, NZ), F32)], [keep, got]
-    )
-    (coupled,) = call(
-        coupled_kernel,
-        [(4, CX, 8, NZ)],
+        start_kernel, [fine, fine, (CX, 4, 8, NZ), fine, (28, 8, NZ)], [], [head, late, keep, next_head]
+    )
+    coupled, cc_r, cb_r, v2_r = call(
+        rest_kernel,
+        [(4, CX, 8, NZ), (10, 4, 8, NZ), (10, 4, 8, NZ), (12, 4, 8, NZ)],
         [((CX * 32, NZ), F32)],
-        [place, keep, got],
+        [place, head, late, keep, next_head, next_late, cc, cb],
         smem_first=True,
     )
     scratch = [(mid, F32), (mid, F32), (mid, F32), (low, F32), (low, F32), (low, F32), (fine, F32), (fine, F32)]
@@ -495,7 +559,7 @@
         middle_kernel,
         [fine, mid, mid, low, (8, 8, NZ)],
         scratch,
-        [place] + parts + [cc, cb, gg, v2],
+        [place] + parts + [cc, cb, gg, v2, cc_r, cb_r, v2_r],
         smem_first=True,
     )
     parts, _ = around(second, core)

time: 113 us -> 110 us (0.973)
  waiting for transfers between devices: 25.8 us -> 20 us
  starting transfers between devices: 54.8 us -> 56.9 us
    ppermute x6 -> x7, waiting for transfers between devices: 13.2 us -> 7.49 us  [fetch(): lax.ppermute(block, 'box', [((i + distance) % count, i) for i in range(co...]
    ppermute x6 -> x7, starting transfers between devices: 24.2 us -> 26.3 us  [fetch(): lax.ppermute(block, 'box', [((i + distance) % count, i) for i in range(co...]
    pallas_call x7 -> x8, Pallas kernels: 16.2 us -> 16.9 us  [call(): pl.pallas_call(kernel, out_shape=shapes, in_specs=specs, out_specs=[pl.Bl...]
  transfers between devices with their start and end apart: 11 -> 12, of which waited for: 5 -> 5; matrix products, arithmetic and copies ran while one was open for 0% -> 0% of each run, Pallas kernels for 1% -> 4%
where the time goes in v4:
time: 110 us
  starting transfers between devices  56.9 us (52%)
  waiting for transfers between devices  20 us (18%)
  Pallas kernels  16.9 us (15%)
  blocking collectives  13.4 us (12%)
  local copies, waits for them, and re-layouts  1.61 us (1%)
    ppermute x7, starting transfers between devices, fetch(): lax.ppermute(block, 'box', [((i + distance) % count, i) for i in range(co...  26.3 us
    all_to_all x1, starting transfers between devices, shards(): lax.all_to_all(outgoing, 'box', split_axis=0, concat_axis=0, tiled=True)  20.4 us
    pallas_call x8, Pallas kernels, call(): pl.pallas_call(kernel, out_shape=shapes, in_specs=specs, out_specs=[pl.Bl...  16.9 us
    all_gather x1, blocking collectives, shards(): slabs = lax.all_gather(pay, 'slab')  13.4 us
    all_to_all x1, waiting for transfers between devices, shards(): lax.all_to_all(outgoing, 'box', split_axis=0, concat_axis=0, tiled=True)  10.8 us
    ppermute x4, starting transfers between devices, swap(): lax.ppermute(block, 'box', [(i ^ 1, i) for i in range(lax.axis_size('box'...  10.2 us
    ppermute x7, waiting for transfers between devices, fetch(): lax.ppermute(block, 'box', [((i + distance) % count, i) for i in range(co...  7.49 us
  transfers between devices with their start and end apart: 12, of which 5 were waited for; matrix products, arithmetic and copies ran while one was open for 0% of the time, Pallas kernels for 4%

profile of v4, /device:TPU:1, one launch (start us, length us, event | category | flops | bytes accessed | tf_op | source)
XLA Modules:
  0.0 109.8 jit_solution(10373801303976786936)
XLA Ops:
  0.6 2.9 %shard_map.95 = f32[128,1,256]{2,1,0:T(1,128)} custom-call(f32[1,2048]{1,0:T(1,128)} %bitcast.13, f32[1,2048]{1,0:T(1,128)} %bitcast.14, f32[2,2048]{1,0:T(2,128)} %mom_in.1, f32[3,2048]{1,0:T(4,128)} %off_in.1, s32[1,2048]{1,0:T(1,128)} %bitcast.15, s32[1,2048]{1,0:T(1,128)} %bitcast.16), custom_call_target="tpu_custom_call" | custom-call | flops 1000000 | bytes 1000000 | tf_op jit(solution)/shard_map/pallas_call | solution.py:486
  3.6 20.4 %all-to-all-start = ((f32[128,1,256]{2,1,0:T(1,128)}), f32[128,1,256]{2,1,0:T(1,128)S(1)}, u32[]{:S(2)}, u32[]{:S(2)}) async-start(f32[128,1,256]{2,1,0:T(1,128)} %shard_map.95), calls=%async_computation | async-start | bytes 262144 | tf_op jit(solution)/shard_map/all_to_all | solution.py:529
  24.0 0.0 copy-start.1
  24.0 0.8 copy-done.1
  24.8 0.0 slice-start
  24.8 0.8 slice-done
  25.6 0.0 copy-start
  25.6 3.7 %collective-permute-start = (f32[18,8,128]{2,1,0:T(8,128)S(1)}, f32[18,8,128]{2,1,0:T(8,128)S(1)}, u32[]{:S(2)}, u32[]{:S(2)}) collective-permute-start(f32[18,8,128]{2,1,0:T(8,128)S(1)} %pad_maximum_fusion), channel_id=1, source_target_pairs={{508,0},{0,4},{4,8},{8,12},{12,16},{16,20},{20,24},{24,28},{28,32}... | collective-permute-start | bytes 221192 | tf_op jit(solution)/shard_map/ppermute | solution.py:499
  29.3 10.8 %all-to-all-done = f32[128,1,256]{2,1,0:T(1,128)S(1)} async-done(((f32[128,1,256]{2,1,0:T(1,128)}), f32[128,1,256]{2,1,0:T(1,128)S(1)}, u32[]{:S(2)}, u32[]{:S(2)}) %all-to-all-start) | async-done | bytes 131104 | tf_op jit(solution)/shard_map/all_to_all | solution.py:529
  40.1 0.0 collective-permute-done.prev
  40.1 0.0 copy-done
  40.1 2.7 %shard_map.96 = (f32[63,8,128]{2,1,0:T(8,128)S(1)}, f32[3,18,8,128]{3,2,1,0:T(8,128)S(1)}) custom-call(f32[128,256]{1,0:T(8,128)S(1)} %bitcast.12, f32[16,8,128]{2,1,0:T(8,128)S(1)} %copy-done, s32[16,8,128]{2,1,0:T(8,128)S(1)} %copy-done.1, f32[18,8,128]{2,1,0:T(8,128)S(1)} %collective-permute-done.prev), custom_call_target="tpu_custom_call" | custom-call | flops 1000000 | bytes 1000000 | tf_op jit(solution)/shard_map/pallas_call | solution.py:486
  42.8 13.4 %all-gather = f32[252,8,128]{2,1,0:T(8,128)S(1)} all-gather(f32[63,8,128]{2,1,0:T(8,128)S(1)} %get-tuple-element.22), channel_id=2, replica_groups=mesh['box'=128,'slab'=4] {'slab'}, dimensions={0}, use_global_device_ids=true | all-gather | bytes 1290240 | tf_op jit(solution)/shard_map/all_gather | solution.py:537
  56.2 0.2 shard_map.97.own_head
  56.4 4.1 %collective-permute-start.1 = (f32[91,8,128]{2,1,0:T(8,128)S(1)}, f32[91,8,128]{2,1,0:T(8,128)S(1)}, u32[]{:S(2)}, u32[]{:S(2)}) collective-permute-start(f32[91,8,128]{2,1,0:T(8,128)S(1)} %shard_map.97.own_head), channel_id=1, source_target_pairs={{4,0},{8,4},{12,8},{16,12},{20,16},{24,20},{28,24},{32,28},{36,32}... | collective-permute-start | bytes 1118216 | tf_op jit(solution)/shard_map/ppermute | solution.py:499
  60.5 0.1 pad_add_fusion.place
  60.6 0.7 shard_map.98
  61.3 1.9 %collective-permute-start.4 = (f32[68,8,128]{2,1,0:T(8,128)S(1)}, f32[68,8,128]{2,1,0:T(8,128)S(1)}, u32[]{:S(2)}, u32[]{:S(2)}) collective-permute-start(f32[68,8,128]{2,1,0:T(8,128)S(1)} %get-tuple-element.24.own_late), channel_id=1, source_target_pairs={{4,0},{8,4},{12,8},{16,12},{20,16},{24,20},{28,24},{32,28},{36,32}... | collective-permute-start | bytes 835592 | tf_op jit(solution)/shard_map/ppermute | solution.py:499
  63.2 3.8 %collective-permute-done.1.next_head = f32[91,8,128]{2,1,0:T(8,128)S(1)} collective-permute-done((f32[91,8,128]{2,1,0:T(8,128)S(1)}, f32[91,8,128]{2,1,0:T(8,128)S(1)}, u32[]{:S(2)}, u32[]{:S(2)}) %collective-permute-start.1) | collective-permute-done | bytes 372768 | tf_op jit(solution)/shard_map/ppermute | solution.py:499
  67.0 1.9 %shard_map.99 = (f32[30,4,8,128]{3,2,1,0:T(8,128)S(1)}, f32[30,4,8,128]{3,2,1,0:T(8,128)S(1)}, f32[16,4,8,128]{3,2,1,0:T(8,128)S(1)}, f32[30,4,8,128]{3,2,1,0:T(8,128)S(1)}, f32[28,8,128]{2,1,0:T(8,128)}) custom-call(f32[91,8,128]{2,1,0:T(8,128)S(1)} %shard_map.97.own_head, f32[68,8,128]{2,1,0:T(8,128)S(1)} %get-tuple-element.24.own_late, ...), custom_call_target="tpu_custom_call" | custom-call | flops 1000000 | bytes 1000000 | tf_op jit(solution)/shard_map/pallas_call | solution.py:486
  68.9 3.0 %collective-permute-start.3 = (f32[28,8,128]{2,1,0:T(8,128)}, f32[28,8,128]{2,1,0:T(8,128)S(1)}, u32[]{:S(2)}, u32[]{:S(2)}) collective-permute-start(f32[28,8,128]{2,1,0:T(8,128)} %get-tuple-element.26.own), channel_id=1, source_target_pairs={{504,0},{508,4},{0,8},{4,12},{8,16},{12,20},{16,24},{20,28},{24,32... | collective-permute-start | bytes 344072 | tf_op jit(solution)/shard_map/ppermute | solution.py:499
  71.9 5.6 %collective-permute-start.2 = (f32[28,8,128]{2,1,0:T(8,128)}, f32[28,8,128]{2,1,0:T(8,128)S(1)}, u32[]{:S(2)}, u32[]{:S(2)}) collective-permute-start(f32[28,8,128]{2,1,0:T(8,128)} %get-tuple-element.26.own), channel_id=1, source_target_pairs={{8,0},{12,4},{16,8},{20,12},{24,16},{28,20},{32,24},{36,28},{40,32... | collective-permute-start | bytes 344072 | tf_op jit(solution)/shard_map/ppermute | solution.py:499
  77.5 1.9 %collective-permute-start.6 = (f32[28,8,128]{2,1,0:T(8,128)}, f32[28,8,128]{2,1,0:T(8,128)S(1)}, u32[]{:S(2)}, u32[]{:S(2)}) collective-permute-start(f32[28,8,128]{2,1,0:T(8,128)} %get-tuple-element.26.own), channel_id=1, source_target_pairs={{4,0},{0,4},{12,8},{8,12},{20,16},{16,20},{28,24},{24,28},{36,32},... | collective-permute-start | bytes 344072 | tf_op jit(solution)/shard_map/ppermute | solution.py:503
  79.4 0.0 collective-permute-done.4.next_late
  79.4 1.4 %shard_map.100 = (f32[4,16,8,128]{3,2,1,0:T(8,128)}, f32[10,4,8,128]{3,2,1,0:T(8,128)S(1)}, f32[10,4,8,128]{3,2,1,0:T(8,128)S(1)}, f32[12,4,8,128]{3,2,1,0:T(8,128)S(1)}) custom-call(s32[2]{0:T(128)S(1)} %pad_add_fusion.place, f32[91,8,128]{2,1,0:T(8,128)S(1)} %shard_map.97.own_head, f32[68,8,128]{2,1,0:T(8,128)S(1)} %get-tuple-element.24.own_late, ...), custom_call_target="tpu_custom_call" | custom-call | flops 1000000 | bytes 1000000 | tf_op jit(solution)/shard_map/pallas_call | solution.py:486
  80.8 0.0 collective-permute-done.3.far_low
  80.8 0.0 collective-permute-done.2.far_high
  80.8 2.4 %collective-permute-start.5 = (f32[28,8,128]{2,1,0:T(8,128)S(1)}, f32[28,8,128]{2,1,0:T(8,128)S(1)}, u32[]{:S(2)}, u32[]{:S(2)}) collective-permute-start(f32[28,8,128]{2,1,0:T(8,128)S(1)} %broadcast_select_fusion), channel_id=1, source_target_pairs={{4,0},{0,4},{12,8},{8,12},{20,16},{16,20},{28,24},{24,28},{36,32},... | collective-permute-start | bytes 344072 | tf_op jit(solution)/shard_map/ppermute | solution.py:503
  83.2 0.0 collective-permute-done.6.first
  83.3 0.9 collective-permute-done.5.second
  84.2 4.2 %shard_map.101 = (f32[30,4,8,128]{3,2,1,0:T(8,128)S(1)}, f32[40,8,128]{2,1,0:T(8,128)S(1)}, f32[40,8,128]{2,1,0:T(8,128)S(1)}, f32[20,8,128]{2,1,0:T(8,128)S(1)}, f32[8,8,128]{2,1,0:T(8,128)S(1)}) custom-call(s32[2]{0:T(128)S(1)} %pad_add_fusion.place, f32[28,8,128]{2,1,0:T(8,128)S(1)} %collective-permute-done.3.far_low, ...), custom_call_target="tpu_custom_call" | custom-call | flops 1000000 | bytes 1000000 | tf_op jit(solution)/shard_map/pallas_call | solution.py:486
  88.4 6.1 %collective-permute-start.8 = (f32[8,8,128]{2,1,0:T(8,128)S(1)}, f32[8,8,128]{2,1,0:T(8,128)S(1)}, u32[]{:S(2)}, u32[]{:S(2)}) collective-permute-start(f32[8,8,128]{2,1,0:T(8,128)S(1)} %get-tuple-element.37.own), channel_id=1, source_target_pairs={{8,0},{12,4},{16,8},{20,12},{24,16},{28,20},{32,24},{36,28},{40,32... | collective-permute-start | bytes 98312 | tf_op jit(solution)/shard_map/ppermute | solution.py:499
  94.5 1.9 %collective-permute-start.7 = (f32[8,8,128]{2,1,0:T(8,128)S(1)}, f32[8,8,128]{2,1,0:T(8,128)S(1)}, u32[]{:S(2)}, u32[]{:S(2)}) collective-permute-start(f32[8,8,128]{2,1,0:T(8,128)S(1)} %get-tuple-element.37.own), channel_id=1, source_target_pairs={{504,0},{508,4},{0,8},{4,12},{8,16},{12,20},{16,24},{20,28},{24,32... | collective-permute-start | bytes 98312 | tf_op jit(solution)/shard_map/ppermute | solution.py:499
  96.5 2.4 %collective-permute-start.10 = (f32[8,8,128]{2,1,0:T(8,128)S(1)}, f32[8,8,128]{2,1,0:T(8,128)S(1)}, u32[]{:S(2)}, u32[]{:S(2)}) collective-permute-start(f32[8,8,128]{2,1,0:T(8,128)S(1)} %get-tuple-element.37.own), channel_id=1, source_target_pairs={{4,0},{0,4},{12,8},{8,12},{20,16},{16,20},{28,24},{24,28},{36,32},... | collective-permute-start | bytes 98312 | tf_op jit(solution)/shard_map/ppermute | solution.py:503
  98.8 0.0 collective-permute-done.8.far_high
  98.8 3.7 %collective-permute-done.7.far_low = f32[8,8,128]{2,1,0:T(8,128)S(1)} collective-permute-done((f32[8,8,128]{2,1,0:T(8,128)S(1)}, f32[8,8,128]{2,1,0:T(8,128)S(1)}, u32[]{:S(2)}, u32[]{:S(2)}) %collective-permute-start.7) | collective-permute-done | bytes 32800 | tf_op jit(solution)/shard_map/ppermute | solution.py:499
  102.5 3.5 %collective-permute-start.9 = (f32[8,8,128]{2,1,0:T(8,128)S(1)}, f32[8,8,128]{2,1,0:T(8,128)S(1)}, u32[]{:S(2)}, u32[]{:S(2)}) collective-permute-start(f32[8,8,128]{2,1,0:T(8,128)S(1)} %broadcast_select_fusion.1), channel_id=1, source_target_pairs={{4,0},{0,4},{12,8},{8,12},{20,16},{16,20},{28,24},{24,28},{36,32},... | collective-permute-start | bytes 98312 | tf_op jit(solution)/shard_map/ppermute | solution.py:503
  106.0 0.0 collective-permute-done.10.first
  106.0 0.8 collective-permute-done.9.second
  106.8 2.9 %shard_map.102 = f32[16,8,128]{2,1,0:T(8,128)} custom-call(s32[2]{0:T(128)S(1)} %pad_add_fusion.place, f32[8,8,128]{2,1,0:T(8,128)S(1)} %collective-permute-done.7.far_low, f32[8,8,128]{2,1,0:T(8,128)S(1)} %collective-permute-done.9.second, f32[8,8,128]{2,1,0:T(8,128)S(1)} %get-tuple-element.37.own, f32[8,8,128]{2,1,0:T(8,128)S(1)} %collective-permute-done.10.first, ...), custom_call_target="tpu_custom_call" | custom-call | flops 1000000 | bytes 1000000 | tf_op jit(solution)/shard_map/pallas_call | solution.py:486
  (5 shorter events, 0.0 us)
Async XLA Ops:
  3.6 36.5 %all-to-all-start = ((f32[128,1,256]{2,1,0:T(1,128)}), f32[128,1,256]{2,1,0:T(1,128)S(1)}, u32[]{:S(2)}, u32[]{:S(2)}) async-start(f32[128,1,256]{2,1,0:T(1,128)} %shard_map.95), calls=%async_computation | async-start | bytes 262144 | tf_op jit(solution)/shard_map/all_to_all | solution.py:529
  24.0 0.8 copy-start.1
  24.8 0.8 slice-start
  25.6 14.5 %copy-start = (f32[16,8,128]{2,1,0:T(8,128)S(1)}, f32[16,8,128]{2,1,0:T(8,128)}, u32[]{:S(2)}) copy-start(f32[16,8,128]{2,1,0:T(8,128)} %rhs.1) | copy-start | bytes 196612
  25.6 14.5 %collective-permute-start = (f32[18,8,128]{2,1,0:T(8,128)S(1)}, f32[18,8,128]{2,1,0:T(8,128)S(1)}, u32[]{:S(2)}, u32[]{:S(2)}) collective-permute-start(f32[18,8,128]{2,1,0:T(8,128)S(1)} %pad_maximum_fusion), channel_id=1, source_target_pairs={{508,0},{0,4},{4,8},{8,12},{12,16},{16,20},{20,24},{24,28},{28,32}... | collective-permute-start | bytes 221192 | tf_op jit(solution)/shard_map/ppermute | solution.py:499
  56.4 10.6 %collective-permute-start.1 = (f32[91,8,128]{2,1,0:T(8,128)S(1)}, f32[91,8,128]{2,1,0:T(8,128)S(1)}, u32[]{:S(2)}, u32[]{:S(2)}) collective-permute-start(f32[91,8,128]{2,1,0:T(8,128)S(1)} %shard_map.97.own_head), channel_id=1, source_target_pairs={{4,0},{8,4},{12,8},{16,12},{20,16},{24,20},{28,24},{32,28},{36,32}... | collective-permute-start | bytes 1118216 | tf_op jit(solution)/shard_map/ppermute | solution.py:499
  61.3 18.1 %collective-permute-start.4 = (f32[68,8,128]{2,1,0:T(8,128)S(1)}, f32[68,8,128]{2,1,0:T(8,128)S(1)}, u32[]{:S(2)}, u32[]{:S(2)}) collective-permute-start(f32[68,8,128]{2,1,0:T(8,128)S(1)} %get-tuple-element.24.own_late), channel_id=1, source_target_pairs={{4,0},{8,4},{12,8},{16,12},{20,16},{24,20},{28,24},{32,28},{36,32}... | collective-permute-start | bytes 835592 | tf_op jit(solution)/shard_map/ppermute | solution.py:499
  68.9 11.9 %collective-permute-start.3 = (f32[28,8,128]{2,1,0:T(8,128)}, f32[28,8,128]{2,1,0:T(8,128)S(1)}, u32[]{:S(2)}, u32[]{:S(2)}) collective-permute-start(f32[28,8,128]{2,1,0:T(8,128)} %get-tuple-element.26.own), channel_id=1, source_target_pairs={{504,0},{508,4},{0,8},{4,12},{8,16},{12,20},{16,24},{20,28},{24,32... | collective-permute-start | bytes 344072 | tf_op jit(solution)/shard_map/ppermute | solution.py:499
  71.9 8.9 %collective-permute-start.2 = (f32[28,8,128]{2,1,0:T(8,128)}, f32[28,8,128]{2,1,0:T(8,128)S(1)}, u32[]{:S(2)}, u32[]{:S(2)}) collective-permute-start(f32[28,8,128]{2,1,0:T(8,128)} %get-tuple-element.26.own), channel_id=1, source_target_pairs={{8,0},{12,4},{16,8},{20,12},{24,16},{28,20},{32,24},{36,28},{40,32... | collective-permute-start | bytes 344072 | tf_op jit(solution)/shard_map/ppermute | solution.py:499
  77.5 5.8 %collective-permute-start.6 = (f32[28,8,128]{2,1,0:T(8,128)}, f32[28,8,128]{2,1,0:T(8,128)S(1)}, u32[]{:S(2)}, u32[]{:S(2)}) collective-permute-start(f32[28,8,128]{2,1,0:T(8,128)} %get-tuple-element.26.own), channel_id=1, source_target_pairs={{4,0},{0,4},{12,8},{8,12},{20,16},{16,20},{28,24},{24,28},{36,32},... | collective-permute-start | bytes 344072 | tf_op jit(solution)/shard_map/ppermute | solution.py:503
  80.8 3.4 %collective-permute-start.5 = (f32[28,8,128]{2,1,0:T(8,128)S(1)}, f32[28,8,128]{2,1,0:T(8,128)S(1)}, u32[]{:S(2)}, u32[]{:S(2)}) collective-permute-start(f32[28,8,128]{2,1,0:T(8,128)S(1)} %broadcast_select_fusion), channel_id=1, source_target_pairs={{4,0},{0,4},{12,8},{8,12},{20,16},{16,20},{28,24},{24,28},{36,32},... | collective-permute-start | bytes 344072 | tf_op jit(solution)/shard_map/ppermute | solution.py:503
  88.4 10.4 %collective-permute-start.8 = (f32[8,8,128]{2,1,0:T(8,128)S(1)}, f32[8,8,128]{2,1,0:T(8,128)S(1)}, u32[]{:S(2)}, u32[]{:S(2)}) collective-permute-start(f32[8,8,128]{2,1,0:T(8,128)S(1)} %get-tuple-element.37.own), channel_id=1, source_target_pairs={{8,0},{12,4},{16,8},{20,12},{24,16},{28,20},{32,24},{36,28},{40,32... | collective-permute-start | bytes 98312 | tf_op jit(solution)/shard_map/ppermute | solution.py:499
  94.5 8.0 %collective-permute-start.7 = (f32[8,8,128]{2,1,0:T(8,128)S(1)}, f32[8,8,128]{2,1,0:T(8,128)S(1)}, u32[]{:S(2)}, u32[]{:S(2)}) collective-permute-start(f32[8,8,128]{2,1,0:T(8,128)S(1)} %get-tuple-element.37.own), channel_id=1, source_target_pairs={{504,0},{508,4},{0,8},{4,12},{8,16},{12,20},{16,24},{20,28},{24,32... | collective-permute-start | bytes 98312 | tf_op jit(solution)/shard_map/ppermute | solution.py:499
  96.5 9.6 %collective-permute-start.10 = (f32[8,8,128]{2,1,0:T(8,128)S(1)}, f32[8,8,128]{2,1,0:T(8,128)S(1)}, u32[]{:S(2)}, u32[]{:S(2)}) collective-permute-start(f32[8,8,128]{2,1,0:T(8,128)S(1)} %get-tuple-element.37.own), channel_id=1, source_target_pairs={{4,0},{0,4},{12,8},{8,12},{20,16},{16,20},{28,24},{24,28},{36,32},... | collective-permute-start | bytes 98312 | tf_op jit(solution)/shard_map/ppermute | solution.py:503
  102.5 4.3 %collective-permute-start.9 = (f32[8,8,128]{2,1,0:T(8,128)S(1)}, f32[8,8,128]{2,1,0:T(8,128)S(1)}, u32[]{:S(2)}, u32[]{:S(2)}) collective-permute-start(f32[8,8,128]{2,1,0:T(8,128)S(1)} %broadcast_select_fusion.1), channel_id=1, source_target_pairs={{4,0},{0,4},{12,8},{8,12},{20,16},{16,20},{28,24},{24,28},{36,32},... | collective-permute-start | bytes 98312 | tf_op jit(solution)/shard_map/ppermute | solution.py:503

commit v5 on v4

--- a/solution.py
+++ b/solution.py
@@ -426,22 +426,22 @@
             send[24 + k // 2] = jnp.where(lane < 32, 0.0625 * (OMEGA * take(opened, even) / low), 0.0)
 
 
-def window(core, far_low, second, own, first, far_high):
-    even = core == 0
+def window(place, low_pair, second, own, first, high_pair):
+    even_core, even_chip = place[1] == 0, place[2] == 0
 
     def part(n, k):
-        if n == 1:
-            return jnp.where(even, second[k], first[k])
-        if n == 3:
-            return jnp.where(even, first[k], second[k])
-        return (far_low, None, own, None, far_high)[n][k]
+        if n == 2:
+            return own[k]
+        if n in (1, 3):
+            return jnp.where(even_core == (n == 1), second[k], first[k])
+        return jnp.where(even_chip == (n == 0), low_pair[k], high_pair[k])
 
     return part
 
 
-def middle_kernel(place, far_low, second, own, first, far_high, cc, cb, gg, v2, cc_r, cb_r, v2_r, v_out, c1, g1, c2, send,
+def middle_kernel(place, low_pair, second, own, first, high_pair, cc, cb, gg, v2, cc_r, cb_r, v2_r, v_out, c1, g1, c2, send,
                   cb1, w_a, w_b, cb2, u_a, u_b, v_a, v_b):
-    part = window(place[1], far_low, second, own, first, far_high)
+    part = window(place, low_pair, second, own, first, high_pair)
     for n in range(5):
         for k in range(8):
             cb1[8 * n + k] = part(n, k)
@@ -460,9 +460,9 @@
         send[k] = 4.0 * c1[16 + k] * fine_residue(v_out, cc, cb, gg, k)
 
 
-def last_kernel(place, far_low, second, own, first, far_high, cc, cb, v2, c1, g1, c2, out,
+def last_kernel(place, low_pair, second, own, first, high_pair, cc, cb, v2, c1, g1, c2, out,
                 cb1, w_a, w_b, cb2, u_a, u_b, v_a, v_b, flat):
-    part = window(place[1], far_low, second, own, first, far_high)
+    part = window(place, low_pair, second, own, first, high_pair)
     for n in range(5):
         for k in range(8):
             cb1[8 * n + k] = part(n, k)
@@ -503,18 +503,24 @@
     return lax.ppermute(block, "box", [(i ^ 1, i) for i in range(lax.axis_size("box"))])
 
 
-def around(block, core, beside=None):
-    far_low, far_high = fetch(block, -2), fetch(block, 2)
+def meet(block, odd):
+    count = lax.axis_size("box")
+    chips = [((k + odd ^ 1) - odd) % (count // 2) for k in range(count // 2)]
+    return lax.ppermute(block, "box", [(2 * chips[i // 2] + i % 2, i) for i in range(count)])
+
+
+def around(block, place, beside=None):
+    low_pair, high_pair = meet(block, 1), meet(block, 0)
     first = swap(block)
-    onward = jnp.where(core == 0, far_high, far_low)
+    onward = jnp.where(place[1] == place[2], high_pair, low_pair)
     if beside is not None:
         onward, beside = lax.optimization_barrier((onward, beside))
-    return [far_low, swap(onward), block, first, far_high], beside
+    return [low_pair, swap(onward), block, first, high_pair], beside
 
 
 def shards(volume, drag, momentum, offsets, cell_index, destinations, rhs, wall):
-    core = lax.axis_index("box").astype(I32) % 2
-    place = jnp.stack([lax.axis_index("slab").astype(I32), core])
+    box = lax.axis_index("box").astype(I32)
+    place = jnp.stack([lax.axis_index("slab").astype(I32), box % 2, box // 2 % 2])
     prev = fetch(jnp.concatenate([rhs[7:], wall[7:].astype(F32)], axis=0), -1)
     one = (1, PART)
     (outgoing,) = call(
@@ -554,7 +560,7 @@
         smem_first=True,
     )
     scratch = [(mid, F32), (mid, F32), (mid, F32), (low, F32), (low, F32), (low, F32), (fine, F32), (fine, F32)]
-    parts, coupled = around(first, core, coupled)
+    parts, coupled = around(first, place, coupled)
     v3, c1, g1, c2, second = call(
         middle_kernel,
         [fine, mid, mid, low, (8, 8, NZ)],
@@ -562,7 +568,7 @@
         [place] + parts + [cc, cb, gg, v2, cc_r, cb_r, v2_r],
         smem_first=True,
     )
-    parts, _ = around(second, core)
+    parts, _ = around(second, place)
     (pressure,) = call(
         last_kernel,
         [(CX, 8, NZ)],

time: 110 us -> 106 us (0.964)
  starting transfers between devices: 56.9 us -> 54 us
  waiting for transfers between devices: 20 us -> 18.9 us
    ppermute x7 -> x3, starting transfers between devices: 26.3 us -> 9.71 us  [fetch(): lax.ppermute(block, 'box', [((i + distance) % count, i) for i in range(co...]
    ppermute x0 -> x4, starting transfers between devices: none -> 13.5 us  [meet(): lax.ppermute(block, 'box', [(2 * chips[i // 2] + i % 2, i) for i in range...]
    ppermute x7 -> x3, waiting for transfers between devices: 7.49 us -> 3.77 us  [fetch(): lax.ppermute(block, 'box', [((i + distance) % count, i) for i in range(co...]
    ppermute x0 -> x4, waiting for transfers between devices: none -> 2.31 us  [meet(): lax.ppermute(block, 'box', [(2 * chips[i // 2] + i % 2, i) for i in range...]
  transfers between devices with their start and end apart: 12 -> 12, of which waited for: 5 -> 6; matrix products, arithmetic and copies ran while one was open for 0% -> 0% of each run, Pallas kernels for 4% -> 4%
where the time goes in v5:
time: 106 us
  starting transfers between devices  54 us (51%)
  waiting for transfers between devices  18.9 us (18%)
  Pallas kernels  16.9 us (16%)
  blocking collectives  13.4 us (13%)
  local copies, waits for them, and re-layouts  1.61 us (2%)
    all_to_all x1, starting transfers between devices, shards(): lax.all_to_all(outgoing, 'box', split_axis=0, concat_axis=0, tiled=True)  20.4 us
    pallas_call x8, Pallas kernels, call(): pl.pallas_call(kernel, out_shape=shapes, in_specs=specs, out_specs=[pl.Bl...  16.9 us
    ppermute x4, starting transfers between devices, meet(): lax.ppermute(block, 'box', [(2 * chips[i // 2] + i % 2, i) for i in range...  13.5 us
    all_gather x1, blocking collectives, shards(): slabs = lax.all_gather(pay, 'slab')  13.4 us
    all_to_all x1, waiting for transfers between devices, shards(): lax.all_to_all(outgoing, 'box', split_axis=0, concat_axis=0, tiled=True)  10.8 us
    ppermute x4, starting transfers between devices, swap(): lax.ppermute(block, 'box', [(i ^ 1, i) for i in range(lax.axis_size('box'...  10.4 us
    ppermute x3, starting transfers between devices, fetch(): lax.ppermute(block, 'box', [((i + distance) % count, i) for i in range(co...  9.71 us
    ppermute x3, waiting for transfers between devices, fetch(): lax.ppermute(block, 'box', [((i + distance) % count, i) for i in range(co...  3.77 us
  transfers between devices with their start and end apart: 12, of which 6 were waited for; matrix products, arithmetic and copies ran while one was open for 0% of the time, Pallas kernels for 4%

profile of v5, /device:TPU:1, one launch (start us, length us, event | category | flops | bytes accessed | tf_op | source)
XLA Modules:
  0.0 105.8 jit_solution(9248269736134643232)
XLA Ops:
  0.6 2.9 %shard_map.95 = f32[128,1,256]{2,1,0:T(1,128)} custom-call(f32[1,2048]{1,0:T(1,128)} %bitcast.14, f32[1,2048]{1,0:T(1,128)} %bitcast.15, f32[2,2048]{1,0:T(2,128)} %mom_in.1, f32[3,2048]{1,0:T(4,128)} %off_in.1, s32[1,2048]{1,0:T(1,128)} %bitcast.16, s32[1,2048]{1,0:T(1,128)} %bitcast.17), custom_call_target="tpu_custom_call" | custom-call | flops 1000000 | bytes 1000000 | tf_op jit(solution)/shard_map/pallas_call | solution.py:486
  3.6 20.4 %all-to-all-start = ((f32[128,1,256]{2,1,0:T(1,128)}), f32[128,1,256]{2,1,0:T(1,128)S(1)}, u32[]{:S(2)}, u32[]{:S(2)}) async-start(f32[128,1,256]{2,1,0:T(1,128)} %shard_map.95), calls=%async_computation | async-start | bytes 262144 | tf_op jit(solution)/shard_map/all_to_all | solution.py:535
  24.0 0.0 copy-start.1
  24.0 0.8 copy-done.1
  24.8 0.0 slice-start
  24.8 0.8 slice-done
  25.6 0.0 copy-start
  25.6 3.7 %collective-permute-start = (f32[18,8,128]{2,1,0:T(8,128)S(1)}, f32[18,8,128]{2,1,0:T(8,128)S(1)}, u32[]{:S(2)}, u32[]{:S(2)}) collective-permute-start(f32[18,8,128]{2,1,0:T(8,128)S(1)} %pad_maximum_fusion), channel_id=1, source_target_pairs={{508,0},{0,4},{4,8},{8,12},{12,16},{16,20},{20,24},{24,28},{28,32}... | collective-permute-start | bytes 221192 | tf_op jit(solution)/shard_map/ppermute | solution.py:499
  29.3 10.8 %all-to-all-done = f32[128,1,256]{2,1,0:T(1,128)S(1)} async-done(((f32[128,1,256]{2,1,0:T(1,128)}), f32[128,1,256]{2,1,0:T(1,128)S(1)}, u32[]{:S(2)}, u32[]{:S(2)}) %all-to-all-start) | async-done | bytes 131104 | tf_op jit(solution)/shard_map/all_to_all | solution.py:535
  40.1 0.0 collective-permute-done.prev
  40.1 0.0 copy-done
  40.1 2.7 %shard_map.96 = (f32[63,8,128]{2,1,0:T(8,128)S(1)}, f32[3,18,8,128]{3,2,1,0:T(8,128)S(1)}) custom-call(f32[128,256]{1,0:T(8,128)S(1)} %bitcast.13, f32[16,8,128]{2,1,0:T(8,128)S(1)} %copy-done, s32[16,8,128]{2,1,0:T(8,128)S(1)} %copy-done.1, f32[18,8,128]{2,1,0:T(8,128)S(1)} %collective-permute-done.prev), custom_call_target="tpu_custom_call" | custom-call | flops 1000000 | bytes 1000000 | tf_op jit(solution)/shard_map/pallas_call | solution.py:486
  42.8 13.4 %all-gather = f32[252,8,128]{2,1,0:T(8,128)S(1)} all-gather(f32[63,8,128]{2,1,0:T(8,128)S(1)} %get-tuple-element.22), channel_id=2, replica_groups=mesh['box'=128,'slab'=4] {'slab'}, dimensions={0}, use_global_device_ids=true | all-gather | bytes 1290240 | tf_op jit(solution)/shard_map/all_gather | solution.py:543
  56.2 0.2 shard_map.97.own_head
  56.4 4.1 %collective-permute-start.1 = (f32[91,8,128]{2,1,0:T(8,128)S(1)}, f32[91,8,128]{2,1,0:T(8,128)S(1)}, u32[]{:S(2)}, u32[]{:S(2)}) collective-permute-start(f32[91,8,128]{2,1,0:T(8,128)S(1)} %shard_map.97.own_head), channel_id=1, source_target_pairs={{4,0},{8,4},{12,8},{16,12},{20,16},{24,20},{28,24},{32,28},{36,32}... | collective-permute-start | bytes 1118216 | tf_op jit(solution)/shard_map/ppermute | solution.py:499
  60.5 0.1 pad_add_fusion.place
  60.6 0.7 shard_map.98
  61.3 1.9 %collective-permute-start.4 = (f32[68,8,128]{2,1,0:T(8,128)S(1)}, f32[68,8,128]{2,1,0:T(8,128)S(1)}, u32[]{:S(2)}, u32[]{:S(2)}) collective-permute-start(f32[68,8,128]{2,1,0:T(8,128)S(1)} %get-tuple-element.24.own_late), channel_id=1, source_target_pairs={{4,0},{8,4},{12,8},{16,12},{20,16},{24,20},{28,24},{32,28},{36,32}... | collective-permute-start | bytes 835592 | tf_op jit(solution)/shard_map/ppermute | solution.py:499
  63.2 3.8 %collective-permute-done.1.next_head = f32[91,8,128]{2,1,0:T(8,128)S(1)} collective-permute-done((f32[91,8,128]{2,1,0:T(8,128)S(1)}, f32[91,8,128]{2,1,0:T(8,128)S(1)}, u32[]{:S(2)}, u32[]{:S(2)}) %collective-permute-start.1) | collective-permute-done | bytes 372768 | tf_op jit(solution)/shard_map/ppermute | solution.py:499
  67.0 1.9 %shard_map.99 = (f32[30,4,8,128]{3,2,1,0:T(8,128)S(1)}, f32[30,4,8,128]{3,2,1,0:T(8,128)S(1)}, f32[16,4,8,128]{3,2,1,0:T(8,128)S(1)}, f32[30,4,8,128]{3,2,1,0:T(8,128)S(1)}, f32[28,8,128]{2,1,0:T(8,128)}) custom-call(f32[91,8,128]{2,1,0:T(8,128)S(1)} %shard_map.97.own_head, f32[68,8,128]{2,1,0:T(8,128)S(1)} %get-tuple-element.24.own_late, ...), custom_call_target="tpu_custom_call" | custom-call | flops 1000000 | bytes 1000000 | tf_op jit(solution)/shard_map/pallas_call | solution.py:486
  68.9 5.3 %collective-permute-start.3 = (f32[28,8,128]{2,1,0:T(8,128)}, f32[28,8,128]{2,1,0:T(8,128)S(1)}, u32[]{:S(2)}, u32[]{:S(2)}) collective-permute-start(f32[28,8,128]{2,1,0:T(8,128)} %get-tuple-element.26.own), channel_id=1, source_target_pairs={{504,0},{508,4},{16,8},{20,12},{8,16},{12,20},{32,24},{36,28},{24,... | collective-permute-start | bytes 344072 | tf_op jit(solution)/shard_map/ppermute | solution.py:509
  74.2 1.9 %collective-permute-start.2 = (f32[28,8,128]{2,1,0:T(8,128)}, f32[28,8,128]{2,1,0:T(8,128)S(1)}, u32[]{:S(2)}, u32[]{:S(2)}) collective-permute-start(f32[28,8,128]{2,1,0:T(8,128)} %get-tuple-element.26.own), channel_id=1, source_target_pairs={{8,0},{12,4},{0,8},{4,12},{24,16},{28,20},{16,24},{20,28},{40,32},... | collective-permute-start | bytes 344072 | tf_op jit(solution)/shard_map/ppermute | solution.py:509
  76.1 1.9 %collective-permute-start.6 = (f32[28,8,128]{2,1,0:T(8,128)}, f32[28,8,128]{2,1,0:T(8,128)S(1)}, u32[]{:S(2)}, u32[]{:S(2)}) collective-permute-start(f32[28,8,128]{2,1,0:T(8,128)} %get-tuple-element.26.own), channel_id=1, source_target_pairs={{4,0},{0,4},{12,8},{8,12},{20,16},{16,20},{28,24},{24,28},{36,32},... | collective-permute-start | bytes 344072 | tf_op jit(solution)/shard_map/ppermute | solution.py:503
  78.0 0.0 collective-permute-done.4.next_late
  78.0 1.4 %shard_map.100 = (f32[4,16,8,128]{3,2,1,0:T(8,128)}, f32[10,4,8,128]{3,2,1,0:T(8,128)S(1)}, f32[10,4,8,128]{3,2,1,0:T(8,128)S(1)}, f32[12,4,8,128]{3,2,1,0:T(8,128)S(1)}) custom-call(s32[3]{0:T(128)S(1)} %pad_add_fusion.place, f32[91,8,128]{2,1,0:T(8,128)S(1)} %shard_map.97.own_head, f32[68,8,128]{2,1,0:T(8,128)S(1)} %get-tuple-element.24.own_late, ...), custom_call_target="tpu_custom_call" | custom-call | flops 1000000 | bytes 1000000 | tf_op jit(solution)/shard_map/pallas_call | solution.py:486
  79.4 0.0 collective-permute-done.3.low_pair
  79.4 0.5 collective-permute-done.2.high_pair
  79.9 1.9 %collective-permute-start.5 = (f32[28,8,128]{2,1,0:T(8,128)S(1)}, f32[28,8,128]{2,1,0:T(8,128)S(1)}, u32[]{:S(2)}, u32[]{:S(2)}) collective-permute-start(f32[28,8,128]{2,1,0:T(8,128)S(1)} %broadcast_select_fusion), channel_id=1, source_target_pairs={{4,0},{0,4},{12,8},{8,12},{20,16},{16,20},{28,24},{24,28},{36,32},... | collective-permute-start | bytes 344072 | tf_op jit(solution)/shard_map/ppermute | solution.py:503
  81.9 0.0 collective-permute-done.6.first
  81.9 1.3 %collective-permute-done.5.second = f32[28,8,128]{2,1,0:T(8,128)S(1)} collective-permute-done((f32[28,8,128]{2,1,0:T(8,128)S(1)}, f32[28,8,128]{2,1,0:T(8,128)S(1)}, u32[]{:S(2)}, u32[]{:S(2)}) %collective-permute-start.5) | collective-permute-done | bytes 114720 | tf_op jit(solution)/shard_map/ppermute | solution.py:503
  83.1 4.2 %shard_map.101 = (f32[30,4,8,128]{3,2,1,0:T(8,128)S(1)}, f32[40,8,128]{2,1,0:T(8,128)S(1)}, f32[40,8,128]{2,1,0:T(8,128)S(1)}, f32[20,8,128]{2,1,0:T(8,128)S(1)}, f32[8,8,128]{2,1,0:T(8,128)S(1)}) custom-call(s32[3]{0:T(128)S(1)} %pad_add_fusion.place, f32[28,8,128]{2,1,0:T(8,128)S(1)} %collective-permute-done.3.low_pair, ...), custom_call_target="tpu_custom_call" | custom-call | flops 1000000 | bytes 1000000 | tf_op jit(solution)/shard_map/pallas_call | solution.py:486
  87.3 3.0 %collective-permute-start.8 = (f32[8,8,128]{2,1,0:T(8,128)S(1)}, f32[8,8,128]{2,1,0:T(8,128)S(1)}, u32[]{:S(2)}, u32[]{:S(2)}) collective-permute-start(f32[8,8,128]{2,1,0:T(8,128)S(1)} %get-tuple-element.37.own), channel_id=1, source_target_pairs={{8,0},{12,4},{0,8},{4,12},{24,16},{28,20},{16,24},{20,28},{40,32},... | collective-permute-start | bytes 98312 | tf_op jit(solution)/shard_map/ppermute | solution.py:509
  90.4 3.3 %collective-permute-start.7 = (f32[8,8,128]{2,1,0:T(8,128)S(1)}, f32[8,8,128]{2,1,0:T(8,128)S(1)}, u32[]{:S(2)}, u32[]{:S(2)}) collective-permute-start(f32[8,8,128]{2,1,0:T(8,128)S(1)} %get-tuple-element.37.own), channel_id=1, source_target_pairs={{504,0},{508,4},{16,8},{20,12},{8,16},{12,20},{32,24},{36,28},{24,... | collective-permute-start | bytes 98312 | tf_op jit(solution)/shard_map/ppermute | solution.py:509
  93.7 2.8 %collective-permute-start.10 = (f32[8,8,128]{2,1,0:T(8,128)S(1)}, f32[8,8,128]{2,1,0:T(8,128)S(1)}, u32[]{:S(2)}, u32[]{:S(2)}) collective-permute-start(f32[8,8,128]{2,1,0:T(8,128)S(1)} %get-tuple-element.37.own), channel_id=1, source_target_pairs={{4,0},{0,4},{12,8},{8,12},{20,16},{16,20},{28,24},{24,28},{36,32},... | collective-permute-start | bytes 98312 | tf_op jit(solution)/shard_map/ppermute | solution.py:503
  96.5 0.0 collective-permute-done.8.high_pair
  96.5 1.8 %collective-permute-done.7.low_pair = f32[8,8,128]{2,1,0:T(8,128)S(1)} collective-permute-done((f32[8,8,128]{2,1,0:T(8,128)S(1)}, f32[8,8,128]{2,1,0:T(8,128)S(1)}, u32[]{:S(2)}, u32[]{:S(2)}) %collective-permute-start.7) | collective-permute-done | bytes 32800 | tf_op jit(solution)/shard_map/ppermute | solution.py:509
  98.4 3.7 %collective-permute-start.9 = (f32[8,8,128]{2,1,0:T(8,128)S(1)}, f32[8,8,128]{2,1,0:T(8,128)S(1)}, u32[]{:S(2)}, u32[]{:S(2)}) collective-permute-start(f32[8,8,128]{2,1,0:T(8,128)S(1)} %broadcast_select_fusion.1), channel_id=1, source_target_pairs={{4,0},{0,4},{12,8},{8,12},{20,16},{16,20},{28,24},{24,28},{36,32},... | collective-permute-start | bytes 98312 | tf_op jit(solution)/shard_map/ppermute | solution.py:503
  102.1 0.0 collective-permute-done.10.first
  102.1 0.8 collective-permute-done.9.second
  102.9 2.9 %shard_map.102 = f32[16,8,128]{2,1,0:T(8,128)} custom-call(s32[3]{0:T(128)S(1)} %pad_add_fusion.place, f32[8,8,128]{2,1,0:T(8,128)S(1)} %collective-permute-done.7.low_pair, f32[8,8,128]{2,1,0:T(8,128)S(1)} %collective-permute-done.9.second, f32[8,8,128]{2,1,0:T(8,128)S(1)} %get-tuple-element.37.own, f32[8,8,128]{2,1,0:T(8,128)S(1)} %collective-permute-done.10.first, ...), custom_call_target="tpu_custom_call" | custom-call | flops 1000000 | bytes 1000000 | tf_op jit(solution)/shard_map/pallas_call | solution.py:486
  (5 shorter events, 0.0 us)
Async XLA Ops:
  3.6 36.5 %all-to-all-start = ((f32[128,1,256]{2,1,0:T(1,128)}), f32[128,1,256]{2,1,0:T(1,128)S(1)}, u32[]{:S(2)}, u32[]{:S(2)}) async-start(f32[128,1,256]{2,1,0:T(1,128)} %shard_map.95), calls=%async_computation | async-start | bytes 262144 | tf_op jit(solution)/shard_map/all_to_all | solution.py:535
  24.0 0.8 copy-start.1
  24.8 0.8 slice-start
  25.6 14.5 %copy-start = (f32[16,8,128]{2,1,0:T(8,128)S(1)}, f32[16,8,128]{2,1,0:T(8,128)}, u32[]{:S(2)}) copy-start(f32[16,8,128]{2,1,0:T(8,128)} %rhs.1) | copy-start | bytes 196612
  25.6 14.5 %collective-permute-start = (f32[18,8,128]{2,1,0:T(8,128)S(1)}, f32[18,8,128]{2,1,0:T(8,128)S(1)}, u32[]{:S(2)}, u32[]{:S(2)}) collective-permute-start(f32[18,8,128]{2,1,0:T(8,128)S(1)} %pad_maximum_fusion), channel_id=1, source_target_pairs={{508,0},{0,4},{4,8},{8,12},{12,16},{16,20},{20,24},{24,28},{28,32}... | collective-permute-start | bytes 221192 | tf_op jit(solution)/shard_map/ppermute | solution.py:499
  56.4 10.6 %collective-permute-start.1 = (f32[91,8,128]{2,1,0:T(8,128)S(1)}, f32[91,8,128]{2,1,0:T(8,128)S(1)}, u32[]{:S(2)}, u32[]{:S(2)}) collective-permute-start(f32[91,8,128]{2,1,0:T(8,128)S(1)} %shard_map.97.own_head), channel_id=1, source_target_pairs={{4,0},{8,4},{12,8},{16,12},{20,16},{24,20},{28,24},{32,28},{36,32}... | collective-permute-start | bytes 1118216 | tf_op jit(solution)/shard_map/ppermute | solution.py:499
  61.3 16.7 %collective-permute-start.4 = (f32[68,8,128]{2,1,0:T(8,128)S(1)}, f32[68,8,128]{2,1,0:T(8,128)S(1)}, u32[]{:S(2)}, u32[]{:S(2)}) collective-permute-start(f32[68,8,128]{2,1,0:T(8,128)S(1)} %get-tuple-element.24.own_late), channel_id=1, source_target_pairs={{4,0},{8,4},{12,8},{16,12},{20,16},{24,20},{28,24},{32,28},{36,32}... | collective-permute-start | bytes 835592 | tf_op jit(solution)/shard_map/ppermute | solution.py:499
  68.9 10.6 %collective-permute-start.3 = (f32[28,8,128]{2,1,0:T(8,128)}, f32[28,8,128]{2,1,0:T(8,128)S(1)}, u32[]{:S(2)}, u32[]{:S(2)}) collective-permute-start(f32[28,8,128]{2,1,0:T(8,128)} %get-tuple-element.26.own), channel_id=1, source_target_pairs={{504,0},{508,4},{16,8},{20,12},{8,16},{12,20},{32,24},{36,28},{24,... | collective-permute-start | bytes 344072 | tf_op jit(solution)/shard_map/ppermute | solution.py:509
  74.2 5.7 %collective-permute-start.2 = (f32[28,8,128]{2,1,0:T(8,128)}, f32[28,8,128]{2,1,0:T(8,128)S(1)}, u32[]{:S(2)}, u32[]{:S(2)}) collective-permute-start(f32[28,8,128]{2,1,0:T(8,128)} %get-tuple-element.26.own), channel_id=1, source_target_pairs={{8,0},{12,4},{0,8},{4,12},{24,16},{28,20},{16,24},{20,28},{40,32},... | collective-permute-start | bytes 344072 | tf_op jit(solution)/shard_map/ppermute | solution.py:509
  76.1 5.8 %collective-permute-start.6 = (f32[28,8,128]{2,1,0:T(8,128)}, f32[28,8,128]{2,1,0:T(8,128)S(1)}, u32[]{:S(2)}, u32[]{:S(2)}) collective-permute-start(f32[28,8,128]{2,1,0:T(8,128)} %get-tuple-element.26.own), channel_id=1, source_target_pairs={{4,0},{0,4},{12,8},{8,12},{20,16},{16,20},{28,24},{24,28},{36,32},... | collective-permute-start | bytes 344072 | tf_op jit(solution)/shard_map/ppermute | solution.py:503
  79.9 3.2 %collective-permute-start.5 = (f32[28,8,128]{2,1,0:T(8,128)S(1)}, f32[28,8,128]{2,1,0:T(8,128)S(1)}, u32[]{:S(2)}, u32[]{:S(2)}) collective-permute-start(f32[28,8,128]{2,1,0:T(8,128)S(1)} %broadcast_select_fusion), channel_id=1, source_target_pairs={{4,0},{0,4},{12,8},{8,12},{20,16},{16,20},{28,24},{24,28},{36,32},... | collective-permute-start | bytes 344072 | tf_op jit(solution)/shard_map/ppermute | solution.py:503
  87.3 9.2 %collective-permute-start.8 = (f32[8,8,128]{2,1,0:T(8,128)S(1)}, f32[8,8,128]{2,1,0:T(8,128)S(1)}, u32[]{:S(2)}, u32[]{:S(2)}) collective-permute-start(f32[8,8,128]{2,1,0:T(8,128)S(1)} %get-tuple-element.37.own), channel_id=1, source_target_pairs={{8,0},{12,4},{0,8},{4,12},{24,16},{28,20},{16,24},{20,28},{40,32},... | collective-permute-start | bytes 98312 | tf_op jit(solution)/shard_map/ppermute | solution.py:509
  90.4 8.0 %collective-permute-start.7 = (f32[8,8,128]{2,1,0:T(8,128)S(1)}, f32[8,8,128]{2,1,0:T(8,128)S(1)}, u32[]{:S(2)}, u32[]{:S(2)}) collective-permute-start(f32[8,8,128]{2,1,0:T(8,128)S(1)} %get-tuple-element.37.own), channel_id=1, source_target_pairs={{504,0},{508,4},{16,8},{20,12},{8,16},{12,20},{32,24},{36,28},{24,... | collective-permute-start | bytes 98312 | tf_op jit(solution)/shard_map/ppermute | solution.py:509
  93.7 8.4 %collective-permute-start.10 = (f32[8,8,128]{2,1,0:T(8,128)S(1)}, f32[8,8,128]{2,1,0:T(8,128)S(1)}, u32[]{:S(2)}, u32[]{:S(2)}) collective-permute-start(f32[8,8,128]{2,1,0:T(8,128)S(1)} %get-tuple-element.37.own), channel_id=1, source_target_pairs={{4,0},{0,4},{12,8},{8,12},{20,16},{16,20},{28,24},{24,28},{36,32},... | collective-permute-start | bytes 98312 | tf_op jit(solution)/shard_map/ppermute | solution.py:503
  98.4 4.5 %collective-permute-start.9 = (f32[8,8,128]{2,1,0:T(8,128)S(1)}, f32[8,8,128]{2,1,0:T(8,128)S(1)}, u32[]{:S(2)}, u32[]{:S(2)}) collective-permute-start(f32[8,8,128]{2,1,0:T(8,128)S(1)} %broadcast_select_fusion.1), channel_id=1, source_target_pairs={{4,0},{0,4},{12,8},{8,12},{20,16},{16,20},{28,24},{24,28},{36,32},... | collective-permute-start | bytes 98312 | tf_op jit(solution)/shard_map/ppermute | solution.py:503

commit v6 on v5

--- a/solution.py
+++ b/solution.py
@@ -241,7 +241,7 @@
 
     def coefficient(self, t, q):
         diag = 6.0 + self.joined(t, 1, q)
-        coef = OMEGA * self.opened((t + 1) // 4) / diag
+        coef = OMEGA * self.opened((t + 1) // 4) * pl.reciprocal(diag)
         return coef, coef * self.joined(t, 0, q), diag
 
 
@@ -270,10 +270,6 @@
 
 def take(tile, index):
     return jnp.take_along_axis(tile, index, axis=1)
-
-
-def pair_lanes(tile):
-    return tile + pltpu.roll(tile, NZ - 1, 1)
 
 
 def fine_sums(ref, t):
@@ -296,21 +292,37 @@
             dst[t, q] = (1.0 - OMEGA) * cur[q] + base[t, q] + coef[t, q] * sums[q]
 
 
-def fine_residue(src, coef, base, weight, k):
-    total = [0.0, 0.0]
-    for dx in range(2):
-        t = 7 + 2 * k + dx
-        cur, sums = fine_sums(src, t)
-        for q in range(4):
-            tile = weight[2 * k + dx, q] * (base[t, q] + coef[t, q] * sums[q] - OMEGA * cur[q])
-            total[q // 2] = total[q // 2] + tile
-    return 0.125 * pack(total)
-
-
-def pack(total):
-    lane = lane_index()
-    even = (2 * lane) % NZ
-    return jnp.where(lane < 64, take(pair_lanes(total[0]), even), take(pair_lanes(total[1]), even))
+def fine_residue(src, coef, base, weight):
+    rows = []
+    for k in range(8):
+        total = [0.0, 0.0]
+        for dx in range(2):
+            t = 7 + 2 * k + dx
+            cur, sums = fine_sums(src, t)
+            for q in range(4):
+                tile = weight[2 * k + dx, q] * (base[t, q] + coef[t, q] * sums[q] - OMEGA * cur[q])
+                total[q // 2] = total[q // 2] + tile
+        rows.append(jnp.concatenate(total, axis=1))
+    return jnp.concatenate(rows, axis=0)
+
+
+def choice(size, match):
+    row = lax.broadcasted_iota(I32, (size, NZ), 0)
+    column = lax.broadcasted_iota(I32, (size, NZ), 1)
+    return jnp.where(match(row, column), 1.0, 0.0).astype(BF16)
+
+
+def lane_sums(block, chosen):
+    out, left = 0.0, block
+    for _ in range(3):
+        part = left.astype(BF16)
+        out = out + jnp.dot(part, chosen, preferred_element_type=F32)
+        left = left - part.astype(F32)
+    return out
+
+
+def pairs_packed():
+    return choice(256, lambda r, c: r // 2 == c)
 
 
 def fine_correct(v_in, v_out, w, coef, low, high):
@@ -350,15 +362,17 @@
 
 def levels_solve(c1, g1, c2, cb1, w_a, w_b, cb2, u_a, u_b):
     lane = lane_index()
-    even = (2 * lane) % NZ
     mid_sweep(cb1, w_a, c1, cb1, 3, 37)
+    totals = []
     for m in range(2, 18):
         total = 0.0
         for a in (2 * m, 2 * m + 1):
             cur, beside = mid_sums(w_a, a)
             total = total + g1[a] * (cb1[a] + c1[a] * beside - OMEGA * cur)
-        total = total + pltpu.roll(total, 64, 1)
-        cb2[m] = 2.0 * c2[m] * take(pair_lanes(total), even)
+        totals.append(total)
+    below = lane_sums(jnp.concatenate(totals, axis=0), choice(NZ, lambda r, c: r % 64 // 2 == c))
+    for m in range(2, 18):
+        cb2[m] = 2.0 * c2[m] * below[8 * (m - 2) : 8 * (m - 1)]
     low_sweep(cb2, u_a, c2, cb2, 3, 17)
     low_sweep(u_a, u_b, c2, cb2, 4, 16)
     low_sweep(u_b, u_a, c2, cb2, 5, 15)
@@ -403,30 +417,36 @@
             if 7 <= t < 23:
                 gg[t - 7, q] = (1.0 / OMEGA) * diag
     fine_sweep(cb, v2, cc, cb, 6, 24)
-    lane = lane_index()
-    even = (2 * lane) % NZ
+    damps = []
     for k in range(8):
-        opened = take(parts.opened(2 + k // 2), even)
-        d_sum = [0.0, 0.0]
+        total = [0.0, 0.0]
         for dx in range(2):
             for q in range(4):
-                d_sum[q // 2] = d_sum[q // 2] + parts.joined(7 + 2 * k + dx, 1, q)
-        damp = 0.125 * pack(d_sum)
-        diag = 1.5 + damp
-        coef = OMEGA * opened / diag
-        send[k] = coef * fine_residue(v2, cc, cb, gg, k)
+                total[q // 2] = total[q // 2] + parts.joined(7 + 2 * k + dx, 1, q)
+        damps.append(jnp.concatenate(total, axis=1))
+    lows = [damps[2 * m] + damps[2 * m + 1] for m in range(4)]
+    opened = jnp.concatenate([parts.opened(2 + m) for m in range(4)], axis=0).astype(BF16)
+    opened_1 = jnp.dot(opened, choice(NZ, lambda r, c: r == c % 64 * 2), preferred_element_type=F32)
+    opened_2 = jnp.dot(opened, choice(NZ, lambda r, c: r == c * 4), preferred_element_type=F32)
+    packed = pairs_packed()
+    diag = 1.5 + 0.125 * lane_sums(jnp.concatenate(damps, axis=0), packed)
+    low_diag = 0.375 + 0.015625 * lane_sums(
+        jnp.concatenate(lows, axis=0), choice(256, lambda r, c: r % NZ // 4 == c)
+    )
+    source = 0.125 * lane_sums(fine_residue(v2, cc, cb, gg), packed)
+    inverse = OMEGA * pl.reciprocal(diag)
+    below = (0.0625 * OMEGA) * opened_2 * pl.reciprocal(low_diag)
+    for k in range(8):
+        rows = slice(8 * k, 8 * k + 8)
+        coef = opened_1[8 * (k // 2) : 8 * (k // 2) + 8] * inverse[rows]
+        send[k] = coef * source[rows]
         send[8 + k] = 0.25 * coef
-        send[16 + k] = (1.0 / OMEGA) * diag
-        if k % 2 == 0:
-            above = damp
-        else:
-            total = above + damp
-            total = total + pltpu.roll(total, 64, 1)
-            low = 0.375 + 0.125 * take(pair_lanes(total), even)
-            send[24 + k // 2] = jnp.where(lane < 32, 0.0625 * (OMEGA * take(opened, even) / low), 0.0)
-
-
-def window(place, low_pair, second, own, first, high_pair):
+        send[16 + k] = (1.0 / OMEGA) * diag[rows]
+    for m in range(4):
+        send[24 + m] = below[8 * m : 8 * m + 8]
+
+
+def window(place, high_pair, second, own, first, low_pair):
     even_core, even_chip = place[1] == 0, place[2] == 0
 
     def part(n, k):
@@ -439,9 +459,9 @@
     return part
 
 
-def middle_kernel(place, low_pair, second, own, first, high_pair, cc, cb, gg, v2, cc_r, cb_r, v2_r, v_out, c1, g1, c2, send,
+def middle_kernel(place, high_pair, second, own, first, low_pair, cc, cb, gg, v2, cc_r, cb_r, v2_r, v_out, c1, g1, c2, send,
                   cb1, w_a, w_b, cb2, u_a, u_b, v_a, v_b):
-    part = window(place, low_pair, second, own, first, high_pair)
+    part = window(place, high_pair, second, own, first, low_pair)
     for n in range(5):
         for k in range(8):
             cb1[8 * n + k] = part(n, k)
@@ -456,13 +476,16 @@
     fine_sweep(v_b, v_a, cc, cb, 3, 27)
     fine_sweep(v_a, v_b, cc, cb, 4, 26)
     fine_sweep(v_b, v_out, cc, cb, 5, 25)
+    source = lane_sums(fine_residue(v_out, cc, cb, gg), pairs_packed())
     for k in range(8):
-        send[k] = 4.0 * c1[16 + k] * fine_residue(v_out, cc, cb, gg, k)
-
-
-def last_kernel(place, low_pair, second, own, first, high_pair, cc, cb, v2, c1, g1, c2, out,
-                cb1, w_a, w_b, cb2, u_a, u_b, v_a, v_b, flat):
-    part = window(place, low_pair, second, own, first, high_pair)
+        send[k] = 0.5 * c1[16 + k] * source[8 * k : 8 * k + 8]
+
+
+def last_kernel(place, high_pair, second, own, first, low_pair, cc, cb, v2, c1, g1, c2, deposits, out, coupled,
+                cb1, w_a, w_b, cb2, u_a, u_b, v_a, v_b, flat, sem):
+    copy = pltpu.make_async_copy(deposits, coupled, sem)
+    copy.start()
+    part = window(place, high_pair, second, own, first, low_pair)
     for n in range(5):
         for k in range(8):
             cb1[8 * n + k] = part(n, k)
@@ -475,9 +498,10 @@
             flat[pl.ds(x * 32 + q, 8, stride=4), :] = v_a[7 + x, q]
     for x in range(CX):
         out[x] = flat[pl.ds(pl.multiple_of(x * 32 + 8 * place[0], 8), 8), :]
-
-
-def call(kernel, outs, scratch, operands, smem_first=False, in_hbm=False, cost=1000000, limit=LIMIT):
+    copy.wait()
+
+
+def call(kernel, outs, scratch, operands, smem_first=False, in_hbm=False, outs_hbm=0, cost=1000000, limit=LIMIT):
     kind = pltpu.HBM if in_hbm else pltpu.VMEM
     specs = [pl.BlockSpec(memory_space=kind) for _ in operands]
     if smem_first:
@@ -487,7 +511,9 @@
         kernel,
         out_shape=shapes,
         in_specs=specs,
-        out_specs=[pl.BlockSpec(memory_space=pltpu.VMEM) for _ in outs],
+        out_specs=[
+            pl.BlockSpec(memory_space=pltpu.VMEM if n < len(outs) - outs_hbm else pltpu.HBM) for n in range(len(outs))
+        ],
         scratch_shapes=[pltpu.VMEM(*piece) if isinstance(piece, tuple) else piece for piece in scratch],
         compiler_params=pltpu.CompilerParams(vmem_limit_bytes=limit),
         cost_estimate=pl.CostEstimate(flops=cost, bytes_accessed=cost, transcendentals=0),
@@ -515,7 +541,7 @@
     onward = jnp.where(place[1] == place[2], high_pair, low_pair)
     if beside is not None:
         onward, beside = lax.optimization_barrier((onward, beside))
-    return [low_pair, swap(onward), block, first, high_pair], beside
+    return [high_pair, swap(onward), block, first, low_pair], beside
 
 
 def shards(volume, drag, momentum, offsets, cell_index, destinations, rhs, wall):
@@ -552,7 +578,7 @@
     cc, cb, gg, v2, first = call(
         start_kernel, [fine, fine, (CX, 4, 8, NZ), fine, (28, 8, NZ)], [], [head, late, keep, next_head]
     )
-    coupled, cc_r, cb_r, v2_r = call(
+    deposits, cc_r, cb_r, v2_r = call(
         rest_kernel,
         [(4, CX, 8, NZ), (10, 4, 8, NZ), (10, 4, 8, NZ), (12, 4, 8, NZ)],
         [((CX * 32, NZ), F32)],
@@ -560,7 +586,7 @@
         smem_first=True,
     )
     scratch = [(mid, F32), (mid, F32), (mid, F32), (low, F32), (low, F32), (low, F32), (fine, F32), (fine, F32)]
-    parts, coupled = around(first, place, coupled)
+    parts, deposits = around(first, place, deposits)
     v3, c1, g1, c2, second = call(
         middle_kernel,
         [fine, mid, mid, low, (8, 8, NZ)],
@@ -569,12 +595,13 @@
         smem_first=True,
     )
     parts, _ = around(second, place)
-    (pressure,) = call(
+    pressure, coupled = call(
         last_kernel,
-        [(CX, 8, NZ)],
-        scratch + [((CX * 32, NZ), F32)],
-        [place] + parts + [cc, cb, v3, c1, g1, c2],
+        [(CX, 8, NZ), (4, CX, 8, NZ)],
+        scratch + [((CX * 32, NZ), F32), pltpu.SemaphoreType.DMA],
+        [place] + parts + [cc, cb, v3, c1, g1, c2, deposits],
         smem_first=True,
+        outs_hbm=1,
     )
     return coupled, pressure
 

time: 106 us -> 102 us (0.962)
  Pallas kernels: 16.9 us -> 14 us
  starting transfers between devices: 54 us -> 52.5 us
    pallas_call x8, Pallas kernels: 16.9 us -> 14 us  [call(): pl.pallas_call(kernel, out_shape=shapes, in_specs=specs, out_specs=[pl.Bl...]
  transfers between devices with their start and end apart: 12 -> 12, of which waited for: 6 -> 6; matrix products, arithmetic and copies ran while one was open for 0% -> 0% of each run, Pallas kernels for 4% -> 3%
where the time goes in v6:
time: 102 us; the launch traced here: 101 us
  starting transfers between devices  52.5 us (51%)
  waiting for transfers between devices  18.4 us (18%)
  Pallas kernels  14 us (14%)
  blocking collectives  13.4 us (13%)
  local copies, waits for them, and re-layouts  1.61 us (2%)
    all_to_all x1, starting transfers between devices, shards(): lax.all_to_all(outgoing, 'box', split_axis=0, concat_axis=0, tiled=True)  20.4 us
    pallas_call x8, Pallas kernels, call(): pl.pallas_call(kernel, out_shape=shapes, in_specs=specs, out_specs=[pl.Bl...  14 us
    all_gather x1, blocking collectives, shards(): slabs = lax.all_gather(pay, 'slab')  13.4 us
    ppermute x4, starting transfers between devices, meet(): lax.ppermute(block, 'box', [(2 * chips[i // 2] + i % 2, i) for i in range...  13 us
    all_to_all x1, waiting for transfers between devices, shards(): lax.all_to_all(outgoing, 'box', split_axis=0, concat_axis=0, tiled=True)  10.8 us
    ppermute x3, starting transfers between devices, fetch(): lax.ppermute(block, 'box', [((i + distance) % count, i) for i in range(co...  9.71 us
    ppermute x4, starting transfers between devices, swap(): lax.ppermute(block, 'box', [(i ^ 1, i) for i in range(lax.axis_size('box'...  9.39 us
    ppermute x3, waiting for transfers between devices, fetch(): lax.ppermute(block, 'box', [((i + distance) % count, i) for i in range(co...  3.77 us
  transfers between devices with their start and end apart: 12, of which 6 were waited for; matrix products, arithmetic and copies ran while one was open for 0% of the time, Pallas kernels for 3%

profile of v6, /device:TPU:1, one launch (start us, length us, event | category | flops | bytes accessed | tf_op | source)
XLA Modules:
  0.0 100.9 jit_solution(14230642415997918739)
XLA Ops:
  0.6 2.9 %shard_map.95 = f32[128,1,256]{2,1,0:T(1,128)} custom-call(f32[1,2048]{1,0:T(1,128)} %bitcast.14, f32[1,2048]{1,0:T(1,128)} %bitcast.15, f32[2,2048]{1,0:T(2,128)} %mom_in.1, f32[3,2048]{1,0:T(4,128)} %off_in.1, s32[1,2048]{1,0:T(1,128)} %bitcast.16, s32[1,2048]{1,0:T(1,128)} %bitcast.17), custom_call_target="tpu_custom_call" | custom-call | flops 1000000 | bytes 1000000 | tf_op jit(solution)/shard_map/pallas_call | solution.py:510
  3.6 20.4 %all-to-all-start = ((f32[128,1,256]{2,1,0:T(1,128)}), f32[128,1,256]{2,1,0:T(1,128)S(1)}, u32[]{:S(2)}, u32[]{:S(2)}) async-start(f32[128,1,256]{2,1,0:T(1,128)} %shard_map.95), calls=%async_computation | async-start | bytes 262144 | tf_op jit(solution)/shard_map/all_to_all | solution.py:561
  24.0 0.0 copy-start.1
  24.0 0.8 copy-done.1
  24.8 0.0 slice-start
  24.8 0.8 slice-done
  25.6 0.0 copy-start
  25.6 3.7 %collective-permute-start = (f32[18,8,128]{2,1,0:T(8,128)S(1)}, f32[18,8,128]{2,1,0:T(8,128)S(1)}, u32[]{:S(2)}, u32[]{:S(2)}) collective-permute-start(f32[18,8,128]{2,1,0:T(8,128)S(1)} %pad_maximum_fusion), channel_id=1, source_target_pairs={{508,0},{0,4},{4,8},{8,12},{12,16},{16,20},{20,24},{24,28},{28,32}... | collective-permute-start | bytes 221192 | tf_op jit(solution)/shard_map/ppermute | solution.py:525
  29.3 10.8 %all-to-all-done = f32[128,1,256]{2,1,0:T(1,128)S(1)} async-done(((f32[128,1,256]{2,1,0:T(1,128)}), f32[128,1,256]{2,1,0:T(1,128)S(1)}, u32[]{:S(2)}, u32[]{:S(2)}) %all-to-all-start) | async-done | bytes 131104 | tf_op jit(solution)/shard_map/all_to_all | solution.py:561
  40.1 0.0 collective-permute-done.prev
  40.1 0.0 copy-done
  40.1 2.7 %shard_map.96 = (f32[63,8,128]{2,1,0:T(8,128)S(1)}, f32[3,18,8,128]{3,2,1,0:T(8,128)S(1)}) custom-call(f32[128,256]{1,0:T(8,128)S(1)} %bitcast.13, f32[16,8,128]{2,1,0:T(8,128)S(1)} %copy-done, s32[16,8,128]{2,1,0:T(8,128)S(1)} %copy-done.1, f32[18,8,128]{2,1,0:T(8,128)S(1)} %collective-permute-done.prev), custom_call_target="tpu_custom_call" | custom-call | flops 1000000 | bytes 1000000 | tf_op jit(solution)/shard_map/pallas_call | solution.py:510
  42.8 13.4 %all-gather = f32[252,8,128]{2,1,0:T(8,128)S(1)} all-gather(f32[63,8,128]{2,1,0:T(8,128)S(1)} %get-tuple-element.24), channel_id=2, replica_groups=mesh['box'=128,'slab'=4] {'slab'}, dimensions={0}, use_global_device_ids=true | all-gather | bytes 1290240 | tf_op jit(solution)/shard_map/all_gather | solution.py:569
  56.2 0.2 shard_map.97.own_head
  56.4 4.1 %collective-permute-start.1 = (f32[91,8,128]{2,1,0:T(8,128)S(1)}, f32[91,8,128]{2,1,0:T(8,128)S(1)}, u32[]{:S(2)}, u32[]{:S(2)}) collective-permute-start(f32[91,8,128]{2,1,0:T(8,128)S(1)} %shard_map.97.own_head), channel_id=1, source_target_pairs={{4,0},{8,4},{12,8},{16,12},{20,16},{24,20},{28,24},{32,28},{36,32}... | collective-permute-start | bytes 1118216 | tf_op jit(solution)/shard_map/ppermute | solution.py:525
  60.5 0.1 pad_add_fusion.place
  60.6 0.7 shard_map.98
  61.3 1.9 %collective-permute-start.4 = (f32[68,8,128]{2,1,0:T(8,128)S(1)}, f32[68,8,128]{2,1,0:T(8,128)S(1)}, u32[]{:S(2)}, u32[]{:S(2)}) collective-permute-start(f32[68,8,128]{2,1,0:T(8,128)S(1)} %get-tuple-element.26.own_late), channel_id=1, source_target_pairs={{4,0},{8,4},{12,8},{16,12},{20,16},{24,20},{28,24},{32,28},{36,32}... | collective-permute-start | bytes 835592 | tf_op jit(solution)/shard_map/ppermute | solution.py:525
  63.2 3.8 %collective-permute-done.1.next_head = f32[91,8,128]{2,1,0:T(8,128)S(1)} collective-permute-done((f32[91,8,128]{2,1,0:T(8,128)S(1)}, f32[91,8,128]{2,1,0:T(8,128)S(1)}, u32[]{:S(2)}, u32[]{:S(2)}) %collective-permute-start.1) | collective-permute-done | bytes 372768 | tf_op jit(solution)/shard_map/ppermute | solution.py:525
  67.0 1.2 %shard_map.99 = (f32[30,4,8,128]{3,2,1,0:T(8,128)S(1)}, f32[30,4,8,128]{3,2,1,0:T(8,128)S(1)}, f32[16,4,8,128]{3,2,1,0:T(8,128)S(1)}, f32[30,4,8,128]{3,2,1,0:T(8,128)S(1)}, f32[28,8,128]{2,1,0:T(8,128)}) custom-call(f32[91,8,128]{2,1,0:T(8,128)S(1)} %shard_map.97.own_head, f32[68,8,128]{2,1,0:T(8,128)S(1)} %get-tuple-element.26.own_late, ...), custom_call_target="tpu_custom_call" | custom-call | flops 1000000 | bytes 1000000 | tf_op jit(solution)/shard_map/pallas_call | solution.py:510
  68.2 5.3 %collective-permute-start.3 = (f32[28,8,128]{2,1,0:T(8,128)}, f32[28,8,128]{2,1,0:T(8,128)S(1)}, u32[]{:S(2)}, u32[]{:S(2)}) collective-permute-start(f32[28,8,128]{2,1,0:T(8,128)} %get-tuple-element.28.own), channel_id=1, source_target_pairs={{504,0},{508,4},{16,8},{20,12},{8,16},{12,20},{32,24},{36,28},{24,... | collective-permute-start | bytes 344072 | tf_op jit(solution)/shard_map/ppermute | solution.py:535
  73.5 1.9 %collective-permute-start.2 = (f32[28,8,128]{2,1,0:T(8,128)}, f32[28,8,128]{2,1,0:T(8,128)S(1)}, u32[]{:S(2)}, u32[]{:S(2)}) collective-permute-start(f32[28,8,128]{2,1,0:T(8,128)} %get-tuple-element.28.own), channel_id=1, source_target_pairs={{8,0},{12,4},{0,8},{4,12},{24,16},{28,20},{16,24},{20,28},{40,32},... | collective-permute-start | bytes 344072 | tf_op jit(solution)/shard_map/ppermute | solution.py:535
  75.5 1.9 %collective-permute-start.6 = (f32[28,8,128]{2,1,0:T(8,128)}, f32[28,8,128]{2,1,0:T(8,128)S(1)}, u32[]{:S(2)}, u32[]{:S(2)}) collective-permute-start(f32[28,8,128]{2,1,0:T(8,128)} %get-tuple-element.28.own), channel_id=1, source_target_pairs={{4,0},{0,4},{12,8},{8,12},{20,16},{16,20},{28,24},{24,28},{36,32},... | collective-permute-start | bytes 344072 | tf_op jit(solution)/shard_map/ppermute | solution.py:529
  77.4 0.0 collective-permute-done.4.next_late
  77.4 0.7 shard_map.100
  78.1 0.0 collective-permute-done.3.low_pair
  78.1 1.1 %collective-permute-done.2.high_pair = f32[28,8,128]{2,1,0:T(8,128)S(1)} collective-permute-done((f32[28,8,128]{2,1,0:T(8,128)}, f32[28,8,128]{2,1,0:T(8,128)S(1)}, u32[]{:S(2)}, u32[]{:S(2)}) %collective-permute-start.2) | collective-permute-done | bytes 114720 | tf_op jit(solution)/shard_map/ppermute | solution.py:535
  79.3 1.9 %collective-permute-start.5 = (f32[28,8,128]{2,1,0:T(8,128)S(1)}, f32[28,8,128]{2,1,0:T(8,128)S(1)}, u32[]{:S(2)}, u32[]{:S(2)}) collective-permute-start(f32[28,8,128]{2,1,0:T(8,128)S(1)} %broadcast_select_fusion), channel_id=1, source_target_pairs={{4,0},{0,4},{12,8},{8,12},{20,16},{16,20},{28,24},{24,28},{36,32},... | collective-permute-start | bytes 344072 | tf_op jit(solution)/shard_map/ppermute | solution.py:529
  81.2 0.0 collective-permute-done.6.first
  81.2 1.3 %collective-permute-done.5.second = f32[28,8,128]{2,1,0:T(8,128)S(1)} collective-permute-done((f32[28,8,128]{2,1,0:T(8,128)S(1)}, f32[28,8,128]{2,1,0:T(8,128)S(1)}, u32[]{:S(2)}, u32[]{:S(2)}) %collective-permute-start.5) | collective-permute-done | bytes 114720 | tf_op jit(solution)/shard_map/ppermute | solution.py:529
  82.5 3.0 %shard_map.101 = (f32[30,4,8,128]{3,2,1,0:T(8,128)S(1)}, f32[40,8,128]{2,1,0:T(8,128)S(1)}, f32[40,8,128]{2,1,0:T(8,128)S(1)}, f32[20,8,128]{2,1,0:T(8,128)S(1)}, f32[8,8,128]{2,1,0:T(8,128)S(1)}) custom-call(s32[3]{0:T(128)S(1)} %pad_add_fusion.place, f32[28,8,128]{2,1,0:T(8,128)S(1)} %collective-permute-done.2.high_pair, ...), custom_call_target="tpu_custom_call" | custom-call | flops 1000000 | bytes 1000000 | tf_op jit(solution)/shard_map/pallas_call | solution.py:510
  85.6 3.8 %collective-permute-start.8 = (f32[8,8,128]{2,1,0:T(8,128)S(1)}, f32[8,8,128]{2,1,0:T(8,128)S(1)}, u32[]{:S(2)}, u32[]{:S(2)}) collective-permute-start(f32[8,8,128]{2,1,0:T(8,128)S(1)} %get-tuple-element.38.own), channel_id=1, source_target_pairs={{504,0},{508,4},{16,8},{20,12},{8,16},{12,20},{32,24},{36,28},{24,... | collective-permute-start | bytes 98312 | tf_op jit(solution)/shard_map/ppermute | solution.py:535
  89.4 1.9 %collective-permute-start.7 = (f32[8,8,128]{2,1,0:T(8,128)S(1)}, f32[8,8,128]{2,1,0:T(8,128)S(1)}, u32[]{:S(2)}, u32[]{:S(2)}) collective-permute-start(f32[8,8,128]{2,1,0:T(8,128)S(1)} %get-tuple-element.38.own), channel_id=1, source_target_pairs={{8,0},{12,4},{0,8},{4,12},{24,16},{28,20},{16,24},{20,28},{40,32},... | collective-permute-start | bytes 98312 | tf_op jit(solution)/shard_map/ppermute | solution.py:535
  91.3 2.4 %collective-permute-start.10 = (f32[8,8,128]{2,1,0:T(8,128)S(1)}, f32[8,8,128]{2,1,0:T(8,128)S(1)}, u32[]{:S(2)}, u32[]{:S(2)}) collective-permute-start(f32[8,8,128]{2,1,0:T(8,128)S(1)} %get-tuple-element.38.own), channel_id=1, source_target_pairs={{4,0},{0,4},{12,8},{8,12},{20,16},{16,20},{28,24},{24,28},{36,32},... | collective-permute-start | bytes 98312 | tf_op jit(solution)/shard_map/ppermute | solution.py:529
  93.7 0.0 collective-permute-done.8.low_pair
  93.7 0.7 collective-permute-done.7.high_pair
  94.4 3.2 %collective-permute-start.9 = (f32[8,8,128]{2,1,0:T(8,128)S(1)}, f32[8,8,128]{2,1,0:T(8,128)S(1)}, u32[]{:S(2)}, u32[]{:S(2)}) collective-permute-start(f32[8,8,128]{2,1,0:T(8,128)S(1)} %broadcast_select_fusion.1), channel_id=1, source_target_pairs={{4,0},{0,4},{12,8},{8,12},{20,16},{16,20},{28,24},{24,28},{36,32},... | collective-permute-start | bytes 98312 | tf_op jit(solution)/shard_map/ppermute | solution.py:529
  97.6 0.0 collective-permute-done.10.first
  97.6 0.8 collective-permute-done.9.second
  98.4 2.5 %shard_map.102 = (f32[16,8,128]{2,1,0:T(8,128)}, f32[4,16,8,128]{3,2,1,0:T(8,128)}) custom-call(s32[3]{0:T(128)S(1)} %pad_add_fusion.place, f32[8,8,128]{2,1,0:T(8,128)S(1)} %collective-permute-done.7.high_pair, f32[8,8,128]{2,1,0:T(8,128)S(1)} %collective-permute-done.9.second, f32[8,8,128]{2,1,0:T(8,128)S(1)} %get-tuple-element.38.own, ...), custom_call_target="tpu_custom_call" | custom-call | flops 1000000 | bytes 1000000 | tf_op jit(solution)/shard_map/pallas_call | solution.py:510
  (5 shorter events, 0.0 us)
Async XLA Ops:
  3.6 36.5 %all-to-all-start = ((f32[128,1,256]{2,1,0:T(1,128)}), f32[128,1,256]{2,1,0:T(1,128)S(1)}, u32[]{:S(2)}, u32[]{:S(2)}) async-start(f32[128,1,256]{2,1,0:T(1,128)} %shard_map.95), calls=%async_computation | async-start | bytes 262144 | tf_op jit(solution)/shard_map/all_to_all | solution.py:561
  24.0 0.8 copy-start.1
  24.8 0.8 slice-start
  25.6 14.5 %copy-start = (f32[16,8,128]{2,1,0:T(8,128)S(1)}, f32[16,8,128]{2,1,0:T(8,128)}, u32[]{:S(2)}) copy-start(f32[16,8,128]{2,1,0:T(8,128)} %rhs.1) | copy-start | bytes 196612
  25.6 14.5 %collective-permute-start = (f32[18,8,128]{2,1,0:T(8,128)S(1)}, f32[18,8,128]{2,1,0:T(8,128)S(1)}, u32[]{:S(2)}, u32[]{:S(2)}) collective-permute-start(f32[18,8,128]{2,1,0:T(8,128)S(1)} %pad_maximum_fusion), channel_id=1, source_target_pairs={{508,0},{0,4},{4,8},{8,12},{12,16},{16,20},{20,24},{24,28},{28,32}... | collective-permute-start | bytes 221192 | tf_op jit(solution)/shard_map/ppermute | solution.py:525
  56.4 10.6 %collective-permute-start.1 = (f32[91,8,128]{2,1,0:T(8,128)S(1)}, f32[91,8,128]{2,1,0:T(8,128)S(1)}, u32[]{:S(2)}, u32[]{:S(2)}) collective-permute-start(f32[91,8,128]{2,1,0:T(8,128)S(1)} %shard_map.97.own_head), channel_id=1, source_target_pairs={{4,0},{8,4},{12,8},{16,12},{20,16},{24,20},{28,24},{32,28},{36,32}... | collective-permute-start | bytes 1118216 | tf_op jit(solution)/shard_map/ppermute | solution.py:525
  61.3 16.1 %collective-permute-start.4 = (f32[68,8,128]{2,1,0:T(8,128)S(1)}, f32[68,8,128]{2,1,0:T(8,128)S(1)}, u32[]{:S(2)}, u32[]{:S(2)}) collective-permute-start(f32[68,8,128]{2,1,0:T(8,128)S(1)} %get-tuple-element.26.own_late), channel_id=1, source_target_pairs={{4,0},{8,4},{12,8},{16,12},{20,16},{24,20},{28,24},{32,28},{36,32}... | collective-permute-start | bytes 835592 | tf_op jit(solution)/shard_map/ppermute | solution.py:525
  68.2 9.9 %collective-permute-start.3 = (f32[28,8,128]{2,1,0:T(8,128)}, f32[28,8,128]{2,1,0:T(8,128)S(1)}, u32[]{:S(2)}, u32[]{:S(2)}) collective-permute-start(f32[28,8,128]{2,1,0:T(8,128)} %get-tuple-element.28.own), channel_id=1, source_target_pairs={{504,0},{508,4},{16,8},{20,12},{8,16},{12,20},{32,24},{36,28},{24,... | collective-permute-start | bytes 344072 | tf_op jit(solution)/shard_map/ppermute | solution.py:535
  73.5 5.7 %collective-permute-start.2 = (f32[28,8,128]{2,1,0:T(8,128)}, f32[28,8,128]{2,1,0:T(8,128)S(1)}, u32[]{:S(2)}, u32[]{:S(2)}) collective-permute-start(f32[28,8,128]{2,1,0:T(8,128)} %get-tuple-element.28.own), channel_id=1, source_target_pairs={{8,0},{12,4},{0,8},{4,12},{24,16},{28,20},{16,24},{20,28},{40,32},... | collective-permute-start | bytes 344072 | tf_op jit(solution)/shard_map/ppermute | solution.py:535
  75.5 5.8 %collective-permute-start.6 = (f32[28,8,128]{2,1,0:T(8,128)}, f32[28,8,128]{2,1,0:T(8,128)S(1)}, u32[]{:S(2)}, u32[]{:S(2)}) collective-permute-start(f32[28,8,128]{2,1,0:T(8,128)} %get-tuple-element.28.own), channel_id=1, source_target_pairs={{4,0},{0,4},{12,8},{8,12},{20,16},{16,20},{28,24},{24,28},{36,32},... | collective-permute-start | bytes 344072 | tf_op jit(solution)/shard_map/ppermute | solution.py:529
  79.3 3.2 %collective-permute-start.5 = (f32[28,8,128]{2,1,0:T(8,128)S(1)}, f32[28,8,128]{2,1,0:T(8,128)S(1)}, u32[]{:S(2)}, u32[]{:S(2)}) collective-permute-start(f32[28,8,128]{2,1,0:T(8,128)S(1)} %broadcast_select_fusion), channel_id=1, source_target_pairs={{4,0},{0,4},{12,8},{8,12},{20,16},{16,20},{28,24},{24,28},{36,32},... | collective-permute-start | bytes 344072 | tf_op jit(solution)/shard_map/ppermute | solution.py:529
  85.6 8.1 %collective-permute-start.8 = (f32[8,8,128]{2,1,0:T(8,128)S(1)}, f32[8,8,128]{2,1,0:T(8,128)S(1)}, u32[]{:S(2)}, u32[]{:S(2)}) collective-permute-start(f32[8,8,128]{2,1,0:T(8,128)S(1)} %get-tuple-element.38.own), channel_id=1, source_target_pairs={{504,0},{508,4},{16,8},{20,12},{8,16},{12,20},{32,24},{36,28},{24,... | collective-permute-start | bytes 98312 | tf_op jit(solution)/shard_map/ppermute | solution.py:535
  89.4 5.0 %collective-permute-start.7 = (f32[8,8,128]{2,1,0:T(8,128)S(1)}, f32[8,8,128]{2,1,0:T(8,128)S(1)}, u32[]{:S(2)}, u32[]{:S(2)}) collective-permute-start(f32[8,8,128]{2,1,0:T(8,128)S(1)} %get-tuple-element.38.own), channel_id=1, source_target_pairs={{8,0},{12,4},{0,8},{4,12},{24,16},{28,20},{16,24},{20,28},{40,32},... | collective-permute-start | bytes 98312 | tf_op jit(solution)/shard_map/ppermute | solution.py:535
  91.3 6.2 %collective-permute-start.10 = (f32[8,8,128]{2,1,0:T(8,128)S(1)}, f32[8,8,128]{2,1,0:T(8,128)S(1)}, u32[]{:S(2)}, u32[]{:S(2)}) collective-permute-start(f32[8,8,128]{2,1,0:T(8,128)S(1)} %get-tuple-element.38.own), channel_id=1, source_target_pairs={{4,0},{0,4},{12,8},{8,12},{20,16},{16,20},{28,24},{24,28},{36,32},... | collective-permute-start | bytes 98312 | tf_op jit(solution)/shard_map/ppermute | solution.py:529
  94.4 4.0 %collective-permute-start.9 = (f32[8,8,128]{2,1,0:T(8,128)S(1)}, f32[8,8,128]{2,1,0:T(8,128)S(1)}, u32[]{:S(2)}, u32[]{:S(2)}) collective-permute-start(f32[8,8,128]{2,1,0:T(8,128)S(1)} %broadcast_select_fusion.1), channel_id=1, source_target_pairs={{4,0},{0,4},{12,8},{8,12},{20,16},{16,20},{28,24},{24,28},{36,32},... | collective-permute-start | bytes 98312 | tf_op jit(solution)/shard_map/ppermute | solution.py:529

commit v7 on v6

--- a/solution.py
+++ b/solution.py
@@ -22,7 +22,7 @@
 OTHERS = (0, 2, 3)
 CHUNKS = 8
 
-LIMIT = 48 * 1024 * 1024
+LIMIT = 24 * 1024 * 1024
 
 NT = (((1,), (1,)), ((), ()))
 
@@ -131,7 +131,7 @@
         for k in range(each):
             one(n * each + k, amats[n], vmats[n], k * NZ)
         part = lax.dot_general(amats[n][...], vmats[n][...], NT, preferred_element_type=F32)
-        acc[...] = part if n == 0 else acc[...] + part
+        acc[:768, :] = part if n == 0 else acc[:768, :] + part
     for x in range(XE):
         c = [acc[144 * k + 8 * x : 144 * k + 8 * x + 8, :] for k in range(4)]
         for k, channel in enumerate(OTHERS):
@@ -384,7 +384,7 @@
     mid_sweep(w_b, w_a, c1, cb1, 13, 27)
 
 
-def rest_kernel(place, own_head, own_late, keep, next_head, next_late, cc, cb, coupled, cc_r, cb_r, v2_r, flat):
+def rest_kernel(place, own_head, own_late, keep, next_head, next_late, cc, cb, coupled, cc_r, cb_r, v2_r, gg, flat):
     parts = Parts(own_head, own_late, keep, next_head, next_late)
     for k, c in enumerate(OTHERS):
         for x in range(CX):
@@ -407,9 +407,12 @@
             coefs[t, q], bases[t, q], _ = parts.coefficient(t, q)
     fine_sweep(bases, v2, coefs, bases, 1, 6)
     fine_sweep(bases, v2, coefs, bases, 24, 29)
-
-
-def start_kernel(own_head, own_late, keep, next_head, cc, cb, gg, v2, send):
+    for t in range(7, 23):
+        for q in range(4):
+            gg[t - 7, q] = (1.0 / OMEGA) * (6.0 + parts.joined(t, 1, q))
+
+
+def start_kernel(own_head, own_late, keep, next_head, cc, cb, v2, send, gg):
     parts = Parts(own_head, own_late, keep, next_head)
     for t in range(5, 25):
         for q in range(4):
@@ -446,22 +449,23 @@
         send[24 + m] = below[8 * m : 8 * m + 8]
 
 
-def window(place, high_pair, second, own, first, low_pair):
+def window(place, high_pair, both, own, low_pair):
     even_core, even_chip = place[1] == 0, place[2] == 0
+    size = own.shape[0]
 
     def part(n, k):
         if n == 2:
             return own[k]
         if n in (1, 3):
-            return jnp.where(even_core == (n == 1), second[k], first[k])
+            return jnp.where(even_core == (n == 1), both[size + k], both[k])
         return jnp.where(even_chip == (n == 0), low_pair[k], high_pair[k])
 
     return part
 
 
-def middle_kernel(place, high_pair, second, own, first, low_pair, cc, cb, gg, v2, cc_r, cb_r, v2_r, v_out, c1, g1, c2, send,
+def middle_kernel(place, high_pair, both, own, low_pair, cc, cb, gg, v2, cc_r, cb_r, v2_r, v_out, c1, g1, c2, send,
                   cb1, w_a, w_b, cb2, u_a, u_b, v_a, v_b):
-    part = window(place, high_pair, second, own, first, low_pair)
+    part = window(place, high_pair, both, own, low_pair)
     for n in range(5):
         for k in range(8):
             cb1[8 * n + k] = part(n, k)
@@ -481,11 +485,11 @@
         send[k] = 0.5 * c1[16 + k] * source[8 * k : 8 * k + 8]
 
 
-def last_kernel(place, high_pair, second, own, first, low_pair, cc, cb, v2, c1, g1, c2, deposits, out, coupled,
+def last_kernel(place, high_pair, both, own, low_pair, cc, cb, v2, c1, g1, c2, deposits, out, coupled,
                 cb1, w_a, w_b, cb2, u_a, u_b, v_a, v_b, flat, sem):
     copy = pltpu.make_async_copy(deposits, coupled, sem)
     copy.start()
-    part = window(place, high_pair, second, own, first, low_pair)
+    part = window(place, high_pair, both, own, low_pair)
     for n in range(5):
         for k in range(8):
             cb1[8 * n + k] = part(n, k)
@@ -537,11 +541,10 @@
 
 def around(block, place, beside=None):
     low_pair, high_pair = meet(block, 1), meet(block, 0)
-    first = swap(block)
-    onward = jnp.where(place[1] == place[2], high_pair, low_pair)
+    onward = jnp.concatenate([block, jnp.where(place[1] == place[2], high_pair, low_pair)], axis=0)
     if beside is not None:
         onward, beside = lax.optimization_barrier((onward, beside))
-    return [high_pair, swap(onward), block, first, low_pair], beside
+    return [high_pair, swap(onward), block, low_pair], beside
 
 
 def shards(volume, drag, momentum, offsets, cell_index, destinations, rhs, wall):
@@ -562,12 +565,12 @@
     pay, craw = call(
         deposit_kernel,
         [(3 * XE + XE // 2, 8, NZ), (3, XE, 8, NZ)],
-        [((13, CAP, NZ), F32), ((3, CAP, NZ), I32), ((XE, CAP, NZ), F32), ((768, NZ), F32)]
+        [((13, CAP, NZ), F32), ((3, CAP, NZ), I32), ((XE, CAP, NZ), F32), ((800, NZ), F32)]
         + [((768, SLOTS // CHUNKS), BF16)] * CHUNKS + [((NZ, SLOTS // CHUNKS), BF16)] * CHUNKS,
         [incoming.reshape(N_BOX, 8 * CAP), rhs, wall, prev],
     )
     slabs = lax.all_gather(pay, "slab")
-    sums = [((HEAD * 32, NZ), F32)] * 2
+    sums = [((HEAD * 32 + 8, NZ), F32)] * 2
     (head,) = call(head_kernel, [(8 * HEAD + 3, 8, NZ)], sums, [slabs])
     next_head = fetch(head, 1)
     late, keep = call(
@@ -575,13 +578,14 @@
     )
     next_late = fetch(late, 1)
     fine, mid, low = (T0, 4, 8, NZ), (T1, 8, NZ), (T2, 8, NZ)
-    cc, cb, gg, v2, first = call(
-        start_kernel, [fine, fine, (CX, 4, 8, NZ), fine, (28, 8, NZ)], [], [head, late, keep, next_head]
-    )
-    deposits, cc_r, cb_r, v2_r = call(
+    weights = (CX, 4, 8, NZ)
+    cc, cb, v2, first = call(
+        start_kernel, [fine, fine, fine, (28, 8, NZ)], [(weights, F32)], [head, late, keep, next_head]
+    )
+    deposits, cc_r, cb_r, v2_r, gg = call(
         rest_kernel,
-        [(4, CX, 8, NZ), (10, 4, 8, NZ), (10, 4, 8, NZ), (12, 4, 8, NZ)],
-        [((CX * 32, NZ), F32)],
+        [(4, CX, 8, NZ), (10, 4, 8, NZ), (10, 4, 8, NZ), (12, 4, 8, NZ), weights],
+        [((CX * 32 + 8, NZ), F32)],
         [place, head, late, keep, next_head, next_late, cc, cb],
         smem_first=True,
     )
@@ -598,7 +602,7 @@
     pressure, coupled = call(
         last_kernel,
         [(CX, 8, NZ), (4, CX, 8, NZ)],
-        scratch + [((CX * 32, NZ), F32), pltpu.SemaphoreType.DMA],
+        scratch + [((CX * 32 + 8, NZ), F32), pltpu.SemaphoreType.DMA],
         [place] + parts + [cc, cb, v3, c1, g1, c2, deposits],
         smem_first=True,
         outs_hbm=1,

time: 102 us -> 101 us (level)
  waiting for transfers between devices: 18.4 us -> 22.7 us
  starting transfers between devices: 52.5 us -> 48.2 us
    ppermute x4 -> x2, starting transfers between devices: 9.39 us -> 5.12 us  [swap(): lax.ppermute(block, 'box', [(i ^ 1, i) for i in range(lax.axis_size('box'...]
    ppermute x4, waiting for transfers between devices: 1.79 us -> 5.87 us  [meet(): lax.ppermute(block, 'box', [(2 * chips[i // 2] + i % 2, i) for i in range...]
    ppermute x4 -> x2, waiting for transfers between devices: 2.11 us -> 2.33 us  [swap(): lax.ppermute(block, 'box', [(i ^ 1, i) for i in range(lax.axis_size('box'...]
  transfers between devices with their start and end apart: 12 -> 10, of which waited for: 6 -> 8; matrix products, arithmetic and copies ran while one was open for 0% -> 0% of each run, Pallas kernels for 3% -> 2%
where the time goes in v7:
time: 101 us; the launch traced here: 99.9 us
  starting transfers between devices  48.2 us (48%)
  waiting for transfers between devices  22.7 us (22%)
  blocking collectives  13.4 us (13%)
  Pallas kernels  13 us (13%)
  local copies, waits for them, and re-layouts  1.61 us (2%)
    all_to_all x1, starting transfers between devices, shards(): lax.all_to_all(outgoing, 'box', split_axis=0, concat_axis=0, tiled=True)  20.4 us
    all_gather x1, blocking collectives, shards(): slabs = lax.all_gather(pay, 'slab')  13.4 us
    pallas_call x8, Pallas kernels, call(): pl.pallas_call(kernel, out_shape=shapes, in_specs=specs, out_specs=[pl.Bl...  13 us
    ppermute x4, starting transfers between devices, meet(): lax.ppermute(block, 'box', [(2 * chips[i // 2] + i % 2, i) for i in range...  13 us
    all_to_all x1, waiting for transfers between devices, shards(): lax.all_to_all(outgoing, 'box', split_axis=0, concat_axis=0, tiled=True)  10.8 us
    ppermute x3, starting transfers between devices, fetch(): lax.ppermute(block, 'box', [((i + distance) % count, i) for i in range(co...  9.71 us
    ppermute x4, waiting for transfers between devices, meet(): lax.ppermute(block, 'box', [(2 * chips[i // 2] + i % 2, i) for i in range...  5.87 us
    ppermute x2, starting transfers between devices, swap(): lax.ppermute(block, 'box', [(i ^ 1, i) for i in range(lax.axis_size('box'...  5.12 us
  transfers between devices with their start and end apart: 10, of which 8 were waited for; matrix products, arithmetic and copies ran while one was open for 0% of the time, Pallas kernels for 2%

profile of v7, /device:TPU:1, one launch (start us, length us, event | category | flops | bytes accessed | tf_op | source)
XLA Modules:
  0.0 99.9 jit_solution(17397188946590919518)
XLA Ops:
  0.6 2.9 %shard_map.95 = f32[128,1,256]{2,1,0:T(1,128)} custom-call(f32[1,2048]{1,0:T(1,128)} %bitcast.14, f32[1,2048]{1,0:T(1,128)} %bitcast.15, f32[2,2048]{1,0:T(2,128)} %mom_in.1, f32[3,2048]{1,0:T(4,128)} %off_in.1, s32[1,2048]{1,0:T(1,128)} %bitcast.16, s32[1,2048]{1,0:T(1,128)} %bitcast.17), custom_call_target="tpu_custom_call" | custom-call | flops 1000000 | bytes 1000000 | tf_op jit(solution)/shard_map/pallas_call | solution.py:514
  3.6 20.4 %all-to-all-start = ((f32[128,1,256]{2,1,0:T(1,128)}), f32[128,1,256]{2,1,0:T(1,128)S(1)}, u32[]{:S(2)}, u32[]{:S(2)}) async-start(f32[128,1,256]{2,1,0:T(1,128)} %shard_map.95), calls=%async_computation | async-start | bytes 262144 | tf_op jit(solution)/shard_map/all_to_all | solution.py:564
  24.0 0.0 copy-start.1
  24.0 0.8 copy-done.1
  24.8 0.0 slice-start
  24.8 0.8 slice-done
  25.6 0.0 copy-start
  25.6 3.7 %collective-permute-start = (f32[18,8,128]{2,1,0:T(8,128)S(1)}, f32[18,8,128]{2,1,0:T(8,128)S(1)}, u32[]{:S(2)}, u32[]{:S(2)}) collective-permute-start(f32[18,8,128]{2,1,0:T(8,128)S(1)} %pad_maximum_fusion.1), channel_id=1, source_target_pairs={{508,0},{0,4},{4,8},{8,12},{12,16},{16,20},{20,24},{24,28},{28,32}... | collective-permute-start | bytes 221192 | tf_op jit(solution)/shard_map/ppermute | solution.py:529
  29.3 10.8 %all-to-all-done = f32[128,1,256]{2,1,0:T(1,128)S(1)} async-done(((f32[128,1,256]{2,1,0:T(1,128)}), f32[128,1,256]{2,1,0:T(1,128)S(1)}, u32[]{:S(2)}, u32[]{:S(2)}) %all-to-all-start) | async-done | bytes 131104 | tf_op jit(solution)/shard_map/all_to_all | solution.py:564
  40.1 0.0 collective-permute-done.prev
  40.1 0.0 copy-done
  40.1 2.7 %shard_map.96 = (f32[63,8,128]{2,1,0:T(8,128)S(1)}, f32[3,18,8,128]{3,2,1,0:T(8,128)S(1)}) custom-call(f32[128,256]{1,0:T(8,128)S(1)} %bitcast.13, f32[16,8,128]{2,1,0:T(8,128)S(1)} %copy-done, s32[16,8,128]{2,1,0:T(8,128)S(1)} %copy-done.1, f32[18,8,128]{2,1,0:T(8,128)S(1)} %collective-permute-done.prev), custom_call_target="tpu_custom_call" | custom-call | flops 1000000 | bytes 1000000 | tf_op jit(solution)/shard_map/pallas_call | solution.py:514
  42.8 13.4 %all-gather = f32[252,8,128]{2,1,0:T(8,128)S(1)} all-gather(f32[63,8,128]{2,1,0:T(8,128)S(1)} %get-tuple-element.24), channel_id=2, replica_groups=mesh['box'=128,'slab'=4] {'slab'}, dimensions={0}, use_global_device_ids=true | all-gather | bytes 1290240 | tf_op jit(solution)/shard_map/all_gather | solution.py:572
  56.2 0.2 shard_map.97.own_head
  56.4 4.1 %collective-permute-start.1 = (f32[91,8,128]{2,1,0:T(8,128)S(1)}, f32[91,8,128]{2,1,0:T(8,128)S(1)}, u32[]{:S(2)}, u32[]{:S(2)}) collective-permute-start(f32[91,8,128]{2,1,0:T(8,128)S(1)} %shard_map.97.own_head), channel_id=1, source_target_pairs={{4,0},{8,4},{12,8},{16,12},{20,16},{24,20},{28,24},{32,28},{36,32}... | collective-permute-start | bytes 1118216 | tf_op jit(solution)/shard_map/ppermute | solution.py:529
  60.5 0.1 pad_add_fusion.place
  60.6 0.7 shard_map.98
  61.3 1.9 %collective-permute-start.4 = (f32[68,8,128]{2,1,0:T(8,128)S(1)}, f32[68,8,128]{2,1,0:T(8,128)S(1)}, u32[]{:S(2)}, u32[]{:S(2)}) collective-permute-start(f32[68,8,128]{2,1,0:T(8,128)S(1)} %get-tuple-element.26.own_late), channel_id=1, source_target_pairs={{4,0},{8,4},{12,8},{16,12},{20,16},{24,20},{28,24},{32,28},{36,32}... | collective-permute-start | bytes 835592 | tf_op jit(solution)/shard_map/ppermute | solution.py:529
  63.2 3.8 %collective-permute-done.1.next_head = f32[91,8,128]{2,1,0:T(8,128)S(1)} collective-permute-done((f32[91,8,128]{2,1,0:T(8,128)S(1)}, f32[91,8,128]{2,1,0:T(8,128)S(1)}, u32[]{:S(2)}, u32[]{:S(2)}) %collective-permute-start.1) | collective-permute-done | bytes 372768 | tf_op jit(solution)/shard_map/ppermute | solution.py:529
  67.0 0.6 shard_map.99
  67.6 5.3 %collective-permute-start.3 = (f32[28,8,128]{2,1,0:T(8,128)S(1)}, f32[28,8,128]{2,1,0:T(8,128)S(1)}, u32[]{:S(2)}, u32[]{:S(2)}) collective-permute-start(f32[28,8,128]{2,1,0:T(8,128)S(1)} %get-tuple-element.28.own), channel_id=1, source_target_pairs={{504,0},{508,4},{16,8},{20,12},{8,16},{12,20},{32,24},{36,28},{24,... | collective-permute-start | bytes 344072 | tf_op jit(solution)/shard_map/ppermute | solution.py:539
  72.9 1.9 %collective-permute-start.2 = (f32[28,8,128]{2,1,0:T(8,128)S(1)}, f32[28,8,128]{2,1,0:T(8,128)S(1)}, u32[]{:S(2)}, u32[]{:S(2)}) collective-permute-start(f32[28,8,128]{2,1,0:T(8,128)S(1)} %get-tuple-element.28.own), channel_id=1, source_target_pairs={{8,0},{12,4},{0,8},{4,12},{24,16},{28,20},{16,24},{20,28},{40,32},... | collective-permute-start | bytes 344072 | tf_op jit(solution)/shard_map/ppermute | solution.py:539
  74.8 0.0 collective-permute-done.4.next_late
  74.8 0.7 shard_map.100
  75.6 1.1 %collective-permute-done.3.low_pair = f32[28,8,128]{2,1,0:T(8,128)S(1)} collective-permute-done((f32[28,8,128]{2,1,0:T(8,128)S(1)}, f32[28,8,128]{2,1,0:T(8,128)S(1)}, u32[]{:S(2)}, u32[]{:S(2)}) %collective-permute-start.3) | collective-permute-done | bytes 114720 | tf_op jit(solution)/shard_map/ppermute | solution.py:539
  76.7 1.7 %collective-permute-done.2.high_pair = f32[28,8,128]{2,1,0:T(8,128)S(1)} collective-permute-done((f32[28,8,128]{2,1,0:T(8,128)S(1)}, f32[28,8,128]{2,1,0:T(8,128)S(1)}, u32[]{:S(2)}, u32[]{:S(2)}) %collective-permute-start.2) | collective-permute-done | bytes 114720 | tf_op jit(solution)/shard_map/ppermute | solution.py:539
  78.5 1.9 %collective-permute-start.5 = (f32[56,8,128]{2,1,0:T(8,128)S(1)}, f32[56,8,128]{2,1,0:T(8,128)S(1)}, u32[]{:S(2)}, u32[]{:S(2)}) collective-permute-start(f32[56,8,128]{2,1,0:T(8,128)S(1)} %pad_maximum_fusion), channel_id=1, source_target_pairs={{4,0},{0,4},{12,8},{8,12},{20,16},{16,20},{28,24},{24,28},{36,32},... | collective-permute-start | bytes 688136 | tf_op jit(solution)/shard_map/ppermute | solution.py:533
  80.4 1.5 %collective-permute-done.5.both = f32[56,8,128]{2,1,0:T(8,128)S(1)} collective-permute-done((f32[56,8,128]{2,1,0:T(8,128)S(1)}, f32[56,8,128]{2,1,0:T(8,128)S(1)}, u32[]{:S(2)}, u32[]{:S(2)}) %collective-permute-start.5) | collective-permute-done | bytes 229408 | tf_op jit(solution)/shard_map/ppermute | solution.py:533
  81.9 2.7 %shard_map.101 = (f32[30,4,8,128]{3,2,1,0:T(8,128)S(1)}, f32[40,8,128]{2,1,0:T(8,128)S(1)}, f32[40,8,128]{2,1,0:T(8,128)S(1)}, f32[20,8,128]{2,1,0:T(8,128)S(1)}, f32[8,8,128]{2,1,0:T(8,128)S(1)}) custom-call(s32[3]{0:T(128)S(1)} %pad_add_fusion.place, f32[28,8,128]{2,1,0:T(8,128)S(1)} %collective-permute-done.2.high_pair, ...), custom_call_target="tpu_custom_call" | custom-call | flops 1000000 | bytes 1000000 | tf_op jit(solution)/shard_map/pallas_call | solution.py:514
  84.6 3.8 %collective-permute-start.7 = (f32[8,8,128]{2,1,0:T(8,128)S(1)}, f32[8,8,128]{2,1,0:T(8,128)S(1)}, u32[]{:S(2)}, u32[]{:S(2)}) collective-permute-start(f32[8,8,128]{2,1,0:T(8,128)S(1)} %get-tuple-element.38.own), channel_id=1, source_target_pairs={{504,0},{508,4},{16,8},{20,12},{8,16},{12,20},{32,24},{36,28},{24,... | collective-permute-start | bytes 98312 | tf_op jit(solution)/shard_map/ppermute | solution.py:539
  88.4 1.9 %collective-permute-start.6 = (f32[8,8,128]{2,1,0:T(8,128)S(1)}, f32[8,8,128]{2,1,0:T(8,128)S(1)}, u32[]{:S(2)}, u32[]{:S(2)}) collective-permute-start(f32[8,8,128]{2,1,0:T(8,128)S(1)} %get-tuple-element.38.own), channel_id=1, source_target_pairs={{8,0},{12,4},{0,8},{4,12},{24,16},{28,20},{16,24},{20,28},{40,32},... | collective-permute-start | bytes 98312 | tf_op jit(solution)/shard_map/ppermute | solution.py:539
  90.3 2.2 %collective-permute-done.7.low_pair = f32[8,8,128]{2,1,0:T(8,128)S(1)} collective-permute-done((f32[8,8,128]{2,1,0:T(8,128)S(1)}, f32[8,8,128]{2,1,0:T(8,128)S(1)}, u32[]{:S(2)}, u32[]{:S(2)}) %collective-permute-start.7) | collective-permute-done | bytes 32800 | tf_op jit(solution)/shard_map/ppermute | solution.py:539
  92.5 0.8 collective-permute-done.6.high_pair
  93.4 3.2 %collective-permute-start.8 = (f32[16,8,128]{2,1,0:T(8,128)S(1)}, f32[16,8,128]{2,1,0:T(8,128)S(1)}, u32[]{:S(2)}, u32[]{:S(2)}) collective-permute-start(f32[16,8,128]{2,1,0:T(8,128)S(1)} %pad_maximum_fusion.2), channel_id=1, source_target_pairs={{4,0},{0,4},{12,8},{8,12},{20,16},{16,20},{28,24},{24,28},{36,32},... | collective-permute-start | bytes 196616 | tf_op jit(solution)/shard_map/ppermute | solution.py:533
  96.6 0.9 collective-permute-done.8.both
  97.4 2.5 %shard_map.102 = (f32[16,8,128]{2,1,0:T(8,128)}, f32[4,16,8,128]{3,2,1,0:T(8,128)}) custom-call(s32[3]{0:T(128)S(1)} %pad_add_fusion.place, f32[8,8,128]{2,1,0:T(8,128)S(1)} %collective-permute-done.6.high_pair, f32[16,8,128]{2,1,0:T(8,128)S(1)} %collective-permute-done.8.both, f32[8,8,128]{2,1,0:T(8,128)S(1)} %get-tuple-element.38.own, ...), custom_call_target="tpu_custom_call" | custom-call | flops 1000000 | bytes 1000000 | tf_op jit(solution)/shard_map/pallas_call | solution.py:514
  (7 shorter events, 0.1 us)
Async XLA Ops:
  3.6 36.5 %all-to-all-start = ((f32[128,1,256]{2,1,0:T(1,128)}), f32[128,1,256]{2,1,0:T(1,128)S(1)}, u32[]{:S(2)}, u32[]{:S(2)}) async-start(f32[128,1,256]{2,1,0:T(1,128)} %shard_map.95), calls=%async_computation | async-start | bytes 262144 | tf_op jit(solution)/shard_map/all_to_all | solution.py:564
  24.0 0.8 copy-start.1
  24.8 0.8 slice-start
  25.6 14.5 %copy-start = (f32[16,8,128]{2,1,0:T(8,128)S(1)}, f32[16,8,128]{2,1,0:T(8,128)}, u32[]{:S(2)}) copy-start(f32[16,8,128]{2,1,0:T(8,128)} %rhs.1) | copy-start | bytes 196612
  25.6 14.5 %collective-permute-start = (f32[18,8,128]{2,1,0:T(8,128)S(1)}, f32[18,8,128]{2,1,0:T(8,128)S(1)}, u32[]{:S(2)}, u32[]{:S(2)}) collective-permute-start(f32[18,8,128]{2,1,0:T(8,128)S(1)} %pad_maximum_fusion.1), channel_id=1, source_target_pairs={{508,0},{0,4},{4,8},{8,12},{12,16},{16,20},{20,24},{24,28},{28,32}... | collective-permute-start | bytes 221192 | tf_op jit(solution)/shard_map/ppermute | solution.py:529
  56.4 10.6 %collective-permute-start.1 = (f32[91,8,128]{2,1,0:T(8,128)S(1)}, f32[91,8,128]{2,1,0:T(8,128)S(1)}, u32[]{:S(2)}, u32[]{:S(2)}) collective-permute-start(f32[91,8,128]{2,1,0:T(8,128)S(1)} %shard_map.97.own_head), channel_id=1, source_target_pairs={{4,0},{8,4},{12,8},{16,12},{20,16},{24,20},{28,24},{32,28},{36,32}... | collective-permute-start | bytes 1118216 | tf_op jit(solution)/shard_map/ppermute | solution.py:529
  61.3 13.5 %collective-permute-start.4 = (f32[68,8,128]{2,1,0:T(8,128)S(1)}, f32[68,8,128]{2,1,0:T(8,128)S(1)}, u32[]{:S(2)}, u32[]{:S(2)}) collective-permute-start(f32[68,8,128]{2,1,0:T(8,128)S(1)} %get-tuple-element.26.own_late), channel_id=1, source_target_pairs={{4,0},{8,4},{12,8},{16,12},{20,16},{24,20},{28,24},{32,28},{36,32}... | collective-permute-start | bytes 835592 | tf_op jit(solution)/shard_map/ppermute | solution.py:529
  67.6 9.1 %collective-permute-start.3 = (f32[28,8,128]{2,1,0:T(8,128)S(1)}, f32[28,8,128]{2,1,0:T(8,128)S(1)}, u32[]{:S(2)}, u32[]{:S(2)}) collective-permute-start(f32[28,8,128]{2,1,0:T(8,128)S(1)} %get-tuple-element.28.own), channel_id=1, source_target_pairs={{504,0},{508,4},{16,8},{20,12},{8,16},{12,20},{32,24},{36,28},{24,... | collective-permute-start | bytes 344072 | tf_op jit(solution)/shard_map/ppermute | solution.py:539
  72.9 5.5 %collective-permute-start.2 = (f32[28,8,128]{2,1,0:T(8,128)S(1)}, f32[28,8,128]{2,1,0:T(8,128)S(1)}, u32[]{:S(2)}, u32[]{:S(2)}) collective-permute-start(f32[28,8,128]{2,1,0:T(8,128)S(1)} %get-tuple-element.28.own), channel_id=1, source_target_pairs={{8,0},{12,4},{0,8},{4,12},{24,16},{28,20},{16,24},{20,28},{40,32},... | collective-permute-start | bytes 344072 | tf_op jit(solution)/shard_map/ppermute | solution.py:539
  78.5 3.4 %collective-permute-start.5 = (f32[56,8,128]{2,1,0:T(8,128)S(1)}, f32[56,8,128]{2,1,0:T(8,128)S(1)}, u32[]{:S(2)}, u32[]{:S(2)}) collective-permute-start(f32[56,8,128]{2,1,0:T(8,128)S(1)} %pad_maximum_fusion), channel_id=1, source_target_pairs={{4,0},{0,4},{12,8},{8,12},{20,16},{16,20},{28,24},{24,28},{36,32},... | collective-permute-start | bytes 688136 | tf_op jit(solution)/shard_map/ppermute | solution.py:533
  84.6 8.0 %collective-permute-start.7 = (f32[8,8,128]{2,1,0:T(8,128)S(1)}, f32[8,8,128]{2,1,0:T(8,128)S(1)}, u32[]{:S(2)}, u32[]{:S(2)}) collective-permute-start(f32[8,8,128]{2,1,0:T(8,128)S(1)} %get-tuple-element.38.own), channel_id=1, source_target_pairs={{504,0},{508,4},{16,8},{20,12},{8,16},{12,20},{32,24},{36,28},{24,... | collective-permute-start | bytes 98312 | tf_op jit(solution)/shard_map/ppermute | solution.py:539
  88.4 5.0 %collective-permute-start.6 = (f32[8,8,128]{2,1,0:T(8,128)S(1)}, f32[8,8,128]{2,1,0:T(8,128)S(1)}, u32[]{:S(2)}, u32[]{:S(2)}) collective-permute-start(f32[8,8,128]{2,1,0:T(8,128)S(1)} %get-tuple-element.38.own), channel_id=1, source_target_pairs={{8,0},{12,4},{0,8},{4,12},{24,16},{28,20},{16,24},{20,28},{40,32},... | collective-permute-start | bytes 98312 | tf_op jit(solution)/shard_map/ppermute | solution.py:539
  93.4 4.1 %collective-permute-start.8 = (f32[16,8,128]{2,1,0:T(8,128)S(1)}, f32[16,8,128]{2,1,0:T(8,128)S(1)}, u32[]{:S(2)}, u32[]{:S(2)}) collective-permute-start(f32[16,8,128]{2,1,0:T(8,128)S(1)} %pad_maximum_fusion.2), channel_id=1, source_target_pairs={{4,0},{0,4},{12,8},{8,12},{20,16},{16,20},{28,24},{24,28},{36,32},... | collective-permute-start | bytes 196616 | tf_op jit(solution)/shard_map/ppermute | solution.py:533

commit v8 on v7

--- a/solution.py
+++ b/solution.py
@@ -444,9 +444,8 @@
         coef = opened_1[8 * (k // 2) : 8 * (k // 2) + 8] * inverse[rows]
         send[k] = coef * source[rows]
         send[8 + k] = 0.25 * coef
-        send[16 + k] = (1.0 / OMEGA) * diag[rows]
     for m in range(4):
-        send[24 + m] = below[8 * m : 8 * m + 8]
+        send[16 + m] = below[8 * m : 8 * m + 8]
 
 
 def window(place, high_pair, both, own, low_pair):
@@ -470,9 +469,9 @@
         for k in range(8):
             cb1[8 * n + k] = part(n, k)
             c1[8 * n + k] = part(n, 8 + k)
-            g1[8 * n + k] = part(n, 16 + k)
+            g1[8 * n + k] = 0.25 * pl.reciprocal(jnp.where(c1[8 * n + k] > 0.0, c1[8 * n + k], 1.0))
         for k in range(4):
-            c2[4 * n + k] = part(n, 24 + k)
+            c2[4 * n + k] = part(n, 16 + k)
     levels_solve(c1, g1, c2, cb1, w_a, w_b, cb2, u_a, u_b)
     cc, cb, v2 = Rows(cc, cc_r, 5, 25), Rows(cb, cb_r, 5, 25), Rows(v2, v2_r, 6, 24)
     fine_correct(v2, v_a, w_a, cc, 13, 27)
@@ -580,7 +579,7 @@
     fine, mid, low = (T0, 4, 8, NZ), (T1, 8, NZ), (T2, 8, NZ)
     weights = (CX, 4, 8, NZ)
     cc, cb, v2, first = call(
-        start_kernel, [fine, fine, fine, (28, 8, NZ)], [(weights, F32)], [head, late, keep, next_head]
+        start_kernel, [fine, fine, fine, (20, 8, NZ)], [(weights, F32)], [head, late, keep, next_head]
     )
     deposits, cc_r, cb_r, v2_r, gg = call(
         rest_kernel,

time: 101 us -> 99.7 us (0.987)
  no operation moved by 1% of the time
where the time goes in v8:
time: 99.7 us; the launch traced here: 99.1 us
  starting transfers between devices  47.9 us (48%)
  waiting for transfers between devices  22.3 us (22%)
  blocking collectives  13.4 us (13%)
  Pallas kernels  13 us (13%)
  local copies, waits for them, and re-layouts  1.61 us (2%)
    all_to_all x1, starting transfers between devices, shards(): lax.all_to_all(outgoing, 'box', split_axis=0, concat_axis=0, tiled=True)  20.4 us
    all_gather x1, blocking collectives, shards(): slabs = lax.all_gather(pay, 'slab')  13.4 us
    pallas_call x8, Pallas kernels, call(): pl.pallas_call(kernel, out_shape=shapes, in_specs=specs, out_specs=[pl.Bl...  13 us
    ppermute x4, starting transfers between devices, meet(): lax.ppermute(block, 'box', [(2 * chips[i // 2] + i % 2, i) for i in range...  12.6 us
    all_to_all x1, waiting for transfers between devices, shards(): lax.all_to_all(outgoing, 'box', split_axis=0, concat_axis=0, tiled=True)  10.8 us
    ppermute x3, starting transfers between devices, fetch(): lax.ppermute(block, 'box', [((i + distance) % count, i) for i in range(co...  9.71 us
    ppermute x4, waiting for transfers between devices, meet(): lax.ppermute(block, 'box', [(2 * chips[i // 2] + i % 2, i) for i in range...  5.52 us
    ppermute x2, starting transfers between devices, swap(): lax.ppermute(block, 'box', [(i ^ 1, i) for i in range(lax.axis_size('box'...  5.12 us
  transfers between devices with their start and end apart: 10, of which 8 were waited for; matrix products, arithmetic and copies ran while one was open for 0% of the time, Pallas kernels for 2%

profile of v8, /device:TPU:1, one launch (start us, length us, event | category | flops | bytes accessed | tf_op | source)
XLA Modules:
  0.0 99.1 jit_solution(15709747760536749942)
XLA Ops:
  0.6 2.9 %shard_map.95 = f32[128,1,256]{2,1,0:T(1,128)} custom-call(f32[1,2048]{1,0:T(1,128)} %bitcast.14, f32[1,2048]{1,0:T(1,128)} %bitcast.15, f32[2,2048]{1,0:T(2,128)} %mom_in.1, f32[3,2048]{1,0:T(4,128)} %off_in.1, s32[1,2048]{1,0:T(1,128)} %bitcast.16, s32[1,2048]{1,0:T(1,128)} %bitcast.17), custom_call_target="tpu_custom_call" | custom-call | flops 1000000 | bytes 1000000 | tf_op jit(solution)/shard_map/pallas_call | solution.py:513
  3.6 20.4 %all-to-all-start = ((f32[128,1,256]{2,1,0:T(1,128)}), f32[128,1,256]{2,1,0:T(1,128)S(1)}, u32[]{:S(2)}, u32[]{:S(2)}) async-start(f32[128,1,256]{2,1,0:T(1,128)} %shard_map.95), calls=%async_computation | async-start | bytes 262144 | tf_op jit(solution)/shard_map/all_to_all | solution.py:563
  24.0 0.0 copy-start.1
  24.0 0.8 copy-done.1
  24.8 0.0 slice-start
  24.8 0.8 slice-done
  25.6 0.0 copy-start
  25.6 3.7 %collective-permute-start = (f32[18,8,128]{2,1,0:T(8,128)S(1)}, f32[18,8,128]{2,1,0:T(8,128)S(1)}, u32[]{:S(2)}, u32[]{:S(2)}) collective-permute-start(f32[18,8,128]{2,1,0:T(8,128)S(1)} %pad_maximum_fusion.1), channel_id=1, source_target_pairs={{508,0},{0,4},{4,8},{8,12},{12,16},{16,20},{20,24},{24,28},{28,32}... | collective-permute-start | bytes 221192 | tf_op jit(solution)/shard_map/ppermute | solution.py:528
  29.3 10.8 %all-to-all-done = f32[128,1,256]{2,1,0:T(1,128)S(1)} async-done(((f32[128,1,256]{2,1,0:T(1,128)}), f32[128,1,256]{2,1,0:T(1,128)S(1)}, u32[]{:S(2)}, u32[]{:S(2)}) %all-to-all-start) | async-done | bytes 131104 | tf_op jit(solution)/shard_map/all_to_all | solution.py:563
  40.1 0.0 collective-permute-done.prev
  40.1 0.0 copy-done
  40.1 2.7 %shard_map.96 = (f32[63,8,128]{2,1,0:T(8,128)S(1)}, f32[3,18,8,128]{3,2,1,0:T(8,128)S(1)}) custom-call(f32[128,256]{1,0:T(8,128)S(1)} %bitcast.13, f32[16,8,128]{2,1,0:T(8,128)S(1)} %copy-done, s32[16,8,128]{2,1,0:T(8,128)S(1)} %copy-done.1, f32[18,8,128]{2,1,0:T(8,128)S(1)} %collective-permute-done.prev), custom_call_target="tpu_custom_call" | custom-call | flops 1000000 | bytes 1000000 | tf_op jit(solution)/shard_map/pallas_call | solution.py:513
  42.8 13.4 %all-gather = f32[252,8,128]{2,1,0:T(8,128)S(1)} all-gather(f32[63,8,128]{2,1,0:T(8,128)S(1)} %get-tuple-element.24), channel_id=2, replica_groups=mesh['box'=128,'slab'=4] {'slab'}, dimensions={0}, use_global_device_ids=true | all-gather | bytes 1290240 | tf_op jit(solution)/shard_map/all_gather | solution.py:571
  56.2 0.2 shard_map.97.own_head
  56.4 4.1 %collective-permute-start.1 = (f32[91,8,128]{2,1,0:T(8,128)S(1)}, f32[91,8,128]{2,1,0:T(8,128)S(1)}, u32[]{:S(2)}, u32[]{:S(2)}) collective-permute-start(f32[91,8,128]{2,1,0:T(8,128)S(1)} %shard_map.97.own_head), channel_id=1, source_target_pairs={{4,0},{8,4},{12,8},{16,12},{20,16},{24,20},{28,24},{32,28},{36,32}... | collective-permute-start | bytes 1118216 | tf_op jit(solution)/shard_map/ppermute | solution.py:528
  60.5 0.1 pad_add_fusion.place
  60.6 0.7 shard_map.98
  61.3 1.9 %collective-permute-start.4 = (f32[68,8,128]{2,1,0:T(8,128)S(1)}, f32[68,8,128]{2,1,0:T(8,128)S(1)}, u32[]{:S(2)}, u32[]{:S(2)}) collective-permute-start(f32[68,8,128]{2,1,0:T(8,128)S(1)} %get-tuple-element.26.own_late), channel_id=1, source_target_pairs={{4,0},{8,4},{12,8},{16,12},{20,16},{24,20},{28,24},{32,28},{36,32}... | collective-permute-start | bytes 835592 | tf_op jit(solution)/shard_map/ppermute | solution.py:528
  63.2 3.8 %collective-permute-done.1.next_head = f32[91,8,128]{2,1,0:T(8,128)S(1)} collective-permute-done((f32[91,8,128]{2,1,0:T(8,128)S(1)}, f32[91,8,128]{2,1,0:T(8,128)S(1)}, u32[]{:S(2)}, u32[]{:S(2)}) %collective-permute-start.1) | collective-permute-done | bytes 372768 | tf_op jit(solution)/shard_map/ppermute | solution.py:528
  67.0 0.6 shard_map.99
  67.6 5.3 %collective-permute-start.3 = (f32[20,8,128]{2,1,0:T(8,128)S(1)}, f32[20,8,128]{2,1,0:T(8,128)S(1)}, u32[]{:S(2)}, u32[]{:S(2)}) collective-permute-start(f32[20,8,128]{2,1,0:T(8,128)S(1)} %get-tuple-element.28.own), channel_id=1, source_target_pairs={{504,0},{508,4},{16,8},{20,12},{8,16},{12,20},{32,24},{36,28},{24,... | collective-permute-start | bytes 245768 | tf_op jit(solution)/shard_map/ppermute | solution.py:538
  72.9 1.9 %collective-permute-start.2 = (f32[20,8,128]{2,1,0:T(8,128)S(1)}, f32[20,8,128]{2,1,0:T(8,128)S(1)}, u32[]{:S(2)}, u32[]{:S(2)}) collective-permute-start(f32[20,8,128]{2,1,0:T(8,128)S(1)} %get-tuple-element.28.own), channel_id=1, source_target_pairs={{8,0},{12,4},{0,8},{4,12},{24,16},{28,20},{16,24},{20,28},{40,32},... | collective-permute-start | bytes 245768 | tf_op jit(solution)/shard_map/ppermute | solution.py:538
  74.8 0.0 collective-permute-done.4.next_late
  74.8 0.7 shard_map.100
  75.6 0.5 collective-permute-done.3.low_pair
  76.1 2.0 %collective-permute-done.2.high_pair = f32[20,8,128]{2,1,0:T(8,128)S(1)} collective-permute-done((f32[20,8,128]{2,1,0:T(8,128)S(1)}, f32[20,8,128]{2,1,0:T(8,128)S(1)}, u32[]{:S(2)}, u32[]{:S(2)}) %collective-permute-start.2) | collective-permute-done | bytes 81952 | tf_op jit(solution)/shard_map/ppermute | solution.py:538
  78.1 1.9 %collective-permute-start.5 = (f32[40,8,128]{2,1,0:T(8,128)S(1)}, f32[40,8,128]{2,1,0:T(8,128)S(1)}, u32[]{:S(2)}, u32[]{:S(2)}) collective-permute-start(f32[40,8,128]{2,1,0:T(8,128)S(1)} %pad_maximum_fusion), channel_id=1, source_target_pairs={{4,0},{0,4},{12,8},{8,12},{20,16},{16,20},{28,24},{24,28},{36,32},... | collective-permute-start | bytes 491528 | tf_op jit(solution)/shard_map/ppermute | solution.py:532
  80.1 1.4 %collective-permute-done.5.both = f32[40,8,128]{2,1,0:T(8,128)S(1)} collective-permute-done((f32[40,8,128]{2,1,0:T(8,128)S(1)}, f32[40,8,128]{2,1,0:T(8,128)S(1)}, u32[]{:S(2)}, u32[]{:S(2)}) %collective-permute-start.5) | collective-permute-done | bytes 163872 | tf_op jit(solution)/shard_map/ppermute | solution.py:532
  81.4 2.7 %shard_map.101 = (f32[30,4,8,128]{3,2,1,0:T(8,128)S(1)}, f32[40,8,128]{2,1,0:T(8,128)S(1)}, f32[40,8,128]{2,1,0:T(8,128)S(1)}, f32[20,8,128]{2,1,0:T(8,128)S(1)}, f32[8,8,128]{2,1,0:T(8,128)S(1)}) custom-call(s32[3]{0:T(128)S(1)} %pad_add_fusion.place, f32[20,8,128]{2,1,0:T(8,128)S(1)} %collective-permute-done.2.high_pair, ...), custom_call_target="tpu_custom_call" | custom-call | flops 1000000 | bytes 1000000 | tf_op jit(solution)/shard_map/pallas_call | solution.py:513
  84.1 3.5 %collective-permute-start.7 = (f32[8,8,128]{2,1,0:T(8,128)S(1)}, f32[8,8,128]{2,1,0:T(8,128)S(1)}, u32[]{:S(2)}, u32[]{:S(2)}) collective-permute-start(f32[8,8,128]{2,1,0:T(8,128)S(1)} %get-tuple-element.38.own), channel_id=1, source_target_pairs={{504,0},{508,4},{16,8},{20,12},{8,16},{12,20},{32,24},{36,28},{24,... | collective-permute-start | bytes 98312 | tf_op jit(solution)/shard_map/ppermute | solution.py:538
  87.6 1.9 %collective-permute-start.6 = (f32[8,8,128]{2,1,0:T(8,128)S(1)}, f32[8,8,128]{2,1,0:T(8,128)S(1)}, u32[]{:S(2)}, u32[]{:S(2)}) collective-permute-start(f32[8,8,128]{2,1,0:T(8,128)S(1)} %get-tuple-element.38.own), channel_id=1, source_target_pairs={{8,0},{12,4},{0,8},{4,12},{24,16},{28,20},{16,24},{20,28},{40,32},... | collective-permute-start | bytes 98312 | tf_op jit(solution)/shard_map/ppermute | solution.py:538
  89.5 2.6 %collective-permute-done.7.low_pair = f32[8,8,128]{2,1,0:T(8,128)S(1)} collective-permute-done((f32[8,8,128]{2,1,0:T(8,128)S(1)}, f32[8,8,128]{2,1,0:T(8,128)S(1)}, u32[]{:S(2)}, u32[]{:S(2)}) %collective-permute-start.7) | collective-permute-done | bytes 32800 | tf_op jit(solution)/shard_map/ppermute | solution.py:538
  92.1 0.5 collective-permute-done.6.high_pair
  92.5 3.2 %collective-permute-start.8 = (f32[16,8,128]{2,1,0:T(8,128)S(1)}, f32[16,8,128]{2,1,0:T(8,128)S(1)}, u32[]{:S(2)}, u32[]{:S(2)}) collective-permute-start(f32[16,8,128]{2,1,0:T(8,128)S(1)} %pad_maximum_fusion.2), channel_id=1, source_target_pairs={{4,0},{0,4},{12,8},{8,12},{20,16},{16,20},{28,24},{24,28},{36,32},... | collective-permute-start | bytes 196616 | tf_op jit(solution)/shard_map/ppermute | solution.py:532
  95.8 0.9 collective-permute-done.8.both
  96.6 2.5 %shard_map.102 = (f32[16,8,128]{2,1,0:T(8,128)}, f32[4,16,8,128]{3,2,1,0:T(8,128)}) custom-call(s32[3]{0:T(128)S(1)} %pad_add_fusion.place, f32[8,8,128]{2,1,0:T(8,128)S(1)} %collective-permute-done.6.high_pair, f32[16,8,128]{2,1,0:T(8,128)S(1)} %collective-permute-done.8.both, f32[8,8,128]{2,1,0:T(8,128)S(1)} %get-tuple-element.38.own, ...), custom_call_target="tpu_custom_call" | custom-call | flops 1000000 | bytes 1000000 | tf_op jit(solution)/shard_map/pallas_call | solution.py:513
  (7 shorter events, 0.1 us)
Async XLA Ops:
  3.6 36.5 %all-to-all-start = ((f32[128,1,256]{2,1,0:T(1,128)}), f32[128,1,256]{2,1,0:T(1,128)S(1)}, u32[]{:S(2)}, u32[]{:S(2)}) async-start(f32[128,1,256]{2,1,0:T(1,128)} %shard_map.95), calls=%async_computation | async-start | bytes 262144 | tf_op jit(solution)/shard_map/all_to_all | solution.py:563
  24.0 0.8 copy-start.1
  24.8 0.8 slice-start
  25.6 14.5 %copy-start = (f32[16,8,128]{2,1,0:T(8,128)S(1)}, f32[16,8,128]{2,1,0:T(8,128)}, u32[]{:S(2)}) copy-start(f32[16,8,128]{2,1,0:T(8,128)} %rhs.1) | copy-start | bytes 196612
  25.6 14.5 %collective-permute-start = (f32[18,8,128]{2,1,0:T(8,128)S(1)}, f32[18,8,128]{2,1,0:T(8,128)S(1)}, u32[]{:S(2)}, u32[]{:S(2)}) collective-permute-start(f32[18,8,128]{2,1,0:T(8,128)S(1)} %pad_maximum_fusion.1), channel_id=1, source_target_pairs={{508,0},{0,4},{4,8},{8,12},{12,16},{16,20},{20,24},{24,28},{28,32}... | collective-permute-start | bytes 221192 | tf_op jit(solution)/shard_map/ppermute | solution.py:528
  56.4 10.6 %collective-permute-start.1 = (f32[91,8,128]{2,1,0:T(8,128)S(1)}, f32[91,8,128]{2,1,0:T(8,128)S(1)}, u32[]{:S(2)}, u32[]{:S(2)}) collective-permute-start(f32[91,8,128]{2,1,0:T(8,128)S(1)} %shard_map.97.own_head), channel_id=1, source_target_pairs={{4,0},{8,4},{12,8},{16,12},{20,16},{24,20},{28,24},{32,28},{36,32}... | collective-permute-start | bytes 1118216 | tf_op jit(solution)/shard_map/ppermute | solution.py:528
  61.3 13.5 %collective-permute-start.4 = (f32[68,8,128]{2,1,0:T(8,128)S(1)}, f32[68,8,128]{2,1,0:T(8,128)S(1)}, u32[]{:S(2)}, u32[]{:S(2)}) collective-permute-start(f32[68,8,128]{2,1,0:T(8,128)S(1)} %get-tuple-element.26.own_late), channel_id=1, source_target_pairs={{4,0},{8,4},{12,8},{16,12},{20,16},{24,20},{28,24},{32,28},{36,32}... | collective-permute-start | bytes 835592 | tf_op jit(solution)/shard_map/ppermute | solution.py:528
  67.6 8.5 %collective-permute-start.3 = (f32[20,8,128]{2,1,0:T(8,128)S(1)}, f32[20,8,128]{2,1,0:T(8,128)S(1)}, u32[]{:S(2)}, u32[]{:S(2)}) collective-permute-start(f32[20,8,128]{2,1,0:T(8,128)S(1)} %get-tuple-element.28.own), channel_id=1, source_target_pairs={{504,0},{508,4},{16,8},{20,12},{8,16},{12,20},{32,24},{36,28},{24,... | collective-permute-start | bytes 245768 | tf_op jit(solution)/shard_map/ppermute | solution.py:538
  72.9 5.2 %collective-permute-start.2 = (f32[20,8,128]{2,1,0:T(8,128)S(1)}, f32[20,8,128]{2,1,0:T(8,128)S(1)}, u32[]{:S(2)}, u32[]{:S(2)}) collective-permute-start(f32[20,8,128]{2,1,0:T(8,128)S(1)} %get-tuple-element.28.own), channel_id=1, source_target_pairs={{8,0},{12,4},{0,8},{4,12},{24,16},{28,20},{16,24},{20,28},{40,32},... | collective-permute-start | bytes 245768 | tf_op jit(solution)/shard_map/ppermute | solution.py:538
  78.1 3.3 %collective-permute-start.5 = (f32[40,8,128]{2,1,0:T(8,128)S(1)}, f32[40,8,128]{2,1,0:T(8,128)S(1)}, u32[]{:S(2)}, u32[]{:S(2)}) collective-permute-start(f32[40,8,128]{2,1,0:T(8,128)S(1)} %pad_maximum_fusion), channel_id=1, source_target_pairs={{4,0},{0,4},{12,8},{8,12},{20,16},{16,20},{28,24},{24,28},{36,32},... | collective-permute-start | bytes 491528 | tf_op jit(solution)/shard_map/ppermute | solution.py:532
  84.1 8.0 %collective-permute-start.7 = (f32[8,8,128]{2,1,0:T(8,128)S(1)}, f32[8,8,128]{2,1,0:T(8,128)S(1)}, u32[]{:S(2)}, u32[]{:S(2)}) collective-permute-start(f32[8,8,128]{2,1,0:T(8,128)S(1)} %get-tuple-element.38.own), channel_id=1, source_target_pairs={{504,0},{508,4},{16,8},{20,12},{8,16},{12,20},{32,24},{36,28},{24,... | collective-permute-start | bytes 98312 | tf_op jit(solution)/shard_map/ppermute | solution.py:538
  87.6 5.0 %collective-permute-start.6 = (f32[8,8,128]{2,1,0:T(8,128)S(1)}, f32[8,8,128]{2,1,0:T(8,128)S(1)}, u32[]{:S(2)}, u32[]{:S(2)}) collective-permute-start(f32[8,8,128]{2,1,0:T(8,128)S(1)} %get-tuple-element.38.own), channel_id=1, source_target_pairs={{8,0},{12,4},{0,8},{4,12},{24,16},{28,20},{16,24},{20,28},{40,32},... | collective-permute-start | bytes 98312 | tf_op jit(solution)/shard_map/ppermute | solution.py:538
  92.5 4.1 %collective-permute-start.8 = (f32[16,8,128]{2,1,0:T(8,128)S(1)}, f32[16,8,128]{2,1,0:T(8,128)S(1)}, u32[]{:S(2)}, u32[]{:S(2)}) collective-permute-start(f32[16,8,128]{2,1,0:T(8,128)S(1)} %pad_maximum_fusion.2), channel_id=1, source_target_pairs={{4,0},{0,4},{12,8},{8,12},{20,16},{16,20},{28,24},{24,28},{36,32},... | collective-permute-start | bytes 196616 | tf_op jit(solution)/shard_map/ppermute | solution.py:532
